TPU v7x, 32 devices: a whole 2x2x4 slice. The times are simulated.
32 devices in a mesh: clips: 2 (over y), seq: 4 (over z), tp: 2 (over x), dp: 2 (over core).
Axes of the slice: x: 2, y: 2, z: 4, core: 2. Of those that a mesh axis runs over, the one named last changes fastest.
Arguments:
- video_query: bfloat16 [4, 512, 4096], P(('clips', 'dp'), 'seq', 'tp'), parts along dimension 0, may hold values from -384 to 384
- video_key: bfloat16 [4, 512, 4096], P(('clips', 'dp'), 'seq', 'tp'), parts along dimension 0, may hold values from -384 to 384
- video_value: bfloat16 [4, 512, 4096], P(('clips', 'dp'), 'seq', 'tp'), parts along dimension 0, may hold values from -6 to 6
- cross_query: bfloat16 [4, 512, 2048], P(('clips', 'dp'), 'seq', 'tp'), parts along dimension 0, may hold values from -384 to 384
- audio_key: bfloat16 [4, 32, 2048], P(('clips', 'dp'), 'seq', 'tp'), parts along dimension 0, may hold values from -384 to 384
- audio_value: bfloat16 [4, 32, 2048], P(('clips', 'dp'), 'seq', 'tp'), parts along dimension 0, may hold values from -6 to 6
- audio_query: bfloat16 [4, 32, 2048], P(('clips', 'dp'), 'seq', 'tp'), parts along dimension 0, may hold values from -384 to 384
- cross_key: bfloat16 [4, 512, 2048], P(('clips', 'dp'), 'seq', 'tp'), parts along dimension 0, may hold values from -384 to 384
- cross_value: bfloat16 [4, 512, 2048], P(('clips', 'dp'), 'seq', 'tp'), parts along dimension 0, may hold values from -6 to 6
- audio_input: bfloat16 [4, 32, 2048], P(('clips', 'dp'), 'seq'), parts along dimension 0, may hold values from -0.29882812 to 0.29882812
- norm_gain: float32 [2048], replicated, may hold values from 0.1 to 1.9
- up_weight: bfloat16 [2048, 8192], P('tp', 'seq'), may hold values from -0.125 to 0.125
- down_weight: bfloat16 [8192, 2048], P('seq', 'tp'), may hold values from -0.0625 to 0.0625
Outputs:
- video_mixed: bfloat16 [4, 512, 4096], P(('clips', 'dp'), 'seq', 'tp'), parts along dimension 0
- video_heard: bfloat16 [4, 512, 2048], P(('clips', 'dp'), 'seq', 'tp'), parts along dimension 0
- audio_seen: bfloat16 [4, 32, 2048], P(('clips', 'dp'), 'seq', 'tp'), parts along dimension 0
- audio_mlp: bfloat16 [4, 32, 2048], P(('clips', 'dp'), 'seq', 'tp'), parts along dimension 0
There are 2 independent parts, one for each index of `clips`. A program takes and returns all parts, laid end to end along the dimension named above; an argument that names none is the same for every part. Nothing has to cross between parts.
All inputs are finite; a program needn't handle non-finite values.
Results may differ from a plain program's by a relative error of at most 0.013.
Values may be sent and summed in bfloat16 or wider, within the bound.
No kernel may reach another device: no remote copies, remote signals or barrier semaphores. Data moves between devices by JAX's collectives and lax.ppermute only.
A program may use at most 64 MiB of HBM per device.

v0:
```python
import math

import jax
import jax.numpy as jnp
from jax import lax
from jax.sharding import PartitionSpec as P

VHEAD = 128
CHEAD = 64


def attend_rows(queries, keys_in, values_in, head_count):
    head_size = queries.shape[1] // head_count
    query_heads = queries.reshape(queries.shape[0], head_count, head_size)
    key_heads = keys_in.reshape(keys_in.shape[0], head_count, head_size)
    value_heads = values_in.reshape(values_in.shape[0], head_count, head_size)
    scores = jnp.einsum(
        "qhd,khd->qhk", query_heads, key_heads, preferred_element_type=jnp.float32
    ) / math.sqrt(head_size)
    peak_value = jnp.max(scores, axis=2, keepdims=True)
    weights = jnp.exp(scores - peak_value)
    totals = jnp.sum(weights, axis=2)
    weighted = jnp.einsum(
        "qhk,khd->qhd",
        weights.astype(jnp.bfloat16),
        value_heads,
        preferred_element_type=jnp.float32,
    )
    result = weighted / totals[:, :, None]
    return result.reshape(queries.shape[0], head_count * head_size).astype(jnp.bfloat16)


def attend(queries, keys_in, values_in, head_count):
    row_total = queries.shape[0]
    block_rows = 512 if row_total % 512 == 0 else row_total
    pieces = queries.reshape(row_total // block_rows, block_rows, queries.shape[1])
    result = lax.map(
        lambda row_piece: attend_rows(row_piece, keys_in, values_in, head_count), pieces
    )
    return result.reshape(row_total, queries.shape[1])


def video_self(queries, keys_in, values_in):
    seq_count = lax.axis_size("seq")
    local_heads = queries.shape[1] // VHEAD
    dest_heads = max(local_heads // seq_count, 1)
    blocks = seq_count * dest_heads // local_heads
    groups = local_heads // dest_heads
    group_width = dest_heads * VHEAD
    token_count = queries.shape[0]
    block_tokens = token_count // blocks

    def spread(tensor):
        shaped = tensor.reshape(token_count, groups, group_width).transpose(1, 0, 2)
        shaped = jnp.broadcast_to(shaped[:, None], (groups, blocks, token_count, group_width))
        return shaped.reshape(seq_count, token_count, group_width)

    shaped = queries.reshape(blocks, block_tokens, groups, group_width).transpose(2, 0, 1, 3)
    own_queries = lax.all_to_all(
        shaped.reshape(seq_count, block_tokens, group_width),
        "seq",
        split_axis=0,
        concat_axis=0,
        tiled=True,
    )
    keys_all = lax.all_to_all(spread(keys_in), "seq", split_axis=0, concat_axis=0, tiled=True)
    values_all = lax.all_to_all(spread(values_in), "seq", split_axis=0, concat_axis=0, tiled=True)
    keys_all = keys_all.reshape(-1, group_width)
    values_all = values_all.reshape(-1, group_width)
    own_queries = own_queries.reshape(-1, group_width)
    attended = attend(own_queries, keys_all, values_all, dest_heads)
    returned = lax.all_to_all(
        attended.reshape(seq_count, block_tokens, group_width),
        "seq",
        split_axis=0,
        concat_axis=0,
        tiled=True,
    )
    returned = returned.reshape(groups, blocks, block_tokens, group_width).transpose(1, 2, 0, 3)
    return returned.reshape(token_count, groups * group_width)


def audio_listen(queries, keys_in, values_in, head_count):
    head_size = queries.shape[1] // head_count
    query_heads = queries.reshape(queries.shape[0], head_count, head_size)
    key_heads = keys_in.reshape(keys_in.shape[0], head_count, head_size)
    value_heads = values_in.reshape(values_in.shape[0], head_count, head_size)
    scores = jnp.einsum(
        "qhd,khd->qhk", query_heads, key_heads, preferred_element_type=jnp.float32
    ) / math.sqrt(head_size)
    local_peak = jnp.max(scores, axis=2)
    peak_value = lax.pmax(local_peak, "seq")
    weights = jnp.exp(scores - peak_value[:, :, None])
    totals = jnp.sum(weights, axis=2)
    weighted = jnp.einsum(
        "qhk,khd->qhd",
        weights.astype(jnp.bfloat16),
        value_heads,
        preferred_element_type=jnp.float32,
    )
    totals, weighted = (totals, weighted.reshape(queries.shape[0], head_count * head_size))
    totals, weighted = (
        lax.psum_scatter(totals, "seq", scatter_dimension=0, tiled=True),
        lax.psum_scatter(weighted, "seq", scatter_dimension=0, tiled=True),
    )
    return (weighted / jnp.repeat(totals, head_size, axis=1)).astype(jnp.bfloat16)


def audio_block(audio_rows, audio_seen, norm_gain, up_weight, down_weight):
    features = lax.all_gather(audio_seen, "tp", axis=1, tiled=True)
    residual = audio_rows.astype(jnp.float32) + features.astype(jnp.float32)
    scale_factor = lax.rsqrt(jnp.mean(residual * residual, axis=1, keepdims=True) + 1e-06)
    normed = (residual * scale_factor * norm_gain).astype(jnp.bfloat16)
    slice_width = up_weight.shape[0]
    own_features = lax.dynamic_slice_in_dim(
        normed, lax.axis_index("tp") * slice_width, slice_width, 1
    )
    partial_sum = jnp.dot(
        lax.all_gather(own_features, "seq", axis=0, tiled=True),
        up_weight,
        preferred_element_type=jnp.float32,
    )
    hidden = jax.nn.gelu(lax.psum(partial_sum, "tp")).astype(jnp.bfloat16)
    return lax.psum_scatter(
        jnp.dot(hidden, down_weight, preferred_element_type=jnp.float32),
        "seq",
        scatter_dimension=0,
        tiled=True,
    ).astype(jnp.bfloat16)


def body(
    video_query,
    video_key,
    video_value,
    cross_query,
    audio_key,
    audio_value,
    audio_query,
    cross_key,
    cross_value,
    audio_input,
    norm_gain,
    up_weight,
    down_weight,
):
    mixed_list, heard_list, seen_list, output_list = ([], [], [], [])
    cross_heads = cross_query.shape[2] // CHEAD
    mixed_list.append(video_self(video_query[0], video_key[0], video_value[0]))
    gathered_query = lax.all_gather(audio_query[0], "seq", axis=0, tiled=True)
    gathered_key = lax.all_gather(audio_key[0], "seq", axis=0, tiled=True)
    gathered_value = lax.all_gather(audio_value[0], "seq", axis=0, tiled=True)
    heard_list.append(attend(cross_query[0], gathered_key, gathered_value, cross_heads))
    audio_seen = audio_listen(gathered_query, cross_key[0], cross_value[0], cross_heads)
    seen_list.append(audio_seen)
    output_list.append(audio_block(audio_input[0], audio_seen, norm_gain, up_weight, down_weight))
    return (
        jnp.stack(mixed_list),
        jnp.stack(heard_list),
        jnp.stack(seen_list),
        jnp.stack(output_list),
    )


def solution(mesh):
    placed = (
        P(("clips", "dp"), "seq", "tp"),
        P(("clips", "dp"), "seq", "tp"),
        P(("clips", "dp"), "seq", "tp"),
        P(("clips", "dp"), "seq", "tp"),
        P(("clips", "dp"), "seq", "tp"),
        P(("clips", "dp"), "seq", "tp"),
        P(("clips", "dp"), "seq", "tp"),
        P(("clips", "dp"), "seq", "tp"),
        P(("clips", "dp"), "seq", "tp"),
        P(("clips", "dp"), "seq", None),
        P(),
        P("tp", "seq"),
        P("seq", "tp"),
    )
    return jax.shard_map(
        body,
        mesh=mesh,
        in_specs=placed,
        out_specs=(
            P(("clips", "dp"), "seq", "tp"),
            P(("clips", "dp"), "seq", "tp"),
            P(("clips", "dp"), "seq", "tp"),
            P(("clips", "dp"), "seq", "tp"),
        ),
        check_vma=False,
    )
```

profile of v0, /device:TPU:0, one launch (start us, length us, event | category | flops | bytes accessed | tf_op | source)
XLA Modules:
  0.0 170.7 jit_solution(16451558797304456168)
XLA Ops:
  7.2 2.0 %copy.100 = bf16[1,16,4,8,512]{4,3,1,2,0:T(8,128)(2,1)} copy(bf16[1,16,4,8,512]{4,3,2,1,0:T(8,128)(2,1)} %bitcast.77) | data formatting | bytes 1048576 | tf_op jit(solution)/shard_map/reshape;squeeze | solution.py:58
  9.2 6.3 %all-to-all-start.1 = ((bf16[4,128,512]{2,1,0:T(8,128)(2,1)}), bf16[4,128,512]{2,1,0:T(8,128)(2,1)S(1)}, u32[]{:S(2)}, u32[]{:S(2)}) async-start(bf16[4,128,512]{2,1,0:T(8,128)(2,1)} %bitcast.69), calls=%async_computation.1 | async-start | bytes 1048576 | tf_op jit(solution)/shard_map/all_to_all | solution.py:59
  15.5 1.2 copy.70
  16.7 1.1 copy.68
  17.8 17.8 %all-gather.2 = bf16[1,32,1024]{2,1,0:T(8,128)(2,1)S(1)} all-gather(bf16[1,8,1024]{2,1,0:T(8,128)(2,1)} %param.19), channel_id=4, replica_groups=mesh['clips'=2,'seq'=4,'tp'=2,'dp'=2] {'seq'}, dimensions={1}, use_global_device_ids=true | all-gather | bytes 81920 | tf_op jit(solution)/shard_map/all_gather | solution.py:150
  36.1 11.0 %pmax.7 = f32[32,16]{0,1:T(8,128)S(1)} all-reduce(f32[32,16]{0,1:T(8,128)S(1)} %get-tuple-element.56), channel_id=1, replica_groups=mesh['clips'=2,'seq'=4,'tp'=2,'dp'=2] {'seq'}, use_global_device_ids=true, to_apply=%region_5.6 | all-reduce | flops 512 | bytes 4096 | tf_op jit(solution)/shard_map/pmax | solution.py:92
  51.1 13.2 %all-gather = bf16[1,32,1024]{2,1,0:T(8,128)(2,1)S(1)} all-gather(bf16[1,8,1024]{2,1,0:T(8,128)(2,1)S(1)} %copy-done.6), channel_id=2, replica_groups=mesh['clips'=2,'seq'=4,'tp'=2,'dp'=2] {'seq'}, dimensions={1}, use_global_device_ids=true | all-gather | bytes 81920 | tf_op jit(solution)/shard_map/all_gather | solution.py:151
  66.1 15.7 %all-reduce = f32[32,16]{1,0:T(8,128)S(1)} all-reduce(f32[32,16]{1,0:T(8,128)S(1)} %copy.72), channel_id=6, replica_groups=mesh['clips'=2,'seq'=4,'tp'=2,'dp'=2] {'seq'}, use_global_device_ids=true, to_apply=%region_8.9.clone | all-reduce | flops 512 | bytes 4096
  82.3 3.5 %all-to-all-start = ((bf16[4,128,512]{2,1,0:T(8,128)(2,1)}), bf16[4,128,512]{2,1,0:T(8,128)(2,1)S(1)}, u32[]{:S(2)}, u32[]{:S(2)}) async-start(bf16[4,128,512]{2,1,0:T(8,128)(2,1)} %bitcast.71), calls=%async_computation | async-start | bytes 1048576 | tf_op jit(solution)/shard_map/all_to_all | solution.py:66
  86.6 4.4 %all_gather.18 = bf16[8,2048]{1,0:T(8,128)(2,1)S(1)} all-gather(bf16[8,1024]{1,0:T(8,128)(2,1)S(1)} %divide_convert_fusion), channel_id=1, replica_groups=mesh['clips'=2,'seq'=4,'tp'=2,'dp'=2] {'tp'}, dimensions={1}, use_global_device_ids=true | all-gather | bytes 49152 | tf_op jit(solution)/shard_map/all_gather | solution.py:110
  91.2 13.9 %all_gather.19 = bf16[32,1024]{1,0:T(8,128)(2,1)S(1)} all-gather(bf16[8,1024]{1,0:T(8,128)(2,1)S(1)} %fusion.50), channel_id=1, replica_groups=mesh['clips'=2,'seq'=4,'tp'=2,'dp'=2] {'seq'}, dimensions={0}, use_global_device_ids=true | all-gather | bytes 81920 | tf_op jit(solution)/shard_map/all_gather | solution.py:119
  105.1 4.7 %all-to-all-start.2 = ((bf16[4,128,512]{2,1,0:T(8,128)(2,1)}), bf16[4,128,512]{2,1,0:T(8,128)(2,1)S(1)}, u32[]{:S(2)}, u32[]{:S(2)}) async-start(bf16[4,128,512]{2,1,0:T(8,128)(2,1)} %bitcast.70), calls=%async_computation.2 | async-start | bytes 1048576 | tf_op jit(solution)/shard_map/all_to_all | solution.py:67
  109.9 3.7 %fusion.58 = f32[32,2048]{1,0:T(8,128)} fusion(bf16[32,1024]{1,0:T(8,128)(2,1)S(1)} %all_gather.19, bf16[1024,2048]{1,0:T(8,128)(2,1)} %param.24), kind=kOutput, calls=%fused_computation.67 | convolution fusion | flops 134217728 | bytes 4521984 | tf_op jit(solution)/shard_map/dot_general | solution.py:118
  114.6 1.9 %copy-done = f32[4,512,512]{2,1,0:T(8,128)} copy-done((f32[4,512,512]{2,1,0:T(8,128)}, f32[4,512,512]{2,1,0:T(8,128)S(1)}, u32[]{:S(2)}) %copy-start) | copy-done | bytes 4194328
  117.2 7.5 %all-to-all-done.2 = bf16[4,128,512]{2,1,0:T(8,128)(2,1)S(1)} async-done(((bf16[4,128,512]{2,1,0:T(8,128)(2,1)}), bf16[4,128,512]{2,1,0:T(8,128)(2,1)S(1)}, u32[]{:S(2)}, u32[]{:S(2)}) %all-to-all-start.2) | async-done | bytes 524320 | tf_op jit(solution)/shard_map/all_to_all | solution.py:67
  124.9 3.4 %fusion.17 = bf16[512,4,128]{2,0,1:T(8,128)(2,1)S(1)} fusion(f32[4,512,512]{2,1,0:T(8,128)} %copy-done, f32[512,4]{0,1:T(4,128)S(1)} %get-tuple-element.52, bf16[512,4,128]{2,1,0:T(4,128)(2,1)S(1)} %reshape_reshape.11, f32[512,4]{0,1:T(4,128)S(1)} %fusion.1), kind=kOutput, calls=%fused_computation.18 | convolution fusion | flops 272105472 | bytes 5259264 | tf_op jit(solution)/shard_map/while/body/eval_jaxpr/qhk,khd->qhd/dot_general | solution.py:23
  128.7 1.0 convert_element_type.56
  129.7 3.5 %all-to-all-start.3 = ((bf16[4,128,512]{2,1,0:T(8,128)(2,1)}), bf16[4,128,512]{2,1,0:T(8,128)(2,1)S(1)}, u32[]{:S(2)}, u32[]{:S(2)}) async-start(bf16[4,128,512]{2,1,0:T(8,128)(2,1)} %convert_element_type.56), calls=%async_computation.3 | async-start | bytes 1048576 | tf_op jit(solution)/shard_map/all_to_all | solution.py:72
  133.2 5.1 %all-reduce.3.cloned.1.call-done = f32[32,2048]{1,0:T(8,128)} async-done(((f32[32,2048]{1,0:T(8,128)}), f32[32,2048]{1,0:T(8,128)}) %all-reduce.3.cloned.1.call-update) | async-done | bytes 262160 | tf_op jit(solution)/shard_map/psum | solution.py:123
  138.4 3.7 %fusion.38 = f32[32,1024]{1,0:T(8,128)} fusion(bf16[2048,1024]{1,0:T(8,128)(2,1)} %param.25, f32[32,2048]{1,0:T(8,128)} %all-reduce.3.cloned.1.call-done), kind=kOutput, calls=%fused_computation.41 | convolution fusion | flops 134807552 | bytes 4587520 | tf_op jit(solution)/shard_map/dot_general | solution.py:125
  142.1 13.2 %all-gather.1 = bf16[1,32,1024]{2,1,0:T(8,128)(2,1)S(1)} all-gather(bf16[1,8,1024]{2,1,0:T(8,128)(2,1)S(1)} %copy-done.7), channel_id=3, replica_groups=mesh['clips'=2,'seq'=4,'tp'=2,'dp'=2] {'seq'}, dimensions={1}, use_global_device_ids=true | all-gather | bytes 81920 | tf_op jit(solution)/shard_map/all_gather | solution.py:152
  156.6 4.9 %reduce-scatter.5.cloned.1.call-done = f32[8,1024]{1,0:T(8,128)} async-done(((f32[32,1024]{1,0:T(8,128)}), f32[8,1024]{1,0:T(8,128)}) %reduce-scatter.5.cloned.1.call-update) | async-done | bytes 32784 | tf_op jit(solution)/shard_map/reduce_scatter | solution.py:124
  161.6 1.4 convert_bitcast_fusion
  163.2 1.0 copy.73
  (63 shorter events, 10.8 us)
Async XLA Ops:
  7.2 41.2 %copy-start.1 = (bf16[1,128,2048]{2,1,0:T(8,128)(2,1)S(1)}, bf16[1,128,2048]{2,1,0:T(8,128)(2,1)}, u32[]{:S(2)}) copy-start(bf16[1,128,2048]{2,1,0:T(8,128)(2,1)} %param.14) | copy-start | bytes 1572868
  7.2 42.5 %copy-start.2 = (bf16[1,128,2048]{2,1,0:T(8,128)(2,1)S(1)}, bf16[1,128,2048]{2,1,0:T(8,128)(2,1)}, u32[]{:S(2)}) copy-start(bf16[1,128,2048]{2,1,0:T(8,128)(2,1)} %param.15) | copy-start | bytes 1572868
  9.2 73.1 %all-to-all-start.1 = ((bf16[4,128,512]{2,1,0:T(8,128)(2,1)}), bf16[4,128,512]{2,1,0:T(8,128)(2,1)S(1)}, u32[]{:S(2)}, u32[]{:S(2)}) async-start(bf16[4,128,512]{2,1,0:T(8,128)(2,1)} %bitcast.69), calls=%async_computation.1 | async-start | bytes 1048576 | tf_op jit(solution)/shard_map/all_to_all | solution.py:59
  15.5 35.4 %copy-start.3 = (bf16[1,128,1024]{2,1,0:T(8,128)(2,1)S(1)}, bf16[1,128,1024]{2,1,0:T(8,128)(2,1)}, u32[]{:S(2)}) copy-start(bf16[1,128,1024]{2,1,0:T(8,128)(2,1)} %param.16) | copy-start | bytes 786436
  15.5 35.6 %copy-start.6 = (bf16[1,8,1024]{2,1,0:T(8,128)(2,1)S(1)}, bf16[1,8,1024]{2,1,0:T(8,128)(2,1)}, u32[]{:S(2)}) copy-start(bf16[1,8,1024]{2,1,0:T(8,128)(2,1)} %param.17) | copy-start | bytes 49156
  15.5 70.3 %reduce-scatter.3.cloned.1.call-start = ((), (), s32[]{:S(2)}) async-start(), calls=%async_computation.6 | async-start | bytes 163840 | tf_op jit(solution)/shard_map/reduce_scatter | solution.py:104
  17.8 47.0 %copy-start.9 = (u32[32]{0:T(128)S(1)}, u32[32]{0:T(128)}, u32[]{:S(2)}) copy-start(u32[32]{0:T(128)} %constant.75) | copy-start | bytes 388
  17.8 64.2 %copy-start.8 = (f32[2048]{0:T(1024)S(1)}, f32[2048]{0:T(1024)}, u32[]{:S(2)}) copy-start(f32[2048]{0:T(1024)} %param.23) | copy-start | bytes 24580
  47.5 43.5 %copy-start.5 = (bf16[1,8,2048]{2,1,0:T(8,128)(2,1)S(1)}, bf16[1,8,2048]{2,1,0:T(8,128)(2,1)}, u32[]{:S(2)}) copy-start(bf16[1,8,2048]{2,1,0:T(8,128)(2,1)} %param.22) | copy-start | bytes 98308
  82.3 22.9 %all-to-all-start = ((bf16[4,128,512]{2,1,0:T(8,128)(2,1)}), bf16[4,128,512]{2,1,0:T(8,128)(2,1)S(1)}, u32[]{:S(2)}, u32[]{:S(2)}) async-start(bf16[4,128,512]{2,1,0:T(8,128)(2,1)} %bitcast.71), calls=%async_computation | async-start | bytes 1048576 | tf_op jit(solution)/shard_map/all_to_all | solution.py:66
  86.6 28.0 %copy-start.4 = (bf16[8,1024]{1,0:T(8,128)(2,1)}, bf16[8,1024]{1,0:T(8,128)(2,1)S(1)}, u32[]{:S(2)}) copy-start(bf16[8,1024]{1,0:T(8,128)(2,1)S(1)} %divide_convert_fusion) | copy-start | bytes 49156
  105.1 19.6 %all-to-all-start.2 = ((bf16[4,128,512]{2,1,0:T(8,128)(2,1)}), bf16[4,128,512]{2,1,0:T(8,128)(2,1)S(1)}, u32[]{:S(2)}, u32[]{:S(2)}) async-start(bf16[4,128,512]{2,1,0:T(8,128)(2,1)} %bitcast.70), calls=%async_computation.2 | async-start | bytes 1048576 | tf_op jit(solution)/shard_map/all_to_all | solution.py:67
  109.9 28.5 %all-reduce.3.cloned.1.call-start = ((), (), s32[]{:S(2)}) async-start(), calls=%async_computation.7 | async-start | bytes 524288 | tf_op jit(solution)/shard_map/psum | solution.py:123
  114.6 1.9 %copy-start = (f32[4,512,512]{2,1,0:T(8,128)}, f32[4,512,512]{2,1,0:T(8,128)S(1)}, u32[]{:S(2)}) copy-start(f32[4,512,512]{2,1,0:T(8,128)S(1)} %get-tuple-element.53) | copy-start | bytes 12582916
  128.3 13.8 %copy-start.7 = (bf16[1,8,1024]{2,1,0:T(8,128)(2,1)S(1)}, bf16[1,8,1024]{2,1,0:T(8,128)(2,1)}, u32[]{:S(2)}) copy-start(bf16[1,8,1024]{2,1,0:T(8,128)(2,1)} %param.18) | copy-start | bytes 49156
  129.7 33.2 %all-to-all-start.3 = ((bf16[4,128,512]{2,1,0:T(8,128)(2,1)}), bf16[4,128,512]{2,1,0:T(8,128)(2,1)S(1)}, u32[]{:S(2)}, u32[]{:S(2)}) async-start(bf16[4,128,512]{2,1,0:T(8,128)(2,1)} %convert_element_type.56), calls=%async_computation.3 | async-start | bytes 1048576 | tf_op jit(solution)/shard_map/all_to_all | solution.py:72
  133.2 28.4 %reduce-scatter.5.cloned.1.call-start = ((), (), s32[]{:S(2)}) async-start(), calls=%async_computation.8 | async-start | bytes 163840 | tf_op jit(solution)/shard_map/reduce_scatter | solution.py:124
Sparse Core Ops, SparseCore 0:
  48.5 17.4 reduce-scatter.2
  113.7 24.6 all-reduce.2
  142.2 19.2 reduce-scatter.4
where the time goes:
time: 171 us
  blocking collectives  89.3 us (52%)
  starting transfers between devices  18.1 us (11%)
  waiting for transfers between devices  17.7 us (10%)
  local copies, waits for them, and re-layouts  15 us (9%)
  between operations  14.7 us (9%)
  matrix products  12.6 us (7%)
  other arithmetic  3.38 us (2%)
    all_gather x1, blocking collectives, body(): gathered_query = lax.all_gather(audio_query[0], 'seq', axis=0, tiled=True)  17.8 us
    unnamed x1, blocking collectives  15.7 us
    all_gather x1, blocking collectives, audio_block(): lax.all_gather(own_features, 'seq', axis=0, tiled=True)  13.9 us
    all_gather x1, blocking collectives, body(): gathered_key = lax.all_gather(audio_key[0], 'seq', axis=0, tiled=True)  13.2 us
    all_gather x1, blocking collectives, body(): gathered_value = lax.all_gather(audio_value[0], 'seq', axis=0, tiled=True)  13.2 us
    pmax x1, blocking collectives, audio_listen(): peak_value = lax.pmax(local_peak, 'seq')  11 us
    all_to_all x1, waiting for transfers between devices, video_self(): lax.all_to_all(spread(values_in), 'seq', split_axis=0, concat_axis=0, til...  7.52 us
    unnamed x27, local copies, waits for them, and re-layouts  6.86 us
  transfers between devices with their start and end apart: 7, of which 3 were waited for; matrix products, arithmetic and copies ran while one was open for 15% of the time, Pallas kernels for 0%

commit v1 on v0

--- a/solution.py
+++ b/solution.py
@@ -1,12 +1,22 @@
+import functools
 import math
 
 import jax
 import jax.numpy as jnp
 from jax import lax
+from jax.experimental import pallas as pl
+from jax.experimental.pallas import tpu as pltpu
 from jax.sharding import PartitionSpec as P
 
 VHEAD = 128
 CHEAD = 64
+LANES = 128
+F32 = jnp.float32
+BF16 = jnp.bfloat16
+LOG2E = math.log2(math.e)
+MIB = 1024 * 1024
+NT = (((1,), (1,)), ((), ()))
+TN = (((0,), (0,)), ((), ()))
 
 
 def attend_rows(queries, keys_in, values_in, head_count):
@@ -98,11 +108,9 @@
         value_heads,
         preferred_element_type=jnp.float32,
     )
-    totals, weighted = (totals, weighted.reshape(queries.shape[0], head_count * head_size))
-    totals, weighted = (
-        lax.psum_scatter(totals, "seq", scatter_dimension=0, tiled=True),
-        lax.psum_scatter(weighted, "seq", scatter_dimension=0, tiled=True),
-    )
+    weighted = weighted.reshape(queries.shape[0], head_count * head_size)
+    totals = lax.psum_scatter(totals, "seq", scatter_dimension=0, tiled=True)
+    weighted = lax.psum_scatter(weighted, "seq", scatter_dimension=0, tiled=True)
     return (weighted / jnp.repeat(totals, head_size, axis=1)).astype(jnp.bfloat16)
 
 
@@ -129,64 +137,401 @@
     ).astype(jnp.bfloat16)
 
 
-def body(
-    video_query,
-    video_key,
-    video_value,
-    cross_query,
-    audio_key,
-    audio_value,
-    audio_query,
-    cross_key,
-    cross_value,
-    audio_input,
-    norm_gain,
-    up_weight,
-    down_weight,
-):
-    mixed_list, heard_list, seen_list, output_list = ([], [], [], [])
-    cross_heads = cross_query.shape[2] // CHEAD
-    mixed_list.append(video_self(video_query[0], video_key[0], video_value[0]))
-    gathered_query = lax.all_gather(audio_query[0], "seq", axis=0, tiled=True)
-    gathered_key = lax.all_gather(audio_key[0], "seq", axis=0, tiled=True)
-    gathered_value = lax.all_gather(audio_value[0], "seq", axis=0, tiled=True)
-    heard_list.append(attend(cross_query[0], gathered_key, gathered_value, cross_heads))
-    audio_seen = audio_listen(gathered_query, cross_key[0], cross_value[0], cross_heads)
-    seen_list.append(audio_seen)
-    output_list.append(audio_block(audio_input[0], audio_seen, norm_gain, up_weight, down_weight))
+def general_body(vq, vk, vv, cq, ak, av, aq, ck, cv, ai, gain, up, down):
+    cross_heads = cq.shape[1] // CHEAD
+    mixed = video_self(vq, vk, vv)
+    gathered_query = lax.all_gather(aq, "seq", axis=0, tiled=True)
+    gathered_key = lax.all_gather(ak, "seq", axis=0, tiled=True)
+    gathered_value = lax.all_gather(av, "seq", axis=0, tiled=True)
+    heard = attend(cq, gathered_key, gathered_value, cross_heads)
+    seen = audio_listen(gathered_query, ck, cv, cross_heads)
+    mlp = audio_block(ai, seen, gain, up, down)
+    return mixed, heard, seen, mlp
+
+
+def vmem():
+    return pl.BlockSpec(memory_space=pltpu.VMEM)
+
+
+def smem():
+    return pl.BlockSpec(memory_space=pltpu.SMEM)
+
+
+def sds(shape, dtype=BF16):
+    return jax.ShapeDtypeStruct(shape, dtype)
+
+
+def call(kernel, ins, outs, flops=0, moved=0, limit=32, scalars=0):
+    return pl.pallas_call(
+        kernel,
+        out_shape=tuple(outs),
+        in_specs=[smem()] * scalars + [vmem()] * (len(ins) - scalars),
+        out_specs=tuple(vmem() for _ in outs),
+        compiler_params=pltpu.CompilerParams(vmem_limit_bytes=limit * MIB),
+        cost_estimate=pl.CostEstimate(flops=flops, bytes_accessed=moved, transcendentals=0),
+    )(*ins)
+
+
+def shift(value, by):
+    n = lax.axis_size("seq")
+    return lax.ppermute(value, "seq", [(i, (i + by) % n) for i in range(n)])
+
+
+def parts3(value):
+    first = value.astype(BF16).astype(F32)
+    second = (value - first).astype(BF16).astype(F32)
+    return first, second, value - first - second
+
+
+def pack_kernel(n, first, width, with_audio, place, q, k, v, *rest):
+    audio, outs = (rest[:3], rest[3:]) if with_audio else ((), rest)
+    tokens = q.shape[0]
+    group = q.shape[1] // n
+    me = place[0]
+    if with_audio:
+        key, value, line = audio
+        half = key.shape[1]
+        mine = line[:, pl.ds(pl.multiple_of(place[1] * half, LANES), half)].astype(F32)
+        rows = []
+        for part in (key[...].astype(F32), value[...].astype(F32), mine):
+            rows += [part[:, c : c + width] for c in range(0, half, width)]
+        extra = jnp.concatenate(rows, axis=0).astype(BF16)
+    for s in range(n):
+        dest = lax.rem(me + s, n)
+        at = pl.ds(pl.multiple_of(dest * group + first, LANES), width)
+        for i, ref in enumerate((q, k, v)):
+            outs[s][i * tokens : (i + 1) * tokens, :] = ref[:, at]
+        if with_audio:
+            outs[s][3 * tokens :, :] = extra
+
+
+def unfold(tail, index, rows, columns, width):
+    per = columns // width
+    return jnp.concatenate(
+        [tail[(index * per + c) * rows : (index * per + c + 1) * rows] for c in range(per)], axis=1
+    )
+
+
+def attend_kernel(n, tokens, *refs):
+    pieces, outs = refs[:n], refs[n:]
+    width = pieces[0].shape[1]
+    scale = LOG2E / math.sqrt(VHEAD)
+    for h in range(width // VHEAD):
+        cols = slice(h * VHEAD, (h + 1) * VHEAD)
+        keys = jnp.concatenate([p[tokens : 2 * tokens, cols] for p in pieces], axis=0)
+        values = jnp.concatenate([p[2 * tokens : 3 * tokens, cols] for p in pieces], axis=0)
+        for p, out in zip(pieces, outs):
+            s = lax.dot_general(p[0:tokens, cols], keys, NT, preferred_element_type=F32)
+            s = s * scale
+            w = jnp.exp2(s - jnp.max(s, axis=1, keepdims=True))
+            total = jnp.sum(w, axis=1, keepdims=True)
+            o = jnp.dot(w.astype(BF16), values, preferred_element_type=F32)
+            out[:, cols] = (o / total).astype(BF16)
+
+
+def unpack_kernel(n, widths, place, *refs):
+    pieces, out = refs[:-1], refs[-1]
+    me = place[0]
+    group = sum(widths)
+    first = 0
+    for c, width in enumerate(widths):
+        for s in range(n):
+            dest = lax.rem(me + s, n)
+            at = pl.ds(pl.multiple_of(dest * group + first, LANES), width)
+            out[:, at] = pieces[c * n + s][...]
+        first += width
+
+
+def low_half(shape):
+    return lax.broadcasted_iota(jnp.int32, shape, 1) < CHEAD
+
+
+def listen_kernel(n, *refs):
+    queries, keys, values, out = refs[:n], refs[n], refs[n + 1], refs[n + 2]
+    columns = keys.shape[1]
+    q = jnp.concatenate([p[...].astype(F32) for p in queries], axis=0)
+    rows = q.shape[0]
+    scale = LOG2E / math.sqrt(CHEAD)
+    low = low_half((rows, LANES))
+    lane = lax.broadcasted_iota(jnp.int32, (rows, LANES), 1)
+    stats = jnp.zeros((rows, LANES), F32)
+    heads = columns // CHEAD
+    for pair in range(columns // LANES):
+        cols = slice(pair * LANES, (pair + 1) * LANES)
+        qp = q[:, cols]
+        both = jnp.concatenate([jnp.where(low, qp, 0.0), jnp.where(low, 0.0, qp)], axis=0)
+        s = lax.dot_general(both.astype(BF16), keys[:, cols], NT, preferred_element_type=F32)
+        s = s * scale
+        peak = jnp.max(s, axis=1, keepdims=True)
+        w = jnp.exp2(s - peak)
+        total = jnp.sum(w, axis=1, keepdims=True)
+        o = jnp.dot(w.astype(BF16), values[:, cols], preferred_element_type=F32) / total
+        out[:, cols] = jnp.where(low, o[:rows], o[rows:]).astype(BF16)
+        for i in range(2):
+            head = 2 * pair + i
+            sel = slice(i * rows, (i + 1) * rows)
+            for j, part in enumerate(parts3(peak[sel]) + parts3(total[sel])):
+                stats = jnp.where(lane == j * heads + head, part, stats)
+    out[:, columns:] = stats.astype(BF16)
+
+
+def combine_kernel(n, tokens, rows, *refs):
+    got, pieces = refs[:n], refs[n : 2 * n]
+    gain, up = refs[2 * n], refs[2 * n + 1]
+    own_sum, sent_sum, seen, x_ref = refs[2 * n + 2 :]
+
+    @pl.when(pl.program_id(0) == 0)
+    def _():
+        columns = seen.shape[1]
+        heads = columns // CHEAD
+        width = pieces[0].shape[1]
+        peaks, totals, parts = [], [], []
+        for s in range(n):
+            whole = got[s][...].astype(F32)
+            if s:
+                whole = jnp.concatenate([whole[-s * rows :], whole[: -s * rows]], axis=0)
+            whole, stats = whole[:, :columns], whole[:, columns:]
+            piece = [stats[:, j * heads : (j + 1) * heads] for j in range(6)]
+            peaks.append(piece[0] + piece[1] + piece[2])
+            totals.append(piece[3] + piece[4] + piece[5])
+            parts.append(whole)
+        top = functools.reduce(jnp.maximum, peaks)
+        weight = [t * jnp.exp2(p - top) for t, p in zip(totals, peaks)]
+        every = functools.reduce(jnp.add, weight)
+        weight = [w / every for w in weight]
+        tails = [p[3 * tokens :, :].astype(F32) for p in pieces]
+        line = jnp.concatenate([unfold(t, 2, rows, columns, width) for t in tails], axis=0)
+        low = low_half((n * rows, LANES))
+        square = jnp.zeros((n * rows, 1), F32)
+        for pair in range(columns // LANES):
+            cols = slice(pair * LANES, (pair + 1) * LANES)
+            o = jnp.zeros((n * rows, LANES), F32)
+            for w, part in zip(weight, parts):
+                a, b = w[:, 2 * pair : 2 * pair + 1], w[:, 2 * pair + 1 : 2 * pair + 2]
+                o = o + jnp.where(low, a, b) * part[:, cols]
+            o = o.astype(BF16)
+            seen[:, cols] = o[:rows]
+            residual = line[:, cols] + o.astype(F32)
+            square = square + jnp.sum(residual * residual, axis=1, keepdims=True)
+            x_ref[:, cols] = (residual * gain[:, cols]).astype(BF16)
+        lane = lax.broadcasted_iota(jnp.int32, (n * rows, LANES), 1)
+        first, second, third = parts3(square)
+        spread = jnp.where(lane == 0, first, jnp.where(lane == 1, second, third))
+        spread = jnp.where(lane < 3, spread, 0.0)
+        own_sum[0, :, :LANES] = spread
+        sent_sum[0, :, :LANES] = spread.astype(BF16)
+
+    @pl.when(pl.program_id(0) > 0)
+    def _():
+        product = jnp.dot(x_ref[...], up[...], preferred_element_type=F32)
+        own_sum[0] = product
+        sent_sum[0] = product.astype(BF16)
+
+
+def combine(got, pieces, gain, up, tokens, rows, block):
+    n = len(got)
+    columns, units = up.shape
+    steps = units // block + 1
+    held = lambda ref: pl.BlockSpec(ref.shape, lambda i: (0,) * ref.ndim)
+    moved = pl.BlockSpec((1, n * rows, block), lambda i: (i, 0, 0))
+    return pl.pallas_call(
+        functools.partial(combine_kernel, n, tokens, rows),
+        grid=(steps,),
+        out_shape=(
+            sds((steps, n * rows, block), F32),
+            sds((steps, n * rows, block)),
+            sds((rows, columns)),
+        ),
+        in_specs=[held(r) for r in (*got, *pieces, gain)]
+        + [pl.BlockSpec((columns, block), lambda i: (0, jnp.maximum(i - 1, 0)))],
+        out_specs=(moved, moved, pl.BlockSpec((rows, columns), lambda i: (0, 0))),
+        scratch_shapes=[pltpu.VMEM((n * rows, columns), BF16)],
+        compiler_params=pltpu.CompilerParams(vmem_limit_bytes=32 * MIB),
+        cost_estimate=pl.CostEstimate(
+            flops=8 * n * rows * columns * units, bytes_accessed=4 * columns * units, transcendentals=0
+        ),
+    )(*got, *pieces, gain, up)
+
+
+def finish_kernel(n, features, own, other, down, *refs):
+    outs, hidden = refs[:n], refs[n]
+    rows = outs[0].shape[0]
+
+    @pl.when(pl.program_id(0) == 0)
+    def _():
+        square = own[0, :, :LANES] + other[0, :, :LANES].astype(F32)
+        square = jnp.sum(square, axis=1, keepdims=True)
+        scale = lax.rsqrt(square / features + 1e-6)
+        block = own.shape[2]
+        for i in range(1, own.shape[0]):
+            total = (own[i] + other[i].astype(F32)) * scale
+            hidden[:, (i - 1) * block : i * block] = jax.nn.gelu(total).astype(BF16)
+
+    product = jnp.dot(hidden[...], down[...], preferred_element_type=F32)
+    for s in range(n):
+        outs[s][...] = product[s * rows : (s + 1) * rows].astype(outs[s].dtype)
+
+
+def finish(own, other, down, n, rows, features, block):
+    units, columns = down.shape
+    held = lambda ref: pl.BlockSpec(ref.shape, lambda i: (0,) * ref.ndim)
+    return pl.pallas_call(
+        functools.partial(finish_kernel, n, features),
+        grid=(columns // block,),
+        out_shape=(sds((rows, columns), F32),) + (sds((rows, columns)),) * (n - 1),
+        in_specs=[held(own), held(other), pl.BlockSpec((units, block), lambda i: (0, i))],
+        out_specs=(pl.BlockSpec((rows, block), lambda i: (0, i)),) * n,
+        scratch_shapes=[pltpu.VMEM((n * rows, units), BF16)],
+        compiler_params=pltpu.CompilerParams(vmem_limit_bytes=32 * MIB),
+        cost_estimate=pl.CostEstimate(
+            flops=8 * n * rows * columns * units, bytes_accessed=4 * columns * units, transcendentals=0
+        ),
+    )(own, other, down)
+
+
+def heard_kernel(n, tokens, rows, q, *refs):
+    pieces, out = refs[:n], refs[n]
+    columns = q.shape[1]
+    width = pieces[0].shape[1]
+    tails = [p[3 * tokens :, :].astype(F32) for p in pieces]
+    keys = jnp.concatenate([unfold(t, 0, rows, columns, width) for t in tails], axis=0)
+    values = jnp.concatenate([unfold(t, 1, rows, columns, width) for t in tails], axis=0)
+    count = n * rows
+    low = low_half((count, LANES))
+    scale = LOG2E / math.sqrt(CHEAD)
+    for pair in range(columns // LANES):
+        cols = slice(pair * LANES, (pair + 1) * LANES)
+
+        def both(x):
+            x = x[:, cols]
+            return jnp.concatenate([jnp.where(low, x, 0.0), jnp.where(low, 0.0, x)], axis=0).astype(BF16)
+
+        s = lax.dot_general(both(keys), q[:, cols], NT, preferred_element_type=F32) * scale
+        probs = []
+        for i in range(2):
+            t = s[i * count : (i + 1) * count]
+            w = jnp.exp2(t - jnp.max(t, axis=0, keepdims=True))
+            probs.append(w / jnp.sum(w, axis=0, keepdims=True))
+        w = jnp.concatenate(probs, axis=0).astype(BF16)
+        out[:, cols] = lax.dot_general(w, both(values), TN, preferred_element_type=F32).astype(BF16)
+
+
+def add_kernel(own, *refs):
+    total = own[...]
+    for ref in refs[:-1]:
+        total = total + ref[...].astype(F32)
+    refs[-1][...] = total.astype(BF16)
+
+
+def short_body(vq, vk, vv, cq, ak, av, aq, ck, cv, ai, gain, up, down):
+    n = lax.axis_size("seq")
+    tokens = vq.shape[0]
+    rows = aq.shape[0]
+    columns = aq.shape[1]
+    features = ai.shape[1]
+    tp = lax.axis_index("tp")
+    place = jnp.stack([lax.axis_index("seq"), tp]).astype(jnp.int32)
+    group = vq.shape[1] // n
+    head_split = [group // VHEAD // 2 * VHEAD, group - group // VHEAD // 2 * VHEAD]
+    video_bytes = 6 * vq.size
+
+    queries = [aq] + [shift(aq, s) for s in range(1, n)]
+
+    wide = head_split[0]
+    extra = 3 * rows * columns // wide
+    packed = call(
+        functools.partial(pack_kernel, n, 0, wide, True),
+        (place, vq, vk, vv, ak, av, ai),
+        [sds((3 * tokens + extra, wide))] * n,
+        moved=video_bytes,
+        scalars=1,
+    )
+    chunk_a = [packed[0]] + [shift(packed[s], s) for s in range(1, n)]
+
+    (share,) = call(
+        functools.partial(listen_kernel, n),
+        (*queries, ck, cv),
+        [sds((n * rows, columns + LANES))],
+        flops=8 * n * rows * tokens * columns,
+        moved=4 * ck.size,
+    )
+    shares = [share] + [shift(share, s) for s in range(1, n)]
+
+    wide_b = head_split[1]
+    packed_b = call(
+        functools.partial(pack_kernel, n, wide, wide_b, False),
+        (place, vq, vk, vv),
+        [sds((3 * tokens, wide_b))] * n,
+        moved=video_bytes,
+        scalars=1,
+    )
+    chunk_b = [packed_b[0]] + [shift(packed_b[s], s) for s in range(1, n)]
+
+    own_gain = lax.dynamic_slice_in_dim(gain.reshape(1, -1), tp * columns, columns, 1)
+    own_sum, sent_sum, seen = combine(shares, chunk_a, own_gain, up, tokens, rows, 512)
+    other_sum = lax.ppermute(sent_sum, "tp", [(0, 1), (1, 0)])
+    results = finish(own_sum, other_sum, down, n, rows, features, 512)
+    back = [results[0]] + [shift(results[s], -s) for s in range(1, n)]
+    (mlp,) = call(add_kernel, back, [sds((rows, columns))])
+
+    flops = 8 * n * n * tokens * tokens
+    def attended(chunk, width):
+        outs = call(
+            functools.partial(attend_kernel, n, tokens),
+            chunk,
+            [sds((tokens, width))] * n,
+            flops=flops * width,
+            moved=4 * n * tokens * width * 2,
+        )
+        return [outs[0]] + [shift(outs[s], -s) for s in range(1, n)]
+
+    mixed_a = attended(chunk_a, wide)
+    (heard,) = call(
+        functools.partial(heard_kernel, n, tokens, rows),
+        (cq, *chunk_a),
+        [sds(cq.shape)],
+        flops=8 * n * rows * cq.size,
+        moved=4 * cq.size,
+    )
+    mixed_b = attended(chunk_b, wide_b)
+    (mixed,) = call(
+        functools.partial(unpack_kernel, n, head_split),
+        (place, *mixed_a, *mixed_b),
+        [sds(vq.shape)],
+        moved=4 * vq.size,
+        scalars=1,
+    )
+    return mixed, heard, seen, mlp
+
+
+def fits(vq, cq, aq, up, down):
+    n = lax.axis_size("seq")
+    heads = vq.shape[1] // VHEAD
     return (
-        jnp.stack(mixed_list),
-        jnp.stack(heard_list),
-        jnp.stack(seen_list),
-        jnp.stack(output_list),
-    )
+        1 < n <= 8
+        and lax.axis_size("tp") == 2
+        and heads % (2 * n) == 0
+        and vq.shape[0] == LANES
+        and n * vq.shape[0] <= 1024
+        and aq.shape[0] % 8 == 0
+        and n * aq.shape[0] <= 64
+        and 6 * (aq.shape[1] // CHEAD) <= LANES
+        and aq.shape[1] % (heads // n // 2 * VHEAD) == 0
+        and up.shape[1] % 512 == 0
+        and down.shape[1] % 512 == 0
+    )
+
+
+def body(*args):
+    *arrays, gain, up, down = args
+    arrays = [a[0] for a in arrays]
+    path = short_body if fits(arrays[0], arrays[3], arrays[6], up, down) else general_body
+    return tuple(out[None] for out in path(*arrays, gain, up, down))
 
 
 def solution(mesh):
-    placed = (
-        P(("clips", "dp"), "seq", "tp"),
-        P(("clips", "dp"), "seq", "tp"),
-        P(("clips", "dp"), "seq", "tp"),
-        P(("clips", "dp"), "seq", "tp"),
-        P(("clips", "dp"), "seq", "tp"),
-        P(("clips", "dp"), "seq", "tp"),
-        P(("clips", "dp"), "seq", "tp"),
-        P(("clips", "dp"), "seq", "tp"),
-        P(("clips", "dp"), "seq", "tp"),
-        P(("clips", "dp"), "seq", None),
-        P(),
-        P("tp", "seq"),
-        P("seq", "tp"),
-    )
+    rows = P(("clips", "dp"), "seq", "tp")
+    placed = (rows,) * 9 + (P(("clips", "dp"), "seq", None), P(), P("tp", "seq"), P("seq", "tp"))
     return jax.shard_map(
-        body,
-        mesh=mesh,
-        in_specs=placed,
-        out_specs=(
-            P(("clips", "dp"), "seq", "tp"),
-            P(("clips", "dp"), "seq", "tp"),
-            P(("clips", "dp"), "seq", "tp"),
-            P(("clips", "dp"), "seq", "tp"),
-        ),
-        check_vma=False,
-    )
+        body, mesh=mesh, in_specs=placed, out_specs=(rows,) * 4, check_vma=False
+    )

time: 171 us -> 92 us (0.54)
  blocking collectives: 89.3 us -> 0 us
  Pallas kernels: 0 us -> 17.3 us
  starting transfers between devices: 18.1 us -> 32.2 us
  between operations: 14.7 us -> 0.72 us
  matrix products: 12.6 us -> 0 us
  waiting for transfers between devices: 17.7 us -> 28.1 us
  other arithmetic: 3.38 us -> 0.08 us
  local copies, waits for them, and re-layouts: 15 us -> 12.9 us
    all_gather x5 -> x0, blocking collectives: 62.6 us -> none  [the longest x1 17.8 us: body(): gathered_query = lax.all_gather(audio_query[0], 'seq', axis=0, tiled=True)]
    ppermute x0 -> x22, starting transfers between devices: none -> 32.2 us  [the longest x21 30.7 us: shift(): return lax.ppermute(value, 'seq', [(i, (i + by) % n) for i in range(n)])]
    ppermute x0 -> x22, waiting for transfers between devices: none -> 28.1 us  [the longest x21 28.1 us: shift(): return lax.ppermute(value, 'seq', [(i, (i + by) % n) for i in range(n)])]
    all_to_all x4 -> x0, starting transfers between devices: 18 us -> none  [the longest x1 6.32 us: video_self(): lax.all_to_all(shaped.reshape(seq_count, block_tokens, group_width), 'seq...]
    pallas_call x0 -> x10, Pallas kernels: none -> 17.3 us  [the longest x8 12.6 us: call(): pl.pallas_call(kernel, out_shape=tuple(outs), in_specs=[smem()] * scalars...]
    unnamed x1 -> x0, blocking collectives: 15.7 us -> none
    dot_general x8 -> x0, matrix products: 12.6 us -> none  [the longest x1 3.72 us: audio_block(): jnp.dot(hidden, down_weight, preferred_element_type=jnp.float32)]
    pmax x1 -> x0, blocking collectives: 11 us -> none  [audio_listen(): peak_value = lax.pmax(local_peak, 'seq')]
  transfers between devices with their start and end apart: 7 -> 22, of which waited for: 3 -> 6; matrix products, arithmetic and copies ran while one was open for 15% -> 1% of each run, Pallas kernels for 0% -> 18%
where the time goes in v1:
time: 92 us; the launch traced here: 91.3 us
  starting transfers between devices  32.2 us (35%)
  waiting for transfers between devices  28.1 us (31%)
  Pallas kernels  17.3 us (19%)
  local copies, waits for them, and re-layouts  12.9 us (14%)
    ppermute x21, starting transfers between devices, shift(): return lax.ppermute(value, 'seq', [(i, (i + by) % n) for i in range(n)])  30.7 us
    ppermute x21, waiting for transfers between devices, shift(): return lax.ppermute(value, 'seq', [(i, (i + by) % n) for i in range(n)])  28.1 us
    pallas_call x8, Pallas kernels, call(): pl.pallas_call(kernel, out_shape=tuple(outs), in_specs=[smem()] * scalars...  12.6 us
    unnamed x28, local copies, waits for them, and re-layouts  12.2 us
    pallas_call x1, Pallas kernels, combine(): pl.pallas_call(functools.partial(combine_kernel, n, tokens, rows), grid=(...  3.28 us
  transfers between devices with their start and end apart: 22, of which 6 were waited for; matrix products, arithmetic and copies ran while one was open for 1% of the time, Pallas kernels for 18%

profile of v1, /device:TPU:0, one launch (start us, length us, event | category | flops | bytes accessed | tf_op | source)
XLA Modules:
  0.0 91.3 jit_solution(18431000613732953530)
XLA Ops:
  6.7 3.1 %collective-permute-start = (bf16[480,256]{1,0:T(8,128)(2,1)S(1)}, bf16[480,256]{1,0:T(8,128)(2,1)S(1)}, u32[]{:S(2)}, u32[]{:S(2)}) collective-permute-start(bf16[480,256]{1,0:T(8,128)(2,1)S(1)} %get-tuple-element.28), channel_id=1, source_target_pairs={{0,4},{4,8},{8,12},{12,0},{1,5},{5,9},{9,13},{13,1},{2,6},{6,10},{... | collective-permute-start | bytes 737288 | tf_op jit(solution)/shard_map/ppermute | solution.py:177
  9.8 2.1 %collective-permute-start.14 = (bf16[8,1024]{1,0:T(8,128)(2,1)}, bf16[8,1024]{1,0:T(8,128)(2,1)S(1)}, u32[]{:S(2)}, u32[]{:S(2)}) collective-permute-start(bf16[8,1024]{1,0:T(8,128)(2,1)} %bitcast.30), channel_id=1, source_target_pairs={{0,12},{4,0},{8,4},{12,8},{1,13},{5,1},{9,5},{13,9},{2,14},{6,2},{... | collective-permute-start | bytes 49160 | tf_op jit(solution)/shard_map/ppermute | solution.py:177
  12.8 1.6 %collective-permute-start.12 = (bf16[8,1024]{1,0:T(8,128)(2,1)}, bf16[8,1024]{1,0:T(8,128)(2,1)S(1)}, u32[]{:S(2)}, u32[]{:S(2)}) collective-permute-start(bf16[8,1024]{1,0:T(8,128)(2,1)} %bitcast.32), channel_id=1, source_target_pairs={{0,4},{4,8},{8,12},{12,0},{1,5},{5,9},{9,13},{13,1},{2,6},{6,10},{... | collective-permute-start | bytes 49160 | tf_op jit(solution)/shard_map/ppermute | solution.py:177
  14.4 2.9 %collective-permute-done.14.refs_3_ = bf16[8,1024]{1,0:T(8,128)(2,1)S(1)} collective-permute-done((bf16[8,1024]{1,0:T(8,128)(2,1)}, bf16[8,1024]{1,0:T(8,128)(2,1)S(1)}, u32[]{:S(2)}, u32[]{:S(2)}) %collective-permute-start.14) | collective-permute-done | bytes 16416 | tf_op jit(solution)/shard_map/ppermute | solution.py:177
  17.3 1.9 %collective-permute-done.13.refs_2_ = bf16[8,1024]{1,0:T(8,128)(2,1)S(1)} collective-permute-done((bf16[8,1024]{1,0:T(8,128)(2,1)}, bf16[8,1024]{1,0:T(8,128)(2,1)S(1)}, u32[]{:S(2)}, u32[]{:S(2)}) %collective-permute-start.13) | collective-permute-done | bytes 16416 | tf_op jit(solution)/shard_map/ppermute | solution.py:177
  21.8 2.0 %shard_map.162.refs_0_ = bf16[32,1152]{1,0:T(8,128)(2,1)S(1)} custom-call(bf16[8,1024]{1,0:T(8,128)(2,1)S(1)} %bitcast.33, bf16[8,1024]{1,0:T(8,128)(2,1)S(1)} %collective-permute-done.12.refs_1_, bf16[8,1024]{1,0:T(8,128)(2,1)S(1)} %collective-permute-done.13.refs_2_, bf16[8,1024]{1,0:T(8,128)(2,1)S(1)} %collective-permute-done.14.refs_3_, ...), custom_call_target="tpu_custom_call" | custom-call | flops 33554432 | bytes 524288 | tf_op jit(solution)/shard_map/pallas_call | solution.py:165
  23.8 1.5 %collective-permute-start.17 = (bf16[32,1152]{1,0:T(8,128)(2,1)S(1)}, bf16[32,1152]{1,0:T(8,128)(2,1)S(1)}, u32[]{:S(2)}, u32[]{:S(2)}) collective-permute-start(bf16[32,1152]{1,0:T(8,128)(2,1)S(1)} %shard_map.162.refs_0_), channel_id=1, source_target_pairs={{0,12},{4,0},{8,4},{12,8},{1,13},{5,1},{9,5},{13,9},{2,14},{6,2},{... | collective-permute-start | bytes 221192 | tf_op jit(solution)/shard_map/ppermute | solution.py:177
  25.6 2.6 %collective-permute-start.2 = (bf16[480,256]{1,0:T(8,128)(2,1)S(1)}, bf16[480,256]{1,0:T(8,128)(2,1)S(1)}, u32[]{:S(2)}, u32[]{:S(2)}) collective-permute-start(bf16[480,256]{1,0:T(8,128)(2,1)S(1)} %get-tuple-element.30), channel_id=1, source_target_pairs={{0,12},{4,0},{8,4},{12,8},{1,13},{5,1},{9,5},{13,9},{2,14},{6,2},{... | collective-permute-start | bytes 737288 | tf_op jit(solution)/shard_map/ppermute | solution.py:177
  28.2 1.4 %collective-permute-done.17.refs_3_ = bf16[32,1152]{1,0:T(8,128)(2,1)S(1)} collective-permute-done((bf16[32,1152]{1,0:T(8,128)(2,1)S(1)}, bf16[32,1152]{1,0:T(8,128)(2,1)S(1)}, u32[]{:S(2)}, u32[]{:S(2)}) %collective-permute-start.17) | collective-permute-done | bytes 73760 | tf_op jit(solution)/shard_map/ppermute | solution.py:177
  33.0 15.5 %collective-permute-done.16.refs_2_ = bf16[32,1152]{1,0:T(8,128)(2,1)S(1)} collective-permute-done((bf16[32,1152]{1,0:T(8,128)(2,1)S(1)}, bf16[32,1152]{1,0:T(8,128)(2,1)S(1)}, u32[]{:S(2)}, u32[]{:S(2)}) %collective-permute-start.16) | collective-permute-done | bytes 73760 | tf_op jit(solution)/shard_map/ppermute | solution.py:177
  49.8 2.6 %collective-permute-start.8 = (bf16[384,256]{1,0:T(8,128)(2,1)S(1)}, bf16[384,256]{1,0:T(8,128)(2,1)S(1)}, u32[]{:S(2)}, u32[]{:S(2)}) collective-permute-start(bf16[384,256]{1,0:T(8,128)(2,1)S(1)} %get-tuple-element.38), channel_id=1, source_target_pairs={{0,12},{4,0},{8,4},{12,8},{1,13},{5,1},{9,5},{13,9},{2,14},{6,2},{... | collective-permute-start | bytes 589832 | tf_op jit(solution)/shard_map/ppermute | solution.py:177
  53.1 2.2 %copy-done.1 = bf16[1024,2048]{1,0:T(8,128)(2,1)S(1)} copy-done((bf16[1024,2048]{1,0:T(8,128)(2,1)S(1)}, bf16[1024,2048]{1,0:T(8,128)(2,1)}, u32[]{:S(2)}) %copy-start.1) | copy-done | bytes 4194328
  55.3 3.3 %shard_map.163 = (f32[5,32,512]{2,1,0:T(8,128)S(1)}, bf16[5,32,512]{2,1,0:T(8,128)(2,1)S(1)}, bf16[8,1024]{1,0:T(8,128)(2,1)}) custom-call(bf16[32,1152]{1,0:T(8,128)(2,1)S(1)} %shard_map.162.refs_0_, bf16[32,1152]{1,0:T(8,128)(2,1)S(1)} %collective-permute-done.15.refs_1_, bf16[32,1152]{1,0:T(8,128)(2,1)S(1)} %collective-permute-done.16.refs_2_, ...), custom_call_target="tpu_custom_call" | custom-call | flops 536870912 | bytes 8388608 | tf_op jit(solution)/shard_map/pallas_call | solution.py:337
  58.6 1.5 %collective-permute-start.18 = (bf16[5,32,512]{2,1,0:T(8,128)(2,1)S(1)}, bf16[5,32,512]{2,1,0:T(8,128)(2,1)S(1)}, u32[]{:S(2)}, u32[]{:S(2)}) collective-permute-start(bf16[5,32,512]{2,1,0:T(8,128)(2,1)S(1)} %get-tuple-element.45), channel_id=1, source_target_pairs={{0,2},{2,0},{1,3},{3,1},{4,6},{6,4},{5,7},{7,5},{8,10},{10,8},{9,1... | collective-permute-start | bytes 491528 | tf_op jit(solution)/shard_map/ppermute | solution.py:472
  60.1 5.0 %collective-permute-done.7.refs_2_ = bf16[384,256]{1,0:T(8,128)(2,1)S(1)} collective-permute-done((bf16[384,256]{1,0:T(8,128)(2,1)S(1)}, bf16[384,256]{1,0:T(8,128)(2,1)S(1)}, u32[]{:S(2)}, u32[]{:S(2)}) %collective-permute-start.7) | collective-permute-done | bytes 196640 | tf_op jit(solution)/shard_map/ppermute | solution.py:177
  65.1 2.3 %shard_map.159 = (bf16[128,256]{1,0:T(8,128)(2,1)S(1)}, bf16[128,256]{1,0:T(8,128)(2,1)S(1)}, bf16[128,256]{1,0:T(8,128)(2,1)S(1)}, bf16[128,256]{1,0:T(8,128)(2,1)S(1)}) custom-call(bf16[384,256]{1,0:T(8,128)(2,1)S(1)} %get-tuple-element.35.refs_0_, bf16[384,256]{1,0:T(8,128)(2,1)S(1)} %collective-permute-done.6.refs_1_, ...), custom_call_target="tpu_custom_call" | custom-call | flops 536870912 | bytes 1048576 | tf_op jit(solution)/shard_map/pallas_call | solution.py:165
  67.4 2.7 %collective-permute-start.9 = (bf16[128,256]{1,0:T(8,128)(2,1)S(1)}, bf16[128,256]{1,0:T(8,128)(2,1)S(1)}, u32[]{:S(2)}, u32[]{:S(2)}) collective-permute-start(bf16[128,256]{1,0:T(8,128)(2,1)S(1)} %get-tuple-element.40), channel_id=1, source_target_pairs={{0,12},{4,0},{8,4},{12,8},{1,13},{5,1},{9,5},{13,9},{2,14},{6,2},{... | collective-permute-start | bytes 196616 | tf_op jit(solution)/shard_map/ppermute | solution.py:177
  70.1 2.5 %collective-permute-start.10 = (bf16[128,256]{1,0:T(8,128)(2,1)S(1)}, bf16[128,256]{1,0:T(8,128)(2,1)S(1)}, u32[]{:S(2)}, u32[]{:S(2)}) collective-permute-start(bf16[128,256]{1,0:T(8,128)(2,1)S(1)} %get-tuple-element.41), channel_id=1, source_target_pairs={{0,8},{4,12},{8,0},{12,4},{1,9},{5,13},{9,1},{13,5},{2,10},{6,14},... | collective-permute-start | bytes 196616 | tf_op jit(solution)/shard_map/ppermute | solution.py:177
  72.6 2.2 %shard_map.157 = (bf16[128,256]{1,0:T(8,128)(2,1)S(1)}, bf16[128,256]{1,0:T(8,128)(2,1)S(1)}, bf16[128,256]{1,0:T(8,128)(2,1)S(1)}, bf16[128,256]{1,0:T(8,128)(2,1)S(1)}) custom-call(bf16[480,256]{1,0:T(8,128)(2,1)S(1)} %get-tuple-element.27.refs_0_.refs_4_, bf16[480,256]{1,0:T(8,128)(2,1)S(1)} %collective-permute-done.refs_1_.refs_5_, ...), custom_call_target="tpu_custom_call" | custom-call | flops 536870912 | bytes 1048576 | tf_op jit(solution)/shard_map/pallas_call | solution.py:165
  74.9 3.9 %collective-permute-start.3 = (bf16[128,256]{1,0:T(8,128)(2,1)S(1)}, bf16[128,256]{1,0:T(8,128)(2,1)S(1)}, u32[]{:S(2)}, u32[]{:S(2)}) collective-permute-start(bf16[128,256]{1,0:T(8,128)(2,1)S(1)} %get-tuple-element.32), channel_id=1, source_target_pairs={{0,12},{4,0},{8,4},{12,8},{1,13},{5,1},{9,5},{13,9},{2,14},{6,2},{... | collective-permute-start | bytes 196616 | tf_op jit(solution)/shard_map/ppermute | solution.py:177
  79.4 1.4 %shard_map.164 = (f32[8,1024]{1,0:T(8,128)S(1)}, bf16[8,1024]{1,0:T(8,128)(2,1)S(1)}, bf16[8,1024]{1,0:T(8,128)(2,1)S(1)}, bf16[8,1024]{1,0:T(8,128)(2,1)S(1)}) custom-call(f32[5,32,512]{2,1,0:T(8,128)S(1)} %get-tuple-element.44.own, bf16[5,32,512]{2,1,0:T(8,128)(2,1)S(1)} %collective-permute-done.18.other, bf16[2048,1024]{1,0:T(8,128)(2,1)S(1)} %copy-done), custom_call_target="tpu_custom_call" | custom-call | flops 536870912 | bytes 8388608 | tf_op jit(solution)/shard_map/pallas_call | solution.py:378
  80.8 3.3 %collective-permute-start.19 = (bf16[8,1024]{1,0:T(8,128)(2,1)S(1)}, bf16[8,1024]{1,0:T(8,128)(2,1)S(1)}, u32[]{:S(2)}, u32[]{:S(2)}) collective-permute-start(bf16[8,1024]{1,0:T(8,128)(2,1)S(1)} %get-tuple-element.47), channel_id=1, source_target_pairs={{0,12},{4,0},{8,4},{12,8},{1,13},{5,1},{9,5},{13,9},{2,14},{6,2},{... | collective-permute-start | bytes 49160 | tf_op jit(solution)/shard_map/ppermute | solution.py:177
  85.2 2.8 %shard_map.161 = bf16[128,1024]{1,0:T(8,128)(2,1)} custom-call(bf16[128,1024]{1,0:T(8,128)(2,1)S(1)} %bitcast.25, bf16[480,256]{1,0:T(8,128)(2,1)S(1)} %get-tuple-element.27.refs_0_.refs_4_, bf16[480,256]{1,0:T(8,128)(2,1)S(1)} %collective-permute-done.refs_1_.refs_5_, bf16[480,256]{1,0:T(8,128)(2,1)S(1)} %collective-permute-done.1.refs_2_.refs_6_, ...), custom_call_target="tpu_custom_call" | custom-call | flops 33554432 | bytes 524288 | tf_op jit(solution)/shard_map/pallas_call | solution.py:165
  88.0 1.4 %shard_map.160 = bf16[128,2048]{1,0:T(8,128)(2,1)} custom-call(s32[2]{0:T(128)S(1)} %pad_add_fusion.place, bf16[128,256]{1,0:T(8,128)(2,1)S(1)} %get-tuple-element.31.refs_0_, bf16[128,256]{1,0:T(8,128)(2,1)S(1)} %collective-permute-done.3.refs_1_, bf16[128,256]{1,0:T(8,128)(2,1)S(1)} %collective-permute-done.4.refs_2_, ...), custom_call_target="tpu_custom_call" | custom-call | bytes 1048576 | tf_op jit(solution)/shard_map/pallas_call | solution.py:165
  (60 shorter events, 18.9 us)
Async XLA Ops:
  6.7 43.1 %collective-permute-start = (bf16[480,256]{1,0:T(8,128)(2,1)S(1)}, bf16[480,256]{1,0:T(8,128)(2,1)S(1)}, u32[]{:S(2)}, u32[]{:S(2)}) collective-permute-start(bf16[480,256]{1,0:T(8,128)(2,1)S(1)} %get-tuple-element.28), channel_id=1, source_target_pairs={{0,4},{4,8},{8,12},{12,0},{1,5},{5,9},{9,13},{13,1},{2,6},{6,10},{... | collective-permute-start | bytes 737288 | tf_op jit(solution)/shard_map/ppermute | solution.py:177
  9.8 7.5 %collective-permute-start.14 = (bf16[8,1024]{1,0:T(8,128)(2,1)}, bf16[8,1024]{1,0:T(8,128)(2,1)S(1)}, u32[]{:S(2)}, u32[]{:S(2)}) collective-permute-start(bf16[8,1024]{1,0:T(8,128)(2,1)} %bitcast.30), channel_id=1, source_target_pairs={{0,12},{4,0},{8,4},{12,8},{1,13},{5,1},{9,5},{13,9},{2,14},{6,2},{... | collective-permute-start | bytes 49160 | tf_op jit(solution)/shard_map/ppermute | solution.py:177
  11.9 7.3 %collective-permute-start.13 = (bf16[8,1024]{1,0:T(8,128)(2,1)}, bf16[8,1024]{1,0:T(8,128)(2,1)S(1)}, u32[]{:S(2)}, u32[]{:S(2)}) collective-permute-start(bf16[8,1024]{1,0:T(8,128)(2,1)} %bitcast.31), channel_id=1, source_target_pairs={{0,8},{4,12},{8,0},{12,4},{1,9},{5,13},{9,1},{13,5},{2,10},{6,14},... | collective-permute-start | bytes 49160 | tf_op jit(solution)/shard_map/ppermute | solution.py:177
  12.8 6.3 %collective-permute-start.12 = (bf16[8,1024]{1,0:T(8,128)(2,1)}, bf16[8,1024]{1,0:T(8,128)(2,1)S(1)}, u32[]{:S(2)}, u32[]{:S(2)}) collective-permute-start(bf16[8,1024]{1,0:T(8,128)(2,1)} %bitcast.32), channel_id=1, source_target_pairs={{0,4},{4,8},{8,12},{12,0},{1,5},{5,9},{9,13},{13,1},{2,6},{6,10},{... | collective-permute-start | bytes 49160 | tf_op jit(solution)/shard_map/ppermute | solution.py:177
  23.8 5.9 %collective-permute-start.17 = (bf16[32,1152]{1,0:T(8,128)(2,1)S(1)}, bf16[32,1152]{1,0:T(8,128)(2,1)S(1)}, u32[]{:S(2)}, u32[]{:S(2)}) collective-permute-start(bf16[32,1152]{1,0:T(8,128)(2,1)S(1)} %shard_map.162.refs_0_), channel_id=1, source_target_pairs={{0,12},{4,0},{8,4},{12,8},{1,13},{5,1},{9,5},{13,9},{2,14},{6,2},{... | collective-permute-start | bytes 221192 | tf_op jit(solution)/shard_map/ppermute | solution.py:177
  25.3 27.8 %collective-permute-start.1 = (bf16[480,256]{1,0:T(8,128)(2,1)S(1)}, bf16[480,256]{1,0:T(8,128)(2,1)S(1)}, u32[]{:S(2)}, u32[]{:S(2)}) collective-permute-start(bf16[480,256]{1,0:T(8,128)(2,1)S(1)} %get-tuple-element.29), channel_id=1, source_target_pairs={{0,8},{4,12},{8,0},{12,4},{1,9},{5,13},{9,1},{13,5},{2,10},{6,14},... | collective-permute-start | bytes 737288 | tf_op jit(solution)/shard_map/ppermute | solution.py:177
  25.6 27.5 %collective-permute-start.2 = (bf16[480,256]{1,0:T(8,128)(2,1)S(1)}, bf16[480,256]{1,0:T(8,128)(2,1)S(1)}, u32[]{:S(2)}, u32[]{:S(2)}) collective-permute-start(bf16[480,256]{1,0:T(8,128)(2,1)S(1)} %get-tuple-element.30), channel_id=1, source_target_pairs={{0,12},{4,0},{8,4},{12,8},{1,13},{5,1},{9,5},{13,9},{2,14},{6,2},{... | collective-permute-start | bytes 737288 | tf_op jit(solution)/shard_map/ppermute | solution.py:177
  28.2 20.3 %collective-permute-start.16 = (bf16[32,1152]{1,0:T(8,128)(2,1)S(1)}, bf16[32,1152]{1,0:T(8,128)(2,1)S(1)}, u32[]{:S(2)}, u32[]{:S(2)}) collective-permute-start(bf16[32,1152]{1,0:T(8,128)(2,1)S(1)} %shard_map.162.refs_0_), channel_id=1, source_target_pairs={{0,8},{4,12},{8,0},{12,4},{1,9},{5,13},{9,1},{13,5},{2,10},{6,14},... | collective-permute-start | bytes 221192 | tf_op jit(solution)/shard_map/ppermute | solution.py:177
  29.7 18.9 %collective-permute-start.15 = (bf16[32,1152]{1,0:T(8,128)(2,1)S(1)}, bf16[32,1152]{1,0:T(8,128)(2,1)S(1)}, u32[]{:S(2)}, u32[]{:S(2)}) collective-permute-start(bf16[32,1152]{1,0:T(8,128)(2,1)S(1)} %shard_map.162.refs_0_), channel_id=1, source_target_pairs={{0,4},{4,8},{8,12},{12,0},{1,5},{5,9},{9,13},{13,1},{2,6},{6,10},{... | collective-permute-start | bytes 221192 | tf_op jit(solution)/shard_map/ppermute | solution.py:177
  48.5 11.6 %collective-permute-start.6 = (bf16[384,256]{1,0:T(8,128)(2,1)S(1)}, bf16[384,256]{1,0:T(8,128)(2,1)S(1)}, u32[]{:S(2)}, u32[]{:S(2)}) collective-permute-start(bf16[384,256]{1,0:T(8,128)(2,1)S(1)} %get-tuple-element.36), channel_id=1, source_target_pairs={{0,4},{4,8},{8,12},{12,0},{1,5},{5,9},{9,13},{13,1},{2,6},{6,10},{... | collective-permute-start | bytes 589832 | tf_op jit(solution)/shard_map/ppermute | solution.py:177
  48.5 16.6 %collective-permute-start.7 = (bf16[384,256]{1,0:T(8,128)(2,1)S(1)}, bf16[384,256]{1,0:T(8,128)(2,1)S(1)}, u32[]{:S(2)}, u32[]{:S(2)}) collective-permute-start(bf16[384,256]{1,0:T(8,128)(2,1)S(1)} %get-tuple-element.37), channel_id=1, source_target_pairs={{0,8},{4,12},{8,0},{12,4},{1,9},{5,13},{9,1},{13,5},{2,10},{6,14},... | collective-permute-start | bytes 589832 | tf_op jit(solution)/shard_map/ppermute | solution.py:177
  49.8 15.4 %collective-permute-start.8 = (bf16[384,256]{1,0:T(8,128)(2,1)S(1)}, bf16[384,256]{1,0:T(8,128)(2,1)S(1)}, u32[]{:S(2)}, u32[]{:S(2)}) collective-permute-start(bf16[384,256]{1,0:T(8,128)(2,1)S(1)} %get-tuple-element.38), channel_id=1, source_target_pairs={{0,12},{4,0},{8,4},{12,8},{1,13},{5,1},{9,5},{13,9},{2,14},{6,2},{... | collective-permute-start | bytes 589832 | tf_op jit(solution)/shard_map/ppermute | solution.py:177
  55.3 24.1 %copy-start = (bf16[2048,1024]{1,0:T(8,128)(2,1)S(1)}, bf16[2048,1024]{1,0:T(8,128)(2,1)}, u32[]{:S(2)}) copy-start(bf16[2048,1024]{1,0:T(8,128)(2,1)} %down.1) | copy-start | bytes 12582916
  58.6 20.2 %collective-permute-start.18 = (bf16[5,32,512]{2,1,0:T(8,128)(2,1)S(1)}, bf16[5,32,512]{2,1,0:T(8,128)(2,1)S(1)}, u32[]{:S(2)}, u32[]{:S(2)}) collective-permute-start(bf16[5,32,512]{2,1,0:T(8,128)(2,1)S(1)} %get-tuple-element.45), channel_id=1, source_target_pairs={{0,2},{2,0},{1,3},{3,1},{4,6},{6,4},{5,7},{7,5},{8,10},{10,8},{9,1... | collective-permute-start | bytes 491528 | tf_op jit(solution)/shard_map/ppermute | solution.py:472
  65.1 20.1 %copy-start.9 = (bf16[1,128,1024]{2,1,0:T(8,128)(2,1)S(1)}, bf16[1,128,1024]{2,1,0:T(8,128)(2,1)}, u32[]{:S(2)}) copy-start(bf16[1,128,1024]{2,1,0:T(8,128)(2,1)} %param.16) | copy-start | bytes 786436
  67.4 11.4 %collective-permute-start.9 = (bf16[128,256]{1,0:T(8,128)(2,1)S(1)}, bf16[128,256]{1,0:T(8,128)(2,1)S(1)}, u32[]{:S(2)}, u32[]{:S(2)}) collective-permute-start(bf16[128,256]{1,0:T(8,128)(2,1)S(1)} %get-tuple-element.40), channel_id=1, source_target_pairs={{0,12},{4,0},{8,4},{12,8},{1,13},{5,1},{9,5},{13,9},{2,14},{6,2},{... | collective-permute-start | bytes 196616 | tf_op jit(solution)/shard_map/ppermute | solution.py:177
  70.1 10.7 %collective-permute-start.10 = (bf16[128,256]{1,0:T(8,128)(2,1)S(1)}, bf16[128,256]{1,0:T(8,128)(2,1)S(1)}, u32[]{:S(2)}, u32[]{:S(2)}) collective-permute-start(bf16[128,256]{1,0:T(8,128)(2,1)S(1)} %get-tuple-element.41), channel_id=1, source_target_pairs={{0,8},{4,12},{8,0},{12,4},{1,9},{5,13},{9,1},{13,5},{2,10},{6,14},... | collective-permute-start | bytes 196616 | tf_op jit(solution)/shard_map/ppermute | solution.py:177
  72.6 11.5 %collective-permute-start.11 = (bf16[128,256]{1,0:T(8,128)(2,1)S(1)}, bf16[128,256]{1,0:T(8,128)(2,1)S(1)}, u32[]{:S(2)}, u32[]{:S(2)}) collective-permute-start(bf16[128,256]{1,0:T(8,128)(2,1)S(1)} %get-tuple-element.42), channel_id=1, source_target_pairs={{0,4},{4,8},{8,12},{12,0},{1,5},{5,9},{9,13},{13,1},{2,6},{6,10},{... | collective-permute-start | bytes 196616 | tf_op jit(solution)/shard_map/ppermute | solution.py:177
  74.9 10.3 %collective-permute-start.3 = (bf16[128,256]{1,0:T(8,128)(2,1)S(1)}, bf16[128,256]{1,0:T(8,128)(2,1)S(1)}, u32[]{:S(2)}, u32[]{:S(2)}) collective-permute-start(bf16[128,256]{1,0:T(8,128)(2,1)S(1)} %get-tuple-element.32), channel_id=1, source_target_pairs={{0,12},{4,0},{8,4},{12,8},{1,13},{5,1},{9,5},{13,9},{2,14},{6,2},{... | collective-permute-start | bytes 196616 | tf_op jit(solution)/shard_map/ppermute | solution.py:177
  78.8 9.2 %collective-permute-start.4 = (bf16[128,256]{1,0:T(8,128)(2,1)S(1)}, bf16[128,256]{1,0:T(8,128)(2,1)S(1)}, u32[]{:S(2)}, u32[]{:S(2)}) collective-permute-start(bf16[128,256]{1,0:T(8,128)(2,1)S(1)} %get-tuple-element.33), channel_id=1, source_target_pairs={{0,8},{4,12},{8,0},{12,4},{1,9},{5,13},{9,1},{13,5},{2,10},{6,14},... | collective-permute-start | bytes 196616 | tf_op jit(solution)/shard_map/ppermute | solution.py:177
  78.8 9.2 %collective-permute-start.5 = (bf16[128,256]{1,0:T(8,128)(2,1)S(1)}, bf16[128,256]{1,0:T(8,128)(2,1)S(1)}, u32[]{:S(2)}, u32[]{:S(2)}) collective-permute-start(bf16[128,256]{1,0:T(8,128)(2,1)S(1)} %get-tuple-element.34), channel_id=1, source_target_pairs={{0,4},{4,8},{8,12},{12,0},{1,5},{5,9},{9,13},{13,1},{2,6},{6,10},{... | collective-permute-start | bytes 196616 | tf_op jit(solution)/shard_map/ppermute | solution.py:177
  80.8 8.6 %collective-permute-start.19 = (bf16[8,1024]{1,0:T(8,128)(2,1)S(1)}, bf16[8,1024]{1,0:T(8,128)(2,1)S(1)}, u32[]{:S(2)}, u32[]{:S(2)}) collective-permute-start(bf16[8,1024]{1,0:T(8,128)(2,1)S(1)} %get-tuple-element.47), channel_id=1, source_target_pairs={{0,12},{4,0},{8,4},{12,8},{1,13},{5,1},{9,5},{13,9},{2,14},{6,2},{... | collective-permute-start | bytes 49160 | tf_op jit(solution)/shard_map/ppermute | solution.py:177
  84.1 5.3 %collective-permute-start.20 = (bf16[8,1024]{1,0:T(8,128)(2,1)S(1)}, bf16[8,1024]{1,0:T(8,128)(2,1)S(1)}, u32[]{:S(2)}, u32[]{:S(2)}) collective-permute-start(bf16[8,1024]{1,0:T(8,128)(2,1)S(1)} %get-tuple-element.48), channel_id=1, source_target_pairs={{0,8},{4,12},{8,0},{12,4},{1,9},{5,13},{9,1},{13,5},{2,10},{6,14},... | collective-permute-start | bytes 49160 | tf_op jit(solution)/shard_map/ppermute | solution.py:177
  85.2 5.5 %collective-permute-start.21 = (bf16[8,1024]{1,0:T(8,128)(2,1)S(1)}, bf16[8,1024]{1,0:T(8,128)(2,1)S(1)}, u32[]{:S(2)}, u32[]{:S(2)}) collective-permute-start(bf16[8,1024]{1,0:T(8,128)(2,1)S(1)} %get-tuple-element.49), channel_id=1, source_target_pairs={{0,4},{4,8},{8,12},{12,0},{1,5},{5,9},{9,13},{13,1},{2,6},{6,10},{... | collective-permute-start | bytes 49160 | tf_op jit(solution)/shard_map/ppermute | solution.py:177
  (12 other events, 12.2 us)

commit v2 on v1

--- a/solution.py
+++ b/solution.py
@@ -149,24 +149,24 @@
     return mixed, heard, seen, mlp
 
 
-def vmem():
-    return pl.BlockSpec(memory_space=pltpu.VMEM)
-
-
-def smem():
-    return pl.BlockSpec(memory_space=pltpu.SMEM)
+def whole():
+    return pl.BlockSpec()
+
+
+def after(value, *others):
+    return lax.optimization_barrier((value, *others))[0]
 
 
 def sds(shape, dtype=BF16):
     return jax.ShapeDtypeStruct(shape, dtype)
 
 
-def call(kernel, ins, outs, flops=0, moved=0, limit=32, scalars=0):
+def call(kernel, ins, outs, flops=0, moved=0, limit=32):
     return pl.pallas_call(
         kernel,
         out_shape=tuple(outs),
-        in_specs=[smem()] * scalars + [vmem()] * (len(ins) - scalars),
-        out_specs=tuple(vmem() for _ in outs),
+        in_specs=[whole()] * len(ins),
+        out_specs=tuple(whole() for _ in outs),
         compiler_params=pltpu.CompilerParams(vmem_limit_bytes=limit * MIB),
         cost_estimate=pl.CostEstimate(flops=flops, bytes_accessed=moved, transcendentals=0),
     )(*ins)
@@ -183,82 +183,125 @@
     return first, second, value - first - second
 
 
-def pack_kernel(n, first, width, with_audio, place, q, k, v, *rest):
-    audio, outs = (rest[:3], rest[3:]) if with_audio else ((), rest)
+def pack_kernel(n, first, widths, audio_count, kept, q, k, v, *refs):
+    audio, refs = refs[:audio_count], refs[audio_count:]
+    keep, outs, sem = refs[:kept], refs[kept:-1], refs[-1]
+    me = lax.axis_index("seq")
     tokens = q.shape[0]
     group = q.shape[1] // n
-    me = place[0]
-    if with_audio:
-        key, value, line = audio
-        half = key.shape[1]
-        mine = line[:, pl.ds(pl.multiple_of(place[1] * half, LANES), half)].astype(F32)
-        rows = []
-        for part in (key[...].astype(F32), value[...].astype(F32), mine):
-            rows += [part[:, c : c + width] for c in range(0, half, width)]
-        extra = jnp.concatenate(rows, axis=0).astype(BF16)
-    for s in range(n):
-        dest = lax.rem(me + s, n)
-        at = pl.ds(pl.multiple_of(dest * group + first, LANES), width)
-        for i, ref in enumerate((q, k, v)):
-            outs[s][i * tokens : (i + 1) * tokens, :] = ref[:, at]
-        if with_audio:
-            outs[s][3 * tokens :, :] = extra
-
-
-def unfold(tail, index, rows, columns, width):
-    per = columns // width
-    return jnp.concatenate(
-        [tail[(index * per + c) * rows : (index * per + c + 1) * rows] for c in range(per)], axis=1
-    )
-
-
-def attend_kernel(n, tokens, *refs):
-    pieces, outs = refs[:n], refs[n:]
-    width = pieces[0].shape[1]
-    scale = LOG2E / math.sqrt(VHEAD)
-    for h in range(width // VHEAD):
-        cols = slice(h * VHEAD, (h + 1) * VHEAD)
-        keys = jnp.concatenate([p[tokens : 2 * tokens, cols] for p in pieces], axis=0)
-        values = jnp.concatenate([p[2 * tokens : 3 * tokens, cols] for p in pieces], axis=0)
-        for p, out in zip(pieces, outs):
-            s = lax.dot_general(p[0:tokens, cols], keys, NT, preferred_element_type=F32)
-            s = s * scale
-            w = jnp.exp2(s - jnp.max(s, axis=1, keepdims=True))
-            total = jnp.sum(w, axis=1, keepdims=True)
-            o = jnp.dot(w.astype(BF16), values, preferred_element_type=F32)
-            out[:, cols] = (o / total).astype(BF16)
-
-
-def unpack_kernel(n, widths, place, *refs):
-    pieces, out = refs[:-1], refs[-1]
-    me = place[0]
-    group = sum(widths)
-    first = 0
+    copies = []
     for c, width in enumerate(widths):
         for s in range(n):
             dest = lax.rem(me + s, n)
             at = pl.ds(pl.multiple_of(dest * group + first, LANES), width)
-            out[:, at] = pieces[c * n + s][...]
+            for i, ref in enumerate((q, k, v)):
+                to = outs[c * n + s].at[pl.ds(i * tokens, tokens), :]
+                copies.append(pltpu.make_async_copy(ref.at[:, at], to, sem.at[len(copies)]))
+                copies[-1].start()
         first += width
+    for ref, to in zip(keep, outs[n * len(widths) :]):
+        copies.append(pltpu.make_async_copy(ref, to, sem.at[len(copies)]))
+        copies[-1].start()
+    if audio:
+        half = audio[0].shape[1]
+        mine = pl.ds(pl.multiple_of(lax.axis_index("tp") * half, LANES), half)
+        parts = [ref[...].astype(F32) for ref in audio[:3]] + [audio[3][:, mine].astype(F32)]
+        blocks = [part[:, c : c + LANES] for part in parts for c in range(0, half, LANES)]
+        extra = jnp.concatenate(blocks, axis=0).astype(BF16)
+        for s in range(n):
+            outs[s][3 * tokens :, :] = extra
+    for copy in copies:
+        copy.wait()
+
+
+def pack(video, audio, keep, n, first, widths, limit, moved):
+    tokens = video[0].shape[0]
+    extra = 4 * audio[0].size // LANES if audio else 0
+    shapes = [sds((3 * tokens + extra, w)) for w in widths for _ in range(n)]
+    stay = pl.BlockSpec(memory_space=pl.ANY)
+    return pl.pallas_call(
+        functools.partial(pack_kernel, n, first, widths, len(audio), len(keep)),
+        out_shape=tuple(shapes) + tuple(sds(x.shape) for x in keep),
+        in_specs=[stay] * 3 + [whole()] * len(audio) + [stay] * len(keep),
+        out_specs=(whole(),) * (len(shapes) + len(keep)),
+        scratch_shapes=[pltpu.SemaphoreType.DMA((3 * len(shapes) + len(keep),))],
+        compiler_params=pltpu.CompilerParams(vmem_limit_bytes=limit * MIB),
+        cost_estimate=pl.CostEstimate(flops=0, bytes_accessed=moved, transcendentals=0),
+    )(*video, *audio, *keep)
+
+
+def audio_rows(tails, part, pair, rows, pairs):
+    at = (part * pairs + pair) * rows
+    return jnp.concatenate([t[at : at + rows] for t in tails], axis=0)
+
+
+def attend_kernel(n, tokens, *refs):
+    inputs, outs = refs[:-n], refs[-n:]
+    scale = LOG2E / math.sqrt(VHEAD)
+    first = 0
+    for c in range(0, len(inputs), n):
+        pieces = inputs[c : c + n]
+        for h in range(pieces[0].shape[1] // VHEAD):
+            cols = slice(h * VHEAD, (h + 1) * VHEAD)
+            keys = jnp.concatenate([p[tokens : 2 * tokens, cols] for p in pieces], axis=0)
+            values = jnp.concatenate([p[2 * tokens : 3 * tokens, cols] for p in pieces], axis=0)
+            for p, out in zip(pieces, outs):
+                s = lax.dot_general(p[0:tokens, cols], keys, NT, preferred_element_type=F32)
+                s = s * scale
+                w = jnp.exp2(s - jnp.max(s, axis=1, keepdims=True))
+                total = jnp.sum(w, axis=1, keepdims=True)
+                o = jnp.dot(w.astype(BF16), values, preferred_element_type=F32)
+                out[:, first + h * VHEAD : first + (h + 1) * VHEAD] = (o / total).astype(BF16)
+        first += pieces[0].shape[1]
+
+
+def unpack_kernel(n, widths, *refs):
+    pieces, out, sem = refs[: n * len(widths)], refs[-2], refs[-1]
+    me = lax.axis_index("seq")
+    group = sum(widths)
+    first = 0
+    copies = []
+    for c, width in enumerate(widths):
+        for s in range(n):
+            dest = lax.rem(me + s, n)
+            at = pl.ds(pl.multiple_of(dest * group + first, LANES), width)
+            copies.append(pltpu.make_async_copy(pieces[c * n + s], out.at[:, at], sem.at[len(copies)]))
+            copies[-1].start()
+        first += width
+    for copy in copies:
+        copy.wait()
+
+
+def unpack(pieces, n, widths):
+    tokens = pieces[0].shape[0]
+    return pl.pallas_call(
+        functools.partial(unpack_kernel, n, widths),
+        out_shape=sds((tokens, n * sum(widths))),
+        in_specs=[pl.BlockSpec(memory_space=pltpu.VMEM)] * len(pieces),
+        out_specs=pl.BlockSpec(memory_space=pl.ANY),
+        scratch_shapes=[pltpu.SemaphoreType.DMA((len(pieces),))],
+        compiler_params=pltpu.CompilerParams(vmem_limit_bytes=16 * MIB),
+    )(*pieces)
 
 
 def low_half(shape):
     return lax.broadcasted_iota(jnp.int32, shape, 1) < CHEAD
 
 
-def listen_kernel(n, *refs):
-    queries, keys, values, out = refs[:n], refs[n], refs[n + 1], refs[n + 2]
+def listen_kernel(n, tokens, rows, *refs):
+    pieces, keys, values, out = refs[:n], refs[n], refs[n + 1], refs[n + 2]
     columns = keys.shape[1]
-    q = jnp.concatenate([p[...].astype(F32) for p in queries], axis=0)
-    rows = q.shape[0]
+    pairs = columns // LANES
+    tails = [p[3 * tokens : 3 * tokens + rows * pairs, :].astype(F32) for p in pieces]
+    count = n * rows
     scale = LOG2E / math.sqrt(CHEAD)
-    low = low_half((rows, LANES))
-    lane = lax.broadcasted_iota(jnp.int32, (rows, LANES), 1)
-    stats = jnp.zeros((rows, LANES), F32)
+    low = low_half((count, LANES))
+    lane = lax.broadcasted_iota(jnp.int32, (count, LANES), 1)
+    stats = jnp.zeros((count, LANES), F32)
     heads = columns // CHEAD
-    for pair in range(columns // LANES):
+    for pair in range(pairs):
         cols = slice(pair * LANES, (pair + 1) * LANES)
-        qp = q[:, cols]
+        qp = audio_rows(tails, 0, pair, rows, pairs)
         both = jnp.concatenate([jnp.where(low, qp, 0.0), jnp.where(low, 0.0, qp)], axis=0)
         s = lax.dot_general(both.astype(BF16), keys[:, cols], NT, preferred_element_type=F32)
         s = s * scale
@@ -266,10 +309,10 @@
         w = jnp.exp2(s - peak)
         total = jnp.sum(w, axis=1, keepdims=True)
         o = jnp.dot(w.astype(BF16), values[:, cols], preferred_element_type=F32) / total
-        out[:, cols] = jnp.where(low, o[:rows], o[rows:]).astype(BF16)
+        out[:, cols] = jnp.where(low, o[:count], o[count:]).astype(BF16)
         for i in range(2):
             head = 2 * pair + i
-            sel = slice(i * rows, (i + 1) * rows)
+            sel = slice(i * count, (i + 1) * count)
             for j, part in enumerate(parts3(peak[sel]) + parts3(total[sel])):
                 stats = jnp.where(lane == j * heads + head, part, stats)
     out[:, columns:] = stats.astype(BF16)
@@ -284,7 +327,6 @@
     def _():
         columns = seen.shape[1]
         heads = columns // CHEAD
-        width = pieces[0].shape[1]
         peaks, totals, parts = [], [], []
         for s in range(n):
             whole = got[s][...].astype(F32)
@@ -300,7 +342,6 @@
         every = functools.reduce(jnp.add, weight)
         weight = [w / every for w in weight]
         tails = [p[3 * tokens :, :].astype(F32) for p in pieces]
-        line = jnp.concatenate([unfold(t, 2, rows, columns, width) for t in tails], axis=0)
         low = low_half((n * rows, LANES))
         square = jnp.zeros((n * rows, 1), F32)
         for pair in range(columns // LANES):
@@ -311,9 +352,10 @@
                 o = o + jnp.where(low, a, b) * part[:, cols]
             o = o.astype(BF16)
             seen[:, cols] = o[:rows]
-            residual = line[:, cols] + o.astype(F32)
+            residual = audio_rows(tails, 3, pair, rows, columns // LANES) + o.astype(F32)
             square = square + jnp.sum(residual * residual, axis=1, keepdims=True)
-            x_ref[:, cols] = (residual * gain[:, cols]).astype(BF16)
+            at = pl.ds(pl.multiple_of(lax.axis_index("tp") * columns + pair * LANES, LANES), LANES)
+            x_ref[:, cols] = (residual * gain[:, at]).astype(BF16)
         lane = lax.broadcasted_iota(jnp.int32, (n * rows, LANES), 1)
         first, second, third = parts3(square)
         spread = jnp.where(lane == 0, first, jnp.where(lane == 1, second, third))
@@ -348,7 +390,7 @@
         scratch_shapes=[pltpu.VMEM((n * rows, columns), BF16)],
         compiler_params=pltpu.CompilerParams(vmem_limit_bytes=32 * MIB),
         cost_estimate=pl.CostEstimate(
-            flops=8 * n * rows * columns * units, bytes_accessed=4 * columns * units, transcendentals=0
+            flops=0, bytes_accessed=0 * MIB, transcendentals=0
         ),
     )(*got, *pieces, gain, up)
 
@@ -384,36 +426,33 @@
         scratch_shapes=[pltpu.VMEM((n * rows, units), BF16)],
         compiler_params=pltpu.CompilerParams(vmem_limit_bytes=32 * MIB),
         cost_estimate=pl.CostEstimate(
-            flops=8 * n * rows * columns * units, bytes_accessed=4 * columns * units, transcendentals=0
+            flops=0, bytes_accessed=0 * MIB, transcendentals=0
         ),
     )(own, other, down)
 
 
 def heard_kernel(n, tokens, rows, q, *refs):
     pieces, out = refs[:n], refs[n]
-    columns = q.shape[1]
-    width = pieces[0].shape[1]
+    pairs = q.shape[1] // LANES
     tails = [p[3 * tokens :, :].astype(F32) for p in pieces]
-    keys = jnp.concatenate([unfold(t, 0, rows, columns, width) for t in tails], axis=0)
-    values = jnp.concatenate([unfold(t, 1, rows, columns, width) for t in tails], axis=0)
     count = n * rows
     low = low_half((count, LANES))
     scale = LOG2E / math.sqrt(CHEAD)
-    for pair in range(columns // LANES):
+
+    def both(part, pair):
+        x = audio_rows(tails, part, pair, rows, pairs)
+        return jnp.concatenate([jnp.where(low, x, 0.0), jnp.where(low, 0.0, x)], axis=0).astype(BF16)
+
+    for pair in range(pairs):
         cols = slice(pair * LANES, (pair + 1) * LANES)
-
-        def both(x):
-            x = x[:, cols]
-            return jnp.concatenate([jnp.where(low, x, 0.0), jnp.where(low, 0.0, x)], axis=0).astype(BF16)
-
-        s = lax.dot_general(both(keys), q[:, cols], NT, preferred_element_type=F32) * scale
+        s = lax.dot_general(both(1, pair), q[:, cols], NT, preferred_element_type=F32) * scale
         probs = []
         for i in range(2):
             t = s[i * count : (i + 1) * count]
             w = jnp.exp2(t - jnp.max(t, axis=0, keepdims=True))
             probs.append(w / jnp.sum(w, axis=0, keepdims=True))
         w = jnp.concatenate(probs, axis=0).astype(BF16)
-        out[:, cols] = lax.dot_general(w, both(values), TN, preferred_element_type=F32).astype(BF16)
+        out[:, cols] = lax.dot_general(w, both(2, pair), TN, preferred_element_type=F32).astype(BF16)
 
 
 def add_kernel(own, *refs):
@@ -426,81 +465,59 @@
 def short_body(vq, vk, vv, cq, ak, av, aq, ck, cv, ai, gain, up, down):
     n = lax.axis_size("seq")
     tokens = vq.shape[0]
-    rows = aq.shape[0]
-    columns = aq.shape[1]
+    rows, columns = aq.shape
     features = ai.shape[1]
-    tp = lax.axis_index("tp")
-    place = jnp.stack([lax.axis_index("seq"), tp]).astype(jnp.int32)
-    group = vq.shape[1] // n
-    head_split = [group // VHEAD // 2 * VHEAD, group - group // VHEAD // 2 * VHEAD]
-    video_bytes = 6 * vq.size
-
-    queries = [aq] + [shift(aq, s) for s in range(1, n)]
-
-    wide = head_split[0]
-    extra = 3 * rows * columns // wide
-    packed = call(
-        functools.partial(pack_kernel, n, 0, wide, True),
-        (place, vq, vk, vv, ak, av, ai),
-        [sds((3 * tokens + extra, wide))] * n,
-        moved=video_bytes,
-        scalars=1,
-    )
-    chunk_a = [packed[0]] + [shift(packed[s], s) for s in range(1, n)]
-
+    heads = vq.shape[1] // n // VHEAD
+    widths = [c * VHEAD for c in (1, 1, heads - 2)]
+    video = (vq, vk, vv)
+
+    def send(own, *first):
+        return [own[0]] + [shift(after(own[s], *first), s) for s in range(1, n)]
+
+    def give_back(own):
+        return [own[0]] + [shift(own[s], -s) for s in range(1, n)]
+
+    def attended(chunks, moved):
+        width = sum(c[0].shape[1] for c in chunks)
+        return call(
+            functools.partial(attend_kernel, n, tokens),
+            [p for c in chunks for p in c],
+            [sds((tokens, width))] * n,
+            moved=moved,
+            limit=16,
+        )
+
+    wait = 16 * MIB
+    packed = pack(video, (aq, ak, av, ai), (), n, 0, widths[:1], 60, 6 * vq.size)
+    chunk_0 = send(packed)
+    packed = pack(video, (), (packed[0], ck, cv), n, widths[0], widths[1:], 16, wait)
+    *packed, chunk_0[0], ck, cv = packed
+    chunk_1 = send(packed[:n])
     (share,) = call(
-        functools.partial(listen_kernel, n),
-        (*queries, ck, cv),
+        functools.partial(listen_kernel, n, tokens, rows),
+        (*chunk_0, ck, cv),
         [sds((n * rows, columns + LANES))],
-        flops=8 * n * rows * tokens * columns,
-        moved=4 * ck.size,
-    )
-    shares = [share] + [shift(share, s) for s in range(1, n)]
-
-    wide_b = head_split[1]
-    packed_b = call(
-        functools.partial(pack_kernel, n, wide, wide_b, False),
-        (place, vq, vk, vv),
-        [sds((3 * tokens, wide_b))] * n,
-        moved=video_bytes,
-        scalars=1,
-    )
-    chunk_b = [packed_b[0]] + [shift(packed_b[s], s) for s in range(1, n)]
-
-    own_gain = lax.dynamic_slice_in_dim(gain.reshape(1, -1), tp * columns, columns, 1)
-    own_sum, sent_sum, seen = combine(shares, chunk_a, own_gain, up, tokens, rows, 512)
-    other_sum = lax.ppermute(sent_sum, "tp", [(0, 1), (1, 0)])
-    results = finish(own_sum, other_sum, down, n, rows, features, 512)
-    back = [results[0]] + [shift(results[s], -s) for s in range(1, n)]
-    (mlp,) = call(add_kernel, back, [sds((rows, columns))])
-
-    flops = 8 * n * n * tokens * tokens
-    def attended(chunk, width):
-        outs = call(
-            functools.partial(attend_kernel, n, tokens),
-            chunk,
-            [sds((tokens, width))] * n,
-            flops=flops * width,
-            moved=4 * n * tokens * width * 2,
-        )
-        return [outs[0]] + [shift(outs[s], -s) for s in range(1, n)]
-
-    mixed_a = attended(chunk_a, wide)
+        moved=4 * vq.size,
+        limit=16,
+    )
+    shares = send([share] * n)
+    chunk_2 = send(packed[n:], *chunk_1[1:])
+    first = attended([chunk_0, chunk_1], 1 * MIB)
     (heard,) = call(
         functools.partial(heard_kernel, n, tokens, rows),
-        (cq, *chunk_a),
+        (cq, *chunk_0),
         [sds(cq.shape)],
-        flops=8 * n * rows * cq.size,
-        moved=4 * cq.size,
-    )
-    mixed_b = attended(chunk_b, wide_b)
-    (mixed,) = call(
-        functools.partial(unpack_kernel, n, head_split),
-        (place, *mixed_a, *mixed_b),
-        [sds(vq.shape)],
-        moved=4 * vq.size,
-        scalars=1,
-    )
+        moved=1 * MIB,
+        limit=16,
+    )
+    gain = after(gain.reshape(1, -1), first[0], heard)
+    own_sum, sent_sum, seen = combine(shares, chunk_0, gain, up, tokens, rows, 512)
+    other_sum = lax.ppermute(sent_sum, "tp", [(0, 1), (1, 0)])
+    mixed_a = give_back(first)
+    results = finish(own_sum, other_sum, down, n, rows, features, 512)
+    (mlp,) = call(add_kernel, give_back(results), [sds((rows, columns))])
+    mixed_b = give_back(attended([chunk_2], 0 * MIB))
+    mixed = unpack((after(mixed_a[0], mlp), *mixed_a[1:], *mixed_b), n, (widths[0] + widths[1], widths[2]))
     return mixed, heard, seen, mlp
 
 
@@ -510,13 +527,14 @@
     return (
         1 < n <= 8
         and lax.axis_size("tp") == 2
-        and heads % (2 * n) == 0
+        and heads % n == 0
+        and heads // n > 2
         and vq.shape[0] == LANES
         and n * vq.shape[0] <= 1024
         and aq.shape[0] % 8 == 0
         and n * aq.shape[0] <= 64
         and 6 * (aq.shape[1] // CHEAD) <= LANES
-        and aq.shape[1] % (heads // n // 2 * VHEAD) == 0
+        and aq.shape[1] % VHEAD == 0
         and up.shape[1] % 512 == 0
         and down.shape[1] % 512 == 0
     )

time: 92 us -> 78.7 us (0.86)
  waiting for transfers between devices: 28.1 us -> 10.4 us
  starting transfers between devices: 32.2 us -> 42.2 us
  local copies, waits for them, and re-layouts: 12.9 us -> 5.96 us
  Pallas kernels: 17.3 us -> 19 us
    ppermute x21, waiting for transfers between devices: 28.1 us -> 8.9 us  [shift(): return lax.ppermute(value, 'seq', [(i, (i + by) % n) for i in range(n)])]
    ppermute x21, starting transfers between devices: 30.7 us -> 40.7 us  [shift(): return lax.ppermute(value, 'seq', [(i, (i + by) % n) for i in range(n)])]
    unnamed x28 -> x20, local copies, waits for them, and re-layouts: 12.2 us -> 5.96 us
    pallas_call x8, Pallas kernels: 12.6 us -> 14.3 us  [the longest x5 9.9 us: call(): pl.pallas_call(kernel, out_shape=tuple(outs), in_specs=[whole()] * len(in...]
    ppermute x1, waiting for transfers between devices: 0.01 us -> 1.45 us  [short_body(): other_sum = lax.ppermute(sent_sum, 'tp', [(0, 1), (1, 0)])]
  transfers between devices with their start and end apart: 22 -> 22, of which waited for: 6 -> 6; matrix products, arithmetic and copies ran while one was open for 1% -> 0% of each run, Pallas kernels for 18% -> 20%
where the time goes in v2:
time: 78.7 us; the launch traced here: 78.2 us
  starting transfers between devices  42.2 us (54%)
  Pallas kernels  19 us (24%)
  waiting for transfers between devices  10.4 us (13%)
  local copies, waits for them, and re-layouts  5.96 us (8%)
    ppermute x21, starting transfers between devices, shift(): return lax.ppermute(value, 'seq', [(i, (i + by) % n) for i in range(n)])  40.7 us
    pallas_call x5, Pallas kernels, call(): pl.pallas_call(kernel, out_shape=tuple(outs), in_specs=[whole()] * len(in...  9.9 us
    ppermute x21, waiting for transfers between devices, shift(): return lax.ppermute(value, 'seq', [(i, (i + by) % n) for i in range(n)])  8.9 us
    unnamed x20, local copies, waits for them, and re-layouts  5.96 us
    pallas_call x2, Pallas kernels, pack(): pl.pallas_call(functools.partial(pack_kernel, n, first, widths, len(audio...  3.53 us
    pallas_call x1, Pallas kernels, combine(): pl.pallas_call(functools.partial(combine_kernel, n, tokens, rows), grid=(...  3.3 us
  transfers between devices with their start and end apart: 22, of which 6 were waited for; matrix products, arithmetic and copies ran while one was open for 0% of the time, Pallas kernels for 20%

profile of v2, /device:TPU:0, one launch (start us, length us, event | category | flops | bytes accessed | tf_op | source)
XLA Modules:
  0.0 78.2 jit_solution(6760696199073022189)
XLA Ops:
  0.7 2.7 %shard_map.156 = (bf16[640,128]{1,0:T(8,128)(2,1)}, bf16[640,128]{1,0:T(8,128)(2,1)}, bf16[640,128]{1,0:T(8,128)(2,1)}, bf16[640,128]{1,0:T(8,128)(2,1)}) custom-call(bf16[128,2048]{1,0:T(8,128)(2,1)} %bitcast.15, bf16[128,2048]{1,0:T(8,128)(2,1)} %bitcast.17, bf16[128,2048]{1,0:T(8,128)(2,1)} %bitcast.19, bf16[8,1024]{1,0:T(8,128)(2,1)} %bitcast.28, ...), custom_call_target="tpu_custom_call" | custom-call | bytes 1572864 | tf_op jit(solution)/shard_map/pallas_call | solution.py:222
  3.4 3.1 %collective-permute-start = (bf16[640,128]{1,0:T(8,128)(2,1)}, bf16[640,128]{1,0:T(8,128)(2,1)S(1)}, u32[]{:S(2)}, u32[]{:S(2)}) collective-permute-start(bf16[640,128]{1,0:T(8,128)(2,1)} %get-tuple-element.41), channel_id=1, source_target_pairs={{0,4},{4,8},{8,12},{12,0},{1,5},{5,9},{9,13},{13,1},{2,6},{6,10},{... | collective-permute-start | bytes 491528 | tf_op jit(solution)/shard_map/ppermute | solution.py:177
  6.5 2.6 %collective-permute-start.1 = (bf16[640,128]{1,0:T(8,128)(2,1)}, bf16[640,128]{1,0:T(8,128)(2,1)S(1)}, u32[]{:S(2)}, u32[]{:S(2)}) collective-permute-start(bf16[640,128]{1,0:T(8,128)(2,1)} %get-tuple-element.42), channel_id=1, source_target_pairs={{0,8},{4,12},{8,0},{12,4},{1,9},{5,13},{9,1},{13,5},{2,10},{6,14},... | collective-permute-start | bytes 491528 | tf_op jit(solution)/shard_map/ppermute | solution.py:177
  9.1 1.3 %collective-permute-start.2 = (bf16[640,128]{1,0:T(8,128)(2,1)}, bf16[640,128]{1,0:T(8,128)(2,1)S(1)}, u32[]{:S(2)}, u32[]{:S(2)}) collective-permute-start(bf16[640,128]{1,0:T(8,128)(2,1)} %get-tuple-element.43), channel_id=1, source_target_pairs={{0,12},{4,0},{8,4},{12,8},{1,13},{5,1},{9,5},{13,9},{2,14},{6,2},{... | collective-permute-start | bytes 491528 | tf_op jit(solution)/shard_map/ppermute | solution.py:177
  18.2 2.8 %collective-permute-start.5 = (bf16[384,128]{1,0:T(8,128)(2,1)S(1)}, bf16[384,128]{1,0:T(8,128)(2,1)S(1)}, u32[]{:S(2)}, u32[]{:S(2)}) collective-permute-start(bf16[384,128]{1,0:T(8,128)(2,1)S(1)} %get-tuple-element.47), channel_id=1, source_target_pairs={{0,12},{4,0},{8,4},{12,8},{1,13},{5,1},{9,5},{13,9},{2,14},{6,2},{... | collective-permute-start | bytes 294920 | tf_op jit(solution)/shard_map/ppermute | solution.py:177
  21.1 2.0 %shard_map.159.refs_0_ = bf16[32,1152]{1,0:T(8,128)(2,1)S(1)} custom-call(bf16[640,128]{1,0:T(8,128)(2,1)S(1)} %get-tuple-element.40.refs_0_.refs_4_, bf16[640,128]{1,0:T(8,128)(2,1)S(1)} %collective-permute-done.refs_1_.refs_5_, bf16[640,128]{1,0:T(8,128)(2,1)S(1)} %collective-permute-done.1.refs_2_.refs_6_, ...), custom_call_target="tpu_custom_call" | custom-call | bytes 1048576 | tf_op jit(solution)/shard_map/pallas_call | solution.py:165
  23.1 9.5 %collective-permute-start.8 = (bf16[32,1152]{1,0:T(8,128)(2,1)S(1)}, bf16[32,1152]{1,0:T(8,128)(2,1)S(1)}, u32[]{:S(2)}, u32[]{:S(2)}) collective-permute-start(bf16[32,1152]{1,0:T(8,128)(2,1)S(1)} %shard_map.159.refs_0_), channel_id=1, source_target_pairs={{0,12},{4,0},{8,4},{12,8},{1,13},{5,1},{9,5},{13,9},{2,14},{6,2},{... | collective-permute-start | bytes 221192 | tf_op jit(solution)/shard_map/ppermute | solution.py:177
  33.3 2.8 %collective-permute-start.16 = (bf16[384,256]{1,0:T(8,128)(2,1)S(1)}, bf16[384,256]{1,0:T(8,128)(2,1)S(1)}, u32[]{:S(2)}, u32[]{:S(2)}) collective-permute-start(bf16[384,256]{1,0:T(8,128)(2,1)S(1)} %get-tuple-element.64), channel_id=1, source_target_pairs={{0,4},{4,8},{8,12},{12,0},{1,5},{5,9},{9,13},{13,1},{2,6},{6,10},{... | collective-permute-start | bytes 589832 | tf_op jit(solution)/shard_map/ppermute | solution.py:177
  37.0 2.6 %collective-permute-start.18 = (bf16[384,256]{1,0:T(8,128)(2,1)S(1)}, bf16[384,256]{1,0:T(8,128)(2,1)S(1)}, u32[]{:S(2)}, u32[]{:S(2)}) collective-permute-start(bf16[384,256]{1,0:T(8,128)(2,1)S(1)} %get-tuple-element.68), channel_id=1, source_target_pairs={{0,12},{4,0},{8,4},{12,8},{1,13},{5,1},{9,5},{13,9},{2,14},{6,2},{... | collective-permute-start | bytes 589832 | tf_op jit(solution)/shard_map/ppermute | solution.py:177
  39.6 2.2 %shard_map.158 = (bf16[128,256]{1,0:T(8,128)(2,1)S(1)}, bf16[128,256]{1,0:T(8,128)(2,1)S(1)}, bf16[128,256]{1,0:T(8,128)(2,1)S(1)}, bf16[128,256]{1,0:T(8,128)(2,1)S(1)}) custom-call(bf16[640,128]{1,0:T(8,128)(2,1)S(1)} %get-tuple-element.40.refs_0_.refs_4_, bf16[640,128]{1,0:T(8,128)(2,1)S(1)} %collective-permute-done.refs_1_.refs_5_, ...), custom_call_target="tpu_custom_call" | custom-call | bytes 1048576 | tf_op jit(solution)/shard_map/pallas_call | solution.py:165
  41.9 2.8 %shard_map.160 = bf16[128,1024]{1,0:T(8,128)(2,1)} custom-call(bf16[128,1024]{1,0:T(8,128)(2,1)S(1)} %bitcast.23, bf16[640,128]{1,0:T(8,128)(2,1)S(1)} %get-tuple-element.40.refs_0_.refs_4_, bf16[640,128]{1,0:T(8,128)(2,1)S(1)} %collective-permute-done.refs_1_.refs_5_, bf16[640,128]{1,0:T(8,128)(2,1)S(1)} %collective-permute-done.1.refs_2_.refs_6_, ...), custom_call_target="tpu_custom_call" | custom-call | bytes 1048576 | tf_op jit(solution)/shard_map/pallas_call | solution.py:165
  44.6 3.5 %collective-permute-done.7.refs_2_ = bf16[32,1152]{1,0:T(8,128)(2,1)S(1)} collective-permute-done((bf16[32,1152]{1,0:T(8,128)(2,1)S(1)}, bf16[32,1152]{1,0:T(8,128)(2,1)S(1)}, u32[]{:S(2)}, u32[]{:S(2)}) %collective-permute-start.7) | collective-permute-done | bytes 73760 | tf_op jit(solution)/shard_map/ppermute | solution.py:177
  48.1 3.3 %shard_map.161 = (f32[5,32,512]{2,1,0:T(8,128)S(1)}, bf16[5,32,512]{2,1,0:T(8,128)(2,1)S(1)}, bf16[8,1024]{1,0:T(8,128)(2,1)}) custom-call(bf16[32,1152]{1,0:T(8,128)(2,1)S(1)} %shard_map.159.refs_0_, bf16[32,1152]{1,0:T(8,128)(2,1)S(1)} %collective-permute-done.6.refs_1_, bf16[32,1152]{1,0:T(8,128)(2,1)S(1)} %collective-permute-done.7.refs_2_, ...), custom_call_target="tpu_custom_call" | custom-call | tf_op jit(solution)/shard_map/pallas_call | solution.py:379
  51.4 1.5 %collective-permute-start.9 = (bf16[5,32,512]{2,1,0:T(8,128)(2,1)S(1)}, bf16[5,32,512]{2,1,0:T(8,128)(2,1)S(1)}, u32[]{:S(2)}, u32[]{:S(2)}) collective-permute-start(bf16[5,32,512]{2,1,0:T(8,128)(2,1)S(1)} %get-tuple-element.53), channel_id=1, source_target_pairs={{0,2},{2,0},{1,3},{3,1},{4,6},{6,4},{5,7},{7,5},{8,10},{10,8},{9,1... | collective-permute-start | bytes 491528 | tf_op jit(solution)/shard_map/ppermute | solution.py:515
  52.9 2.4 %collective-permute-start.13 = (bf16[128,256]{1,0:T(8,128)(2,1)S(1)}, bf16[128,256]{1,0:T(8,128)(2,1)S(1)}, u32[]{:S(2)}, u32[]{:S(2)}) collective-permute-start(bf16[128,256]{1,0:T(8,128)(2,1)S(1)} %get-tuple-element.59), channel_id=1, source_target_pairs={{0,12},{4,0},{8,4},{12,8},{1,13},{5,1},{9,5},{13,9},{2,14},{6,2},{... | collective-permute-start | bytes 196616 | tf_op jit(solution)/shard_map/ppermute | solution.py:177
  55.3 1.5 %collective-permute-done.9.other = bf16[5,32,512]{2,1,0:T(8,128)(2,1)S(1)} collective-permute-done((bf16[5,32,512]{2,1,0:T(8,128)(2,1)S(1)}, bf16[5,32,512]{2,1,0:T(8,128)(2,1)S(1)}, u32[]{:S(2)}, u32[]{:S(2)}) %collective-permute-start.9) | collective-permute-done | bytes 163872 | tf_op jit(solution)/shard_map/ppermute | solution.py:515
  56.7 1.4 %shard_map.162 = (f32[8,1024]{1,0:T(8,128)S(1)}, bf16[8,1024]{1,0:T(8,128)(2,1)S(1)}, bf16[8,1024]{1,0:T(8,128)(2,1)S(1)}, bf16[8,1024]{1,0:T(8,128)(2,1)S(1)}) custom-call(f32[5,32,512]{2,1,0:T(8,128)S(1)} %get-tuple-element.52.own, bf16[5,32,512]{2,1,0:T(8,128)(2,1)S(1)} %collective-permute-done.9.other, bf16[2048,1024]{1,0:T(8,128)(2,1)S(1)} %copy-done.1), custom_call_target="tpu_custom_call" | custom-call | tf_op jit(solution)/shard_map/pallas_call | solution.py:420
  58.1 2.4 %collective-permute-start.10 = (bf16[8,1024]{1,0:T(8,128)(2,1)S(1)}, bf16[8,1024]{1,0:T(8,128)(2,1)S(1)}, u32[]{:S(2)}, u32[]{:S(2)}) collective-permute-start(bf16[8,1024]{1,0:T(8,128)(2,1)S(1)} %get-tuple-element.55), channel_id=1, source_target_pairs={{0,12},{4,0},{8,4},{12,8},{1,13},{5,1},{9,5},{13,9},{2,14},{6,2},{... | collective-permute-start | bytes 49160 | tf_op jit(solution)/shard_map/ppermute | solution.py:177
  60.5 1.6 %collective-permute-start.11 = (bf16[8,1024]{1,0:T(8,128)(2,1)S(1)}, bf16[8,1024]{1,0:T(8,128)(2,1)S(1)}, u32[]{:S(2)}, u32[]{:S(2)}) collective-permute-start(bf16[8,1024]{1,0:T(8,128)(2,1)S(1)} %get-tuple-element.56), channel_id=1, source_target_pairs={{0,8},{4,12},{8,0},{12,4},{1,9},{5,13},{9,1},{13,5},{2,10},{6,14},... | collective-permute-start | bytes 49160 | tf_op jit(solution)/shard_map/ppermute | solution.py:177
  62.1 2.0 %collective-permute-start.12 = (bf16[8,1024]{1,0:T(8,128)(2,1)S(1)}, bf16[8,1024]{1,0:T(8,128)(2,1)S(1)}, u32[]{:S(2)}, u32[]{:S(2)}) collective-permute-start(bf16[8,1024]{1,0:T(8,128)(2,1)S(1)} %get-tuple-element.57), channel_id=1, source_target_pairs={{0,4},{4,8},{8,12},{12,0},{1,5},{5,9},{9,13},{13,1},{2,6},{6,10},{... | collective-permute-start | bytes 49160 | tf_op jit(solution)/shard_map/ppermute | solution.py:177
  64.1 2.3 %shard_map.164 = (bf16[128,256]{1,0:T(8,128)(2,1)S(1)}, bf16[128,256]{1,0:T(8,128)(2,1)S(1)}, bf16[128,256]{1,0:T(8,128)(2,1)S(1)}, bf16[128,256]{1,0:T(8,128)(2,1)S(1)}) custom-call(bf16[384,256]{1,0:T(8,128)(2,1)S(1)} %get-tuple-element.62.refs_0_, bf16[384,256]{1,0:T(8,128)(2,1)S(1)} %collective-permute-done.16.refs_1_, ...), custom_call_target="tpu_custom_call" | custom-call | tf_op jit(solution)/shard_map/pallas_call | solution.py:165
  66.4 2.4 %collective-permute-start.15 = (bf16[128,256]{1,0:T(8,128)(2,1)S(1)}, bf16[128,256]{1,0:T(8,128)(2,1)S(1)}, u32[]{:S(2)}, u32[]{:S(2)}) collective-permute-start(bf16[128,256]{1,0:T(8,128)(2,1)S(1)} %get-tuple-element.61), channel_id=1, source_target_pairs={{0,4},{4,8},{8,12},{12,0},{1,5},{5,9},{9,13},{13,1},{2,6},{6,10},{... | collective-permute-start | bytes 196616 | tf_op jit(solution)/shard_map/ppermute | solution.py:177
  68.8 1.5 %collective-permute-start.19 = (bf16[128,256]{1,0:T(8,128)(2,1)S(1)}, bf16[128,256]{1,0:T(8,128)(2,1)S(1)}, u32[]{:S(2)}, u32[]{:S(2)}) collective-permute-start(bf16[128,256]{1,0:T(8,128)(2,1)S(1)} %get-tuple-element.70), channel_id=1, source_target_pairs={{0,12},{4,0},{8,4},{12,8},{1,13},{5,1},{9,5},{13,9},{2,14},{6,2},{... | collective-permute-start | bytes 196616 | tf_op jit(solution)/shard_map/ppermute | solution.py:177
  73.2 2.9 %collective-permute-done.20.refs_6_ = bf16[128,256]{1,0:T(8,128)(2,1)S(1)} collective-permute-done((bf16[128,256]{1,0:T(8,128)(2,1)S(1)}, bf16[128,256]{1,0:T(8,128)(2,1)S(1)}, u32[]{:S(2)}, u32[]{:S(2)}) %collective-permute-start.20) | collective-permute-done | bytes 65568 | tf_op jit(solution)/shard_map/ppermute | solution.py:177
  (50 shorter events, 14.5 us)
Async XLA Ops:
  0.6 47.5 %copy-start.9 = (f32[2048]{0:T(1024)S(1)}, f32[2048]{0:T(1024)}, u32[]{:S(2)}) copy-start(f32[2048]{0:T(1024)} %param.23) | copy-start | bytes 24580
  3.4 44.7 %copy-start = (bf16[1024,2048]{1,0:T(8,128)(2,1)S(1)}, bf16[1024,2048]{1,0:T(8,128)(2,1)}, u32[]{:S(2)}) copy-start(bf16[1024,2048]{1,0:T(8,128)(2,1)} %refs_9_.1) | copy-start | bytes 12582916
  3.4 14.8 %collective-permute-start = (bf16[640,128]{1,0:T(8,128)(2,1)}, bf16[640,128]{1,0:T(8,128)(2,1)S(1)}, u32[]{:S(2)}, u32[]{:S(2)}) collective-permute-start(bf16[640,128]{1,0:T(8,128)(2,1)} %get-tuple-element.41), channel_id=1, source_target_pairs={{0,4},{4,8},{8,12},{12,0},{1,5},{5,9},{9,13},{13,1},{2,6},{6,10},{... | collective-permute-start | bytes 491528 | tf_op jit(solution)/shard_map/ppermute | solution.py:177
  6.5 14.6 %collective-permute-start.1 = (bf16[640,128]{1,0:T(8,128)(2,1)}, bf16[640,128]{1,0:T(8,128)(2,1)S(1)}, u32[]{:S(2)}, u32[]{:S(2)}) collective-permute-start(bf16[640,128]{1,0:T(8,128)(2,1)} %get-tuple-element.42), channel_id=1, source_target_pairs={{0,8},{4,12},{8,0},{12,4},{1,9},{5,13},{9,1},{13,5},{2,10},{6,14},... | collective-permute-start | bytes 491528 | tf_op jit(solution)/shard_map/ppermute | solution.py:177
  9.1 12.0 %collective-permute-start.2 = (bf16[640,128]{1,0:T(8,128)(2,1)}, bf16[640,128]{1,0:T(8,128)(2,1)S(1)}, u32[]{:S(2)}, u32[]{:S(2)}) collective-permute-start(bf16[640,128]{1,0:T(8,128)(2,1)} %get-tuple-element.43), channel_id=1, source_target_pairs={{0,12},{4,0},{8,4},{12,8},{1,13},{5,1},{9,5},{13,9},{2,14},{6,2},{... | collective-permute-start | bytes 491528 | tf_op jit(solution)/shard_map/ppermute | solution.py:177
  17.2 15.4 %collective-permute-start.3 = (bf16[384,128]{1,0:T(8,128)(2,1)S(1)}, bf16[384,128]{1,0:T(8,128)(2,1)S(1)}, u32[]{:S(2)}, u32[]{:S(2)}) collective-permute-start(bf16[384,128]{1,0:T(8,128)(2,1)S(1)} %get-tuple-element.45), channel_id=1, source_target_pairs={{0,4},{4,8},{8,12},{12,0},{1,5},{5,9},{9,13},{13,1},{2,6},{6,10},{... | collective-permute-start | bytes 294920 | tf_op jit(solution)/shard_map/ppermute | solution.py:177
  17.9 15.4 %collective-permute-start.4 = (bf16[384,128]{1,0:T(8,128)(2,1)S(1)}, bf16[384,128]{1,0:T(8,128)(2,1)S(1)}, u32[]{:S(2)}, u32[]{:S(2)}) collective-permute-start(bf16[384,128]{1,0:T(8,128)(2,1)S(1)} %get-tuple-element.46), channel_id=1, source_target_pairs={{0,8},{4,12},{8,0},{12,4},{1,9},{5,13},{9,1},{13,5},{2,10},{6,14},... | collective-permute-start | bytes 294920 | tf_op jit(solution)/shard_map/ppermute | solution.py:177
  18.2 15.0 %collective-permute-start.5 = (bf16[384,128]{1,0:T(8,128)(2,1)S(1)}, bf16[384,128]{1,0:T(8,128)(2,1)S(1)}, u32[]{:S(2)}, u32[]{:S(2)}) collective-permute-start(bf16[384,128]{1,0:T(8,128)(2,1)S(1)} %get-tuple-element.47), channel_id=1, source_target_pairs={{0,12},{4,0},{8,4},{12,8},{1,13},{5,1},{9,5},{13,9},{2,14},{6,2},{... | collective-permute-start | bytes 294920 | tf_op jit(solution)/shard_map/ppermute | solution.py:177
  23.1 13.9 %collective-permute-start.8 = (bf16[32,1152]{1,0:T(8,128)(2,1)S(1)}, bf16[32,1152]{1,0:T(8,128)(2,1)S(1)}, u32[]{:S(2)}, u32[]{:S(2)}) collective-permute-start(bf16[32,1152]{1,0:T(8,128)(2,1)S(1)} %shard_map.159.refs_0_), channel_id=1, source_target_pairs={{0,12},{4,0},{8,4},{12,8},{1,13},{5,1},{9,5},{13,9},{2,14},{6,2},{... | collective-permute-start | bytes 221192 | tf_op jit(solution)/shard_map/ppermute | solution.py:177
  32.6 15.5 %collective-permute-start.7 = (bf16[32,1152]{1,0:T(8,128)(2,1)S(1)}, bf16[32,1152]{1,0:T(8,128)(2,1)S(1)}, u32[]{:S(2)}, u32[]{:S(2)}) collective-permute-start(bf16[32,1152]{1,0:T(8,128)(2,1)S(1)} %shard_map.159.refs_0_), channel_id=1, source_target_pairs={{0,8},{4,12},{8,0},{12,4},{1,9},{5,13},{9,1},{13,5},{2,10},{6,14},... | collective-permute-start | bytes 221192 | tf_op jit(solution)/shard_map/ppermute | solution.py:177
  32.6 15.5 %collective-permute-start.6 = (bf16[32,1152]{1,0:T(8,128)(2,1)S(1)}, bf16[32,1152]{1,0:T(8,128)(2,1)S(1)}, u32[]{:S(2)}, u32[]{:S(2)}) collective-permute-start(bf16[32,1152]{1,0:T(8,128)(2,1)S(1)} %shard_map.159.refs_0_), channel_id=1, source_target_pairs={{0,4},{4,8},{8,12},{12,0},{1,5},{5,9},{9,13},{13,1},{2,6},{6,10},{... | collective-permute-start | bytes 221192 | tf_op jit(solution)/shard_map/ppermute | solution.py:177
  33.3 27.3 %collective-permute-start.16 = (bf16[384,256]{1,0:T(8,128)(2,1)S(1)}, bf16[384,256]{1,0:T(8,128)(2,1)S(1)}, u32[]{:S(2)}, u32[]{:S(2)}) collective-permute-start(bf16[384,256]{1,0:T(8,128)(2,1)S(1)} %get-tuple-element.64), channel_id=1, source_target_pairs={{0,4},{4,8},{8,12},{12,0},{1,5},{5,9},{9,13},{13,1},{2,6},{6,10},{... | collective-permute-start | bytes 589832 | tf_op jit(solution)/shard_map/ppermute | solution.py:177
  36.1 26.0 %collective-permute-start.17 = (bf16[384,256]{1,0:T(8,128)(2,1)S(1)}, bf16[384,256]{1,0:T(8,128)(2,1)S(1)}, u32[]{:S(2)}, u32[]{:S(2)}) collective-permute-start(bf16[384,256]{1,0:T(8,128)(2,1)S(1)} %get-tuple-element.66), channel_id=1, source_target_pairs={{0,8},{4,12},{8,0},{12,4},{1,9},{5,13},{9,1},{13,5},{2,10},{6,14},... | collective-permute-start | bytes 589832 | tf_op jit(solution)/shard_map/ppermute | solution.py:177
  37.0 27.0 %collective-permute-start.18 = (bf16[384,256]{1,0:T(8,128)(2,1)S(1)}, bf16[384,256]{1,0:T(8,128)(2,1)S(1)}, u32[]{:S(2)}, u32[]{:S(2)}) collective-permute-start(bf16[384,256]{1,0:T(8,128)(2,1)S(1)} %get-tuple-element.68), channel_id=1, source_target_pairs={{0,12},{4,0},{8,4},{12,8},{1,13},{5,1},{9,5},{13,9},{2,14},{6,2},{... | collective-permute-start | bytes 589832 | tf_op jit(solution)/shard_map/ppermute | solution.py:177
  51.4 5.3 %collective-permute-start.9 = (bf16[5,32,512]{2,1,0:T(8,128)(2,1)S(1)}, bf16[5,32,512]{2,1,0:T(8,128)(2,1)S(1)}, u32[]{:S(2)}, u32[]{:S(2)}) collective-permute-start(bf16[5,32,512]{2,1,0:T(8,128)(2,1)S(1)} %get-tuple-element.53), channel_id=1, source_target_pairs={{0,2},{2,0},{1,3},{3,1},{4,6},{6,4},{5,7},{7,5},{8,10},{10,8},{9,1... | collective-permute-start | bytes 491528 | tf_op jit(solution)/shard_map/ppermute | solution.py:515
  52.9 13.5 %collective-permute-start.13 = (bf16[128,256]{1,0:T(8,128)(2,1)S(1)}, bf16[128,256]{1,0:T(8,128)(2,1)S(1)}, u32[]{:S(2)}, u32[]{:S(2)}) collective-permute-start(bf16[128,256]{1,0:T(8,128)(2,1)S(1)} %get-tuple-element.59), channel_id=1, source_target_pairs={{0,12},{4,0},{8,4},{12,8},{1,13},{5,1},{9,5},{13,9},{2,14},{6,2},{... | collective-permute-start | bytes 196616 | tf_op jit(solution)/shard_map/ppermute | solution.py:177
  58.1 10.7 %collective-permute-start.10 = (bf16[8,1024]{1,0:T(8,128)(2,1)S(1)}, bf16[8,1024]{1,0:T(8,128)(2,1)S(1)}, u32[]{:S(2)}, u32[]{:S(2)}) collective-permute-start(bf16[8,1024]{1,0:T(8,128)(2,1)S(1)} %get-tuple-element.55), channel_id=1, source_target_pairs={{0,12},{4,0},{8,4},{12,8},{1,13},{5,1},{9,5},{13,9},{2,14},{6,2},{... | collective-permute-start | bytes 49160 | tf_op jit(solution)/shard_map/ppermute | solution.py:177
  60.5 9.7 %collective-permute-start.11 = (bf16[8,1024]{1,0:T(8,128)(2,1)S(1)}, bf16[8,1024]{1,0:T(8,128)(2,1)S(1)}, u32[]{:S(2)}, u32[]{:S(2)}) collective-permute-start(bf16[8,1024]{1,0:T(8,128)(2,1)S(1)} %get-tuple-element.56), channel_id=1, source_target_pairs={{0,8},{4,12},{8,0},{12,4},{1,9},{5,13},{9,1},{13,5},{2,10},{6,14},... | collective-permute-start | bytes 49160 | tf_op jit(solution)/shard_map/ppermute | solution.py:177
  62.1 9.2 %collective-permute-start.12 = (bf16[8,1024]{1,0:T(8,128)(2,1)S(1)}, bf16[8,1024]{1,0:T(8,128)(2,1)S(1)}, u32[]{:S(2)}, u32[]{:S(2)}) collective-permute-start(bf16[8,1024]{1,0:T(8,128)(2,1)S(1)} %get-tuple-element.57), channel_id=1, source_target_pairs={{0,4},{4,8},{8,12},{12,0},{1,5},{5,9},{9,13},{13,1},{2,6},{6,10},{... | collective-permute-start | bytes 49160 | tf_op jit(solution)/shard_map/ppermute | solution.py:177
  64.1 8.0 %collective-permute-start.14 = (bf16[128,256]{1,0:T(8,128)(2,1)S(1)}, bf16[128,256]{1,0:T(8,128)(2,1)S(1)}, u32[]{:S(2)}, u32[]{:S(2)}) collective-permute-start(bf16[128,256]{1,0:T(8,128)(2,1)S(1)} %get-tuple-element.60), channel_id=1, source_target_pairs={{0,8},{4,12},{8,0},{12,4},{1,9},{5,13},{9,1},{13,5},{2,10},{6,14},... | collective-permute-start | bytes 196616 | tf_op jit(solution)/shard_map/ppermute | solution.py:177
  66.4 6.1 %collective-permute-start.15 = (bf16[128,256]{1,0:T(8,128)(2,1)S(1)}, bf16[128,256]{1,0:T(8,128)(2,1)S(1)}, u32[]{:S(2)}, u32[]{:S(2)}) collective-permute-start(bf16[128,256]{1,0:T(8,128)(2,1)S(1)} %get-tuple-element.61), channel_id=1, source_target_pairs={{0,4},{4,8},{8,12},{12,0},{1,5},{5,9},{9,13},{13,1},{2,6},{6,10},{... | collective-permute-start | bytes 196616 | tf_op jit(solution)/shard_map/ppermute | solution.py:177
  68.8 4.4 %collective-permute-start.19 = (bf16[128,256]{1,0:T(8,128)(2,1)S(1)}, bf16[128,256]{1,0:T(8,128)(2,1)S(1)}, u32[]{:S(2)}, u32[]{:S(2)}) collective-permute-start(bf16[128,256]{1,0:T(8,128)(2,1)S(1)} %get-tuple-element.70), channel_id=1, source_target_pairs={{0,12},{4,0},{8,4},{12,8},{1,13},{5,1},{9,5},{13,9},{2,14},{6,2},{... | collective-permute-start | bytes 196616 | tf_op jit(solution)/shard_map/ppermute | solution.py:177
  70.3 5.9 %collective-permute-start.20 = (bf16[128,256]{1,0:T(8,128)(2,1)S(1)}, bf16[128,256]{1,0:T(8,128)(2,1)S(1)}, u32[]{:S(2)}, u32[]{:S(2)}) collective-permute-start(bf16[128,256]{1,0:T(8,128)(2,1)S(1)} %get-tuple-element.71), channel_id=1, source_target_pairs={{0,8},{4,12},{8,0},{12,4},{1,9},{5,13},{9,1},{13,5},{2,10},{6,14},... | collective-permute-start | bytes 196616 | tf_op jit(solution)/shard_map/ppermute | solution.py:177
  71.3 6.1 %collective-permute-start.21 = (bf16[128,256]{1,0:T(8,128)(2,1)S(1)}, bf16[128,256]{1,0:T(8,128)(2,1)S(1)}, u32[]{:S(2)}, u32[]{:S(2)}) collective-permute-start(bf16[128,256]{1,0:T(8,128)(2,1)S(1)} %get-tuple-element.72), channel_id=1, source_target_pairs={{0,4},{4,8},{8,12},{12,0},{1,5},{5,9},{9,13},{13,1},{2,6},{6,10},{... | collective-permute-start | bytes 196616 | tf_op jit(solution)/shard_map/ppermute | solution.py:177
  (8 other events, 82.8 us)

commit v3 on v2

--- a/solution.py
+++ b/solution.py
@@ -172,9 +172,9 @@
     )(*ins)
 
 
-def shift(value, by):
+def trade(value, by):
     n = lax.axis_size("seq")
-    return lax.ppermute(value, "seq", [(i, (i + by) % n) for i in range(n)])
+    return lax.ppermute(value, "seq", [(i, i ^ by) for i in range(n)])
 
 
 def parts3(value):
@@ -192,7 +192,7 @@
     copies = []
     for c, width in enumerate(widths):
         for s in range(n):
-            dest = lax.rem(me + s, n)
+            dest = lax.bitwise_xor(me, s)
             at = pl.ds(pl.multiple_of(dest * group + first, LANES), width)
             for i, ref in enumerate((q, k, v)):
                 to = outs[c * n + s].at[pl.ds(i * tokens, tokens), :]
@@ -206,7 +206,7 @@
         half = audio[0].shape[1]
         mine = pl.ds(pl.multiple_of(lax.axis_index("tp") * half, LANES), half)
         parts = [ref[...].astype(F32) for ref in audio[:3]] + [audio[3][:, mine].astype(F32)]
-        blocks = [part[:, c : c + LANES] for part in parts for c in range(0, half, LANES)]
+        blocks = [part[:, c : c + widths[0]] for part in parts for c in range(0, half, widths[0])]
         extra = jnp.concatenate(blocks, axis=0).astype(BF16)
         for s in range(n):
             outs[s][3 * tokens :, :] = extra
@@ -216,7 +216,7 @@
 
 def pack(video, audio, keep, n, first, widths, limit, moved):
     tokens = video[0].shape[0]
-    extra = 4 * audio[0].size // LANES if audio else 0
+    extra = 4 * audio[0].size // widths[0] if audio else 0
     shapes = [sds((3 * tokens + extra, w)) for w in widths for _ in range(n)]
     stay = pl.BlockSpec(memory_space=pl.ANY)
     return pl.pallas_call(
@@ -231,57 +231,121 @@
 
 
 def audio_rows(tails, part, pair, rows, pairs):
-    at = (part * pairs + pair) * rows
-    return jnp.concatenate([t[at : at + rows] for t in tails], axis=0)
-
-
-def attend_kernel(n, tokens, *refs):
-    inputs, outs = refs[:-n], refs[-n:]
+    per = tails[0].shape[1] // LANES
+    at, side = (part * pairs + pair) // per * rows, pair % per * LANES
+    return jnp.concatenate([t[at : at + rows, side : side + LANES] for t in tails], axis=0)
+
+
+def attend_heads(pieces, tokens, put):
     scale = LOG2E / math.sqrt(VHEAD)
-    first = 0
-    for c in range(0, len(inputs), n):
-        pieces = inputs[c : c + n]
-        for h in range(pieces[0].shape[1] // VHEAD):
-            cols = slice(h * VHEAD, (h + 1) * VHEAD)
-            keys = jnp.concatenate([p[tokens : 2 * tokens, cols] for p in pieces], axis=0)
-            values = jnp.concatenate([p[2 * tokens : 3 * tokens, cols] for p in pieces], axis=0)
-            for p, out in zip(pieces, outs):
-                s = lax.dot_general(p[0:tokens, cols], keys, NT, preferred_element_type=F32)
-                s = s * scale
-                w = jnp.exp2(s - jnp.max(s, axis=1, keepdims=True))
-                total = jnp.sum(w, axis=1, keepdims=True)
-                o = jnp.dot(w.astype(BF16), values, preferred_element_type=F32)
-                out[:, first + h * VHEAD : first + (h + 1) * VHEAD] = (o / total).astype(BF16)
-        first += pieces[0].shape[1]
-
-
-def unpack_kernel(n, widths, *refs):
-    pieces, out, sem = refs[: n * len(widths)], refs[-2], refs[-1]
-    me = lax.axis_index("seq")
-    group = sum(widths)
-    first = 0
-    copies = []
-    for c, width in enumerate(widths):
-        for s in range(n):
-            dest = lax.rem(me + s, n)
-            at = pl.ds(pl.multiple_of(dest * group + first, LANES), width)
-            copies.append(pltpu.make_async_copy(pieces[c * n + s], out.at[:, at], sem.at[len(copies)]))
-            copies[-1].start()
-        first += width
+    for h in range(pieces[0].shape[1] // VHEAD):
+        cols = slice(h * VHEAD, (h + 1) * VHEAD)
+        keys = jnp.concatenate([p[tokens : 2 * tokens, cols] for p in pieces], axis=0)
+        values = jnp.concatenate([p[2 * tokens : 3 * tokens, cols] for p in pieces], axis=0)
+        for s, p in enumerate(pieces):
+            t = lax.dot_general(p[0:tokens, cols], keys, NT, preferred_element_type=F32) * scale
+            w = jnp.exp2(t - jnp.max(t, axis=1, keepdims=True))
+            total = jnp.sum(w, axis=1, keepdims=True)
+            o = jnp.dot(w.astype(BF16), values, preferred_element_type=F32)
+            put(s, h, (o / total).astype(BF16))
+
+
+def middle_kernel(n, counts, *refs):
+    inputs, last, outs, sem = refs[: -2 * n - 1], refs[-2 * n - 1 : -n - 1], refs[-n - 1 : -1], refs[-1]
+    tokens = last[0].shape[0] // 3
+    top = pl.ds(0, 3 * tokens)
+    copies = [
+        pltpu.make_async_copy(last[s], outs[s].at[top, :], sem.at[s]) for s in range(n)
+    ]
+    for copy in copies:
+        copy.start()
+    head = 0
+    for c, count in enumerate(counts):
+        first = head * VHEAD
+
+        def put(s, h, rows, first=first):
+            at = first + h * VHEAD
+            low, side = (at // outs[0].shape[1]) * tokens + 3 * tokens, at % outs[0].shape[1]
+            outs[s][low : low + tokens, side : side + VHEAD] = rows
+
+        attend_heads(inputs[c * n : (c + 1) * n], tokens, put)
+        head += count
     for copy in copies:
         copy.wait()
 
 
-def unpack(pieces, n, widths):
-    tokens = pieces[0].shape[0]
+def middle(chunks, last, n, moved):
+    counts = [c[0].shape[1] // VHEAD for c in chunks]
+    tokens = last[0].shape[0] // 3
+    width = last[0].shape[1]
+    tall = 3 * tokens + -(-sum(counts) * VHEAD // width) * tokens
+    pieces = [p for c in chunks for p in c]
     return pl.pallas_call(
-        functools.partial(unpack_kernel, n, widths),
-        out_shape=sds((tokens, n * sum(widths))),
-        in_specs=[pl.BlockSpec(memory_space=pltpu.VMEM)] * len(pieces),
-        out_specs=pl.BlockSpec(memory_space=pl.ANY),
-        scratch_shapes=[pltpu.SemaphoreType.DMA((len(pieces),))],
+        functools.partial(middle_kernel, n, counts),
+        out_shape=(sds((tall, width)),) * n,
+        in_specs=[whole()] * len(pieces) + [pl.BlockSpec(memory_space=pl.ANY)] * n,
+        out_specs=(whole(),) * n,
+        scratch_shapes=[pltpu.SemaphoreType.DMA((n,))],
         compiler_params=pltpu.CompilerParams(vmem_limit_bytes=16 * MIB),
-    )(*pieces)
+        cost_estimate=pl.CostEstimate(flops=0, bytes_accessed=moved, transcendentals=0),
+    )(*pieces, *last)
+
+
+def last_kernel(n, tokens, *refs):
+    pieces, sums, outs = refs[:n], refs[n : 2 * n], refs[2 * n :]
+    width = outs[0].shape[1]
+
+    def put(s, h, rows):
+        outs[s][:tokens, h * VHEAD : (h + 1) * VHEAD] = rows
+
+    for s in range(n):
+        part = sums[s][...].astype(F32)
+        blocks = [part[:, c : c + width] for c in range(0, part.shape[1], width)]
+        outs[s][tokens:, :] = jnp.concatenate(blocks, axis=0).astype(BF16)
+    attend_heads(pieces, tokens, put)
+
+
+def unpack_kernel(n, heads, tokens, *refs):
+    middles, lasts, own = refs[:n], refs[n : 2 * n], refs[2 * n]
+    out, mlp, sem = refs[2 * n + 1 :]
+    me = lax.axis_index("seq")
+    width = lasts[0].shape[1]
+    group = heads * VHEAD
+    copies = []
+
+    def start(source, owner, first, size):
+        at = pl.ds(pl.multiple_of(owner * group + first, LANES), size)
+        copies.append(pltpu.make_async_copy(source, out.at[:, at], sem.at[len(copies)]))
+        copies[-1].start()
+
+    early = group - width
+    for s in range(n):
+        for c in range(0, early, width):
+            rows = pl.ds(3 * tokens + c // width * tokens, tokens)
+            size = min(width, early - c)
+            start(middles[s].at[rows, pl.ds(0, size)], lax.bitwise_xor(me, s), c, size)
+        start(lasts[s].at[pl.ds(0, tokens), :], lax.bitwise_xor(me, s), early, width)
+    rows, columns = own.shape
+    tails = [lasts[s][tokens:, :].astype(F32) for s in range(1, n)]
+    for c in range(columns // width):
+        total = own[:, c * width : (c + 1) * width]
+        for tail in tails:
+            total = total + tail[c * rows : (c + 1) * rows]
+        mlp[:, c * width : (c + 1) * width] = total.astype(BF16)
+    for copy in copies:
+        copy.wait()
+
+
+def unpack(middles, lasts, own, n, heads, tokens):
+    count = n * (-(-(heads * VHEAD - lasts[0].shape[1]) // lasts[0].shape[1]) + 1)
+    return pl.pallas_call(
+        functools.partial(unpack_kernel, n, heads, tokens),
+        out_shape=(sds((tokens, n * heads * VHEAD)), sds(own.shape)),
+        in_specs=[pl.BlockSpec(memory_space=pltpu.VMEM)] * (2 * n + 1),
+        out_specs=(pl.BlockSpec(memory_space=pl.ANY), whole()),
+        scratch_shapes=[pltpu.SemaphoreType.DMA((count,))],
+        compiler_params=pltpu.CompilerParams(vmem_limit_bytes=16 * MIB),
+    )(*middles, *lasts, own)
 
 
 def low_half(shape):
@@ -292,7 +356,7 @@
     pieces, keys, values, out = refs[:n], refs[n], refs[n + 1], refs[n + 2]
     columns = keys.shape[1]
     pairs = columns // LANES
-    tails = [p[3 * tokens : 3 * tokens + rows * pairs, :].astype(F32) for p in pieces]
+    tails = [p[3 * tokens :, :].astype(F32) for p in pieces]
     count = n * rows
     scale = LOG2E / math.sqrt(CHEAD)
     low = low_half((count, LANES))
@@ -331,7 +395,7 @@
         for s in range(n):
             whole = got[s][...].astype(F32)
             if s:
-                whole = jnp.concatenate([whole[-s * rows :], whole[: -s * rows]], axis=0)
+                whole = jnp.concatenate([whole[(i ^ s) * rows :][:rows] for i in range(n)], axis=0)
             whole, stats = whole[:, :columns], whole[:, columns:]
             piece = [stats[:, j * heads : (j + 1) * heads] for j in range(6)]
             peaks.append(piece[0] + piece[1] + piece[2])
@@ -455,13 +519,6 @@
         out[:, cols] = lax.dot_general(w, both(2, pair), TN, preferred_element_type=F32).astype(BF16)
 
 
-def add_kernel(own, *refs):
-    total = own[...]
-    for ref in refs[:-1]:
-        total = total + ref[...].astype(F32)
-    refs[-1][...] = total.astype(BF16)
-
-
 def short_body(vq, vk, vv, cq, ak, av, aq, ck, cv, ai, gain, up, down):
     n = lax.axis_size("seq")
     tokens = vq.shape[0]
@@ -472,20 +529,7 @@
     video = (vq, vk, vv)
 
     def send(own, *first):
-        return [own[0]] + [shift(after(own[s], *first), s) for s in range(1, n)]
-
-    def give_back(own):
-        return [own[0]] + [shift(own[s], -s) for s in range(1, n)]
-
-    def attended(chunks, moved):
-        width = sum(c[0].shape[1] for c in chunks)
-        return call(
-            functools.partial(attend_kernel, n, tokens),
-            [p for c in chunks for p in c],
-            [sds((tokens, width))] * n,
-            moved=moved,
-            limit=16,
-        )
+        return [own[0]] + [trade(after(own[s], *first), s) for s in range(1, n)]
 
     wait = 16 * MIB
     packed = pack(video, (aq, ak, av, ai), (), n, 0, widths[:1], 60, 6 * vq.size)
@@ -501,8 +545,7 @@
         limit=16,
     )
     shares = send([share] * n)
-    chunk_2 = send(packed[n:], *chunk_1[1:])
-    first = attended([chunk_0, chunk_1], 1 * MIB)
+    chunk_2 = send(middle([chunk_0, chunk_1], packed[n:], n, MIB), *shares[1:])
     (heard,) = call(
         functools.partial(heard_kernel, n, tokens, rows),
         (cq, *chunk_0),
@@ -510,14 +553,18 @@
         moved=1 * MIB,
         limit=16,
     )
-    gain = after(gain.reshape(1, -1), first[0], heard)
+    gain = after(gain.reshape(1, -1), heard)
     own_sum, sent_sum, seen = combine(shares, chunk_0, gain, up, tokens, rows, 512)
     other_sum = lax.ppermute(sent_sum, "tp", [(0, 1), (1, 0)])
-    mixed_a = give_back(first)
     results = finish(own_sum, other_sum, down, n, rows, features, 512)
-    (mlp,) = call(add_kernel, give_back(results), [sds((rows, columns))])
-    mixed_b = give_back(attended([chunk_2], 0 * MIB))
-    mixed = unpack((after(mixed_a[0], mlp), *mixed_a[1:], *mixed_b), n, (widths[0] + widths[1], widths[2]))
+    ends = call(
+        functools.partial(last_kernel, n, tokens),
+        (*chunk_2, *results),
+        [sds((tokens + rows * columns // widths[2], widths[2]))] * n,
+        limit=16,
+    )
+    ends = [ends[0]] + [trade(ends[s], s) for s in range(1, n)]
+    mixed, mlp = unpack(chunk_2, ends, results[0], n, heads, tokens)
     return mixed, heard, seen, mlp
 
 
@@ -525,7 +572,7 @@
     n = lax.axis_size("seq")
     heads = vq.shape[1] // VHEAD
     return (
-        1 < n <= 8
+        n in (2, 4, 8)
         and lax.axis_size("tp") == 2
         and heads % n == 0
         and heads // n > 2

time: 78.7 us -> 74.7 us (0.949)
  starting transfers between devices: 42.2 us -> 30.4 us
  waiting for transfers between devices: 10.4 us -> 17.1 us
  Pallas kernels: 19 us -> 20 us
    ppermute x21 -> x15, starting transfers between devices: 40.7 us -> 28.9 us  [trade(): return lax.ppermute(value, 'seq', [(i, i ^ by) for i in range(n)])]
    ppermute x21 -> x15, waiting for transfers between devices: 8.9 us -> 13.3 us  [trade(): return lax.ppermute(value, 'seq', [(i, i ^ by) for i in range(n)])]
    pallas_call x1 -> x2, Pallas kernels: 0.85 us -> 4.78 us  [the longest x1 3.32 us: middle(): pl.pallas_call(functools.partial(middle_kernel, n, counts), out_shape=(sd...]
    pallas_call x5 -> x3, Pallas kernels: 9.9 us -> 7.03 us  [call(): pl.pallas_call(kernel, out_shape=tuple(outs), in_specs=[whole()] * len(in...]
    ppermute x1, waiting for transfers between devices: 1.45 us -> 3.83 us  [short_body(): other_sum = lax.ppermute(sent_sum, 'tp', [(0, 1), (1, 0)])]
  transfers between devices with their start and end apart: 22 -> 16, of which waited for: 6 -> 7; matrix products, arithmetic and copies ran while one was open for 0% -> 0% of each run, Pallas kernels for 20% -> 18%
where the time goes in v3:
time: 74.7 us; the launch traced here: 74.2 us
  starting transfers between devices  30.4 us (41%)
  Pallas kernels  20 us (27%)
  waiting for transfers between devices  17.1 us (23%)
  local copies, waits for them, and re-layouts  5.96 us (8%)
  between operations  0.76 us (1%)
    ppermute x15, starting transfers between devices, trade(): return lax.ppermute(value, 'seq', [(i, i ^ by) for i in range(n)])  28.9 us
    ppermute x15, waiting for transfers between devices, trade(): return lax.ppermute(value, 'seq', [(i, i ^ by) for i in range(n)])  13.3 us
    pallas_call x3, Pallas kernels, call(): pl.pallas_call(kernel, out_shape=tuple(outs), in_specs=[whole()] * len(in...  7.03 us
    unnamed x20, local copies, waits for them, and re-layouts  5.96 us
    ppermute x1, waiting for transfers between devices, short_body(): other_sum = lax.ppermute(sent_sum, 'tp', [(0, 1), (1, 0)])  3.83 us
    pallas_call x2, Pallas kernels, pack(): pl.pallas_call(functools.partial(pack_kernel, n, first, widths, len(audio...  3.52 us
    pallas_call x1, Pallas kernels, middle(): pl.pallas_call(functools.partial(middle_kernel, n, counts), out_shape=(sd...  3.32 us
    pallas_call x1, Pallas kernels, combine(): pl.pallas_call(functools.partial(combine_kernel, n, tokens, rows), grid=(...  3.29 us
  transfers between devices with their start and end apart: 16, of which 7 were waited for; matrix products, arithmetic and copies ran while one was open for 0% of the time, Pallas kernels for 18%

profile of v3, /device:TPU:0, one launch (start us, length us, event | category | flops | bytes accessed | tf_op | source)
XLA Modules:
  0.0 74.2 jit_solution(8738373617748881466)
XLA Ops:
  0.7 2.7 %shard_map.156 = (bf16[640,128]{1,0:T(8,128)(2,1)}, bf16[640,128]{1,0:T(8,128)(2,1)}, bf16[640,128]{1,0:T(8,128)(2,1)}, bf16[640,128]{1,0:T(8,128)(2,1)}) custom-call(bf16[128,2048]{1,0:T(8,128)(2,1)} %bitcast.15, bf16[128,2048]{1,0:T(8,128)(2,1)} %bitcast.17, bf16[128,2048]{1,0:T(8,128)(2,1)} %bitcast.19, bf16[8,1024]{1,0:T(8,128)(2,1)} %bitcast.27, ...), custom_call_target="tpu_custom_call" | custom-call | bytes 1572864 | tf_op jit(solution)/shard_map/pallas_call | solution.py:222
  3.4 3.1 %collective-permute-start = (bf16[640,128]{1,0:T(8,128)(2,1)}, bf16[640,128]{1,0:T(8,128)(2,1)S(1)}, u32[]{:S(2)}, u32[]{:S(2)}) collective-permute-start(bf16[640,128]{1,0:T(8,128)(2,1)} %get-tuple-element.42), channel_id=1, source_target_pairs={{0,4},{4,0},{8,12},{12,8},{1,5},{5,1},{9,13},{13,9},{2,6},{6,2},{1... | collective-permute-start | bytes 491528 | tf_op jit(solution)/shard_map/ppermute | solution.py:177
  6.5 2.6 %collective-permute-start.1 = (bf16[640,128]{1,0:T(8,128)(2,1)}, bf16[640,128]{1,0:T(8,128)(2,1)S(1)}, u32[]{:S(2)}, u32[]{:S(2)}) collective-permute-start(bf16[640,128]{1,0:T(8,128)(2,1)} %get-tuple-element.43), channel_id=1, source_target_pairs={{0,8},{4,12},{8,0},{12,4},{1,9},{5,13},{9,1},{13,5},{2,10},{6,14},... | collective-permute-start | bytes 491528 | tf_op jit(solution)/shard_map/ppermute | solution.py:177
  9.1 1.0 %copy-done.2 = bf16[1,128,2048]{2,1,0:T(8,128)(2,1)S(1)} copy-done((bf16[1,128,2048]{2,1,0:T(8,128)(2,1)S(1)}, bf16[1,128,2048]{2,1,0:T(8,128)(2,1)}, u32[]{:S(2)}) %copy-start.2) | copy-done | bytes 524312
  16.8 3.5 %collective-permute-start.4 = (bf16[384,128]{1,0:T(8,128)(2,1)S(1)}, bf16[384,128]{1,0:T(8,128)(2,1)S(1)}, u32[]{:S(2)}, u32[]{:S(2)}) collective-permute-start(bf16[384,128]{1,0:T(8,128)(2,1)S(1)} %get-tuple-element.47), channel_id=1, source_target_pairs={{0,8},{4,12},{8,0},{12,4},{1,9},{5,13},{9,1},{13,5},{2,10},{6,14},... | collective-permute-start | bytes 294920 | tf_op jit(solution)/shard_map/ppermute | solution.py:177
  20.3 2.2 %collective-permute-done.1.refs_2_.refs_6_ = bf16[640,128]{1,0:T(8,128)(2,1)S(1)} collective-permute-done((bf16[640,128]{1,0:T(8,128)(2,1)}, bf16[640,128]{1,0:T(8,128)(2,1)S(1)}, u32[]{:S(2)}, u32[]{:S(2)}) %collective-permute-start.1) | collective-permute-done | bytes 163872 | tf_op jit(solution)/shard_map/ppermute | solution.py:177
  22.5 2.0 %shard_map.159.refs_0_ = bf16[32,1152]{1,0:T(8,128)(2,1)S(1)} custom-call(bf16[640,128]{1,0:T(8,128)(2,1)S(1)} %get-tuple-element.41.refs_0_.refs_4_, bf16[640,128]{1,0:T(8,128)(2,1)S(1)} %collective-permute-done.refs_1_.refs_5_, bf16[640,128]{1,0:T(8,128)(2,1)S(1)} %collective-permute-done.1.refs_2_.refs_6_, ...), custom_call_target="tpu_custom_call" | custom-call | bytes 1048576 | tf_op jit(solution)/shard_map/pallas_call | solution.py:165
  24.5 5.9 %collective-permute-start.8 = (bf16[32,1152]{1,0:T(8,128)(2,1)S(1)}, bf16[32,1152]{1,0:T(8,128)(2,1)S(1)}, u32[]{:S(2)}, u32[]{:S(2)}) collective-permute-start(bf16[32,1152]{1,0:T(8,128)(2,1)S(1)} %shard_map.159.refs_0_), channel_id=1, source_target_pairs={{0,12},{4,8},{8,4},{12,0},{1,13},{5,9},{9,5},{13,1},{2,14},{6,10},... | collective-permute-start | bytes 221192 | tf_op jit(solution)/shard_map/ppermute | solution.py:177
  30.4 4.0 %collective-permute-start.7 = (bf16[32,1152]{1,0:T(8,128)(2,1)S(1)}, bf16[32,1152]{1,0:T(8,128)(2,1)S(1)}, u32[]{:S(2)}, u32[]{:S(2)}) collective-permute-start(bf16[32,1152]{1,0:T(8,128)(2,1)S(1)} %shard_map.159.refs_0_), channel_id=1, source_target_pairs={{0,8},{4,12},{8,0},{12,4},{1,9},{5,13},{9,1},{13,5},{2,10},{6,14},... | collective-permute-start | bytes 221192 | tf_op jit(solution)/shard_map/ppermute | solution.py:177
  34.5 3.3 %shard_map.158 = (bf16[512,256]{1,0:T(8,128)(2,1)S(1)}, bf16[512,256]{1,0:T(8,128)(2,1)S(1)}, bf16[512,256]{1,0:T(8,128)(2,1)S(1)}, bf16[512,256]{1,0:T(8,128)(2,1)S(1)}) custom-call(bf16[640,128]{1,0:T(8,128)(2,1)S(1)} %get-tuple-element.41.refs_0_.refs_4_, bf16[640,128]{1,0:T(8,128)(2,1)S(1)} %collective-permute-done.refs_1_.refs_5_, ...), custom_call_target="tpu_custom_call" | custom-call | bytes 1048576 | tf_op jit(solution)/shard_map/pallas_call | solution.py:283
  38.8 2.7 %collective-permute-start.11 = (bf16[512,256]{1,0:T(8,128)(2,1)S(1)}, bf16[512,256]{1,0:T(8,128)(2,1)S(1)}, u32[]{:S(2)}, u32[]{:S(2)}) collective-permute-start(bf16[512,256]{1,0:T(8,128)(2,1)S(1)} %get-tuple-element.61), channel_id=1, source_target_pairs={{0,12},{4,8},{8,4},{12,0},{1,13},{5,9},{9,5},{13,1},{2,14},{6,10},... | collective-permute-start | bytes 786440 | tf_op jit(solution)/shard_map/ppermute | solution.py:177
  41.5 1.7 %collective-permute-start.9 = (bf16[512,256]{1,0:T(8,128)(2,1)S(1)}, bf16[512,256]{1,0:T(8,128)(2,1)S(1)}, u32[]{:S(2)}, u32[]{:S(2)}) collective-permute-start(bf16[512,256]{1,0:T(8,128)(2,1)S(1)} %get-tuple-element.57), channel_id=1, source_target_pairs={{0,4},{4,0},{8,12},{12,8},{1,5},{5,1},{9,13},{13,9},{2,6},{6,2},{1... | collective-permute-start | bytes 786440 | tf_op jit(solution)/shard_map/ppermute | solution.py:177
  43.2 2.8 %shard_map.160 = bf16[128,1024]{1,0:T(8,128)(2,1)} custom-call(bf16[128,1024]{1,0:T(8,128)(2,1)S(1)} %bitcast.23, bf16[640,128]{1,0:T(8,128)(2,1)S(1)} %get-tuple-element.41.refs_0_.refs_4_, bf16[640,128]{1,0:T(8,128)(2,1)S(1)} %collective-permute-done.refs_1_.refs_5_, bf16[640,128]{1,0:T(8,128)(2,1)S(1)} %collective-permute-done.1.refs_2_.refs_6_, ...), custom_call_target="tpu_custom_call" | custom-call | bytes 1048576 | tf_op jit(solution)/shard_map/pallas_call | solution.py:165
  45.9 3.3 %shard_map.161 = (f32[5,32,512]{2,1,0:T(8,128)S(1)}, bf16[5,32,512]{2,1,0:T(8,128)(2,1)S(1)}, bf16[8,1024]{1,0:T(8,128)(2,1)}) custom-call(bf16[32,1152]{1,0:T(8,128)(2,1)S(1)} %shard_map.159.refs_0_, bf16[32,1152]{1,0:T(8,128)(2,1)S(1)} %collective-permute-done.6.refs_1_, bf16[32,1152]{1,0:T(8,128)(2,1)S(1)} %collective-permute-done.7.refs_2_, ...), custom_call_target="tpu_custom_call" | custom-call | tf_op jit(solution)/shard_map/pallas_call | solution.py:443
  49.2 1.5 %collective-permute-start.12 = (bf16[5,32,512]{2,1,0:T(8,128)(2,1)S(1)}, bf16[5,32,512]{2,1,0:T(8,128)(2,1)S(1)}, u32[]{:S(2)}, u32[]{:S(2)}) collective-permute-start(bf16[5,32,512]{2,1,0:T(8,128)(2,1)S(1)} %get-tuple-element.64), channel_id=1, source_target_pairs={{0,2},{2,0},{1,3},{3,1},{4,6},{6,4},{5,7},{7,5},{8,10},{10,8},{9,1... | collective-permute-start | bytes 491528 | tf_op jit(solution)/shard_map/ppermute | solution.py:558
  50.7 3.8 %collective-permute-done.12.other = bf16[5,32,512]{2,1,0:T(8,128)(2,1)S(1)} collective-permute-done((bf16[5,32,512]{2,1,0:T(8,128)(2,1)S(1)}, bf16[5,32,512]{2,1,0:T(8,128)(2,1)S(1)}, u32[]{:S(2)}, u32[]{:S(2)}) %collective-permute-start.12) | collective-permute-done | bytes 163872 | tf_op jit(solution)/shard_map/ppermute | solution.py:558
  54.6 1.4 %shard_map.162 = (f32[8,1024]{1,0:T(8,128)S(1)}, bf16[8,1024]{1,0:T(8,128)(2,1)S(1)}, bf16[8,1024]{1,0:T(8,128)(2,1)S(1)}, bf16[8,1024]{1,0:T(8,128)(2,1)S(1)}) custom-call(f32[5,32,512]{2,1,0:T(8,128)S(1)} %get-tuple-element.63.own, bf16[5,32,512]{2,1,0:T(8,128)(2,1)S(1)} %collective-permute-done.12.other, bf16[2048,1024]{1,0:T(8,128)(2,1)S(1)} %copy-done.1), custom_call_target="tpu_custom_call" | custom-call | tf_op jit(solution)/shard_map/pallas_call | solution.py:484
  56.0 5.6 %collective-permute-done.10.refs_2_ = bf16[512,256]{1,0:T(8,128)(2,1)S(1)} collective-permute-done((bf16[512,256]{1,0:T(8,128)(2,1)S(1)}, bf16[512,256]{1,0:T(8,128)(2,1)S(1)}, u32[]{:S(2)}, u32[]{:S(2)}) %collective-permute-start.10) | collective-permute-done | bytes 262176 | tf_op jit(solution)/shard_map/ppermute | solution.py:177
  61.5 2.3 %shard_map.163 = (bf16[160,256]{1,0:T(8,128)(2,1)S(1)}, bf16[160,256]{1,0:T(8,128)(2,1)S(1)}, bf16[160,256]{1,0:T(8,128)(2,1)S(1)}, bf16[160,256]{1,0:T(8,128)(2,1)S(1)}) custom-call(bf16[512,256]{1,0:T(8,128)(2,1)S(1)} %get-tuple-element.53.refs_0_, bf16[512,256]{1,0:T(8,128)(2,1)S(1)} %collective-permute-done.9.refs_1_, ...), custom_call_target="tpu_custom_call" | custom-call | tf_op jit(solution)/shard_map/pallas_call | solution.py:165
  63.9 2.6 %collective-permute-start.14 = (bf16[160,256]{1,0:T(8,128)(2,1)S(1)}, bf16[160,256]{1,0:T(8,128)(2,1)S(1)}, u32[]{:S(2)}, u32[]{:S(2)}) collective-permute-start(bf16[160,256]{1,0:T(8,128)(2,1)S(1)} %get-tuple-element.71), channel_id=1, source_target_pairs={{0,8},{4,12},{8,0},{12,4},{1,9},{5,13},{9,1},{13,5},{2,10},{6,14},... | collective-permute-start | bytes 245768 | tf_op jit(solution)/shard_map/ppermute | solution.py:177
  66.5 1.8 %collective-permute-start.15 = (bf16[160,256]{1,0:T(8,128)(2,1)S(1)}, bf16[160,256]{1,0:T(8,128)(2,1)S(1)}, u32[]{:S(2)}, u32[]{:S(2)}) collective-permute-start(bf16[160,256]{1,0:T(8,128)(2,1)S(1)} %get-tuple-element.72), channel_id=1, source_target_pairs={{0,12},{4,8},{8,4},{12,0},{1,13},{5,9},{9,5},{13,1},{2,14},{6,10},... | collective-permute-start | bytes 245768 | tf_op jit(solution)/shard_map/ppermute | solution.py:177
  68.5 2.5 %collective-permute-done.14.refs_6_ = bf16[160,256]{1,0:T(8,128)(2,1)S(1)} collective-permute-done((bf16[160,256]{1,0:T(8,128)(2,1)S(1)}, bf16[160,256]{1,0:T(8,128)(2,1)S(1)}, u32[]{:S(2)}, u32[]{:S(2)}) %collective-permute-start.14) | collective-permute-done | bytes 81952 | tf_op jit(solution)/shard_map/ppermute | solution.py:177
  71.0 1.8 %collective-permute-done.15.refs_7_ = bf16[160,256]{1,0:T(8,128)(2,1)S(1)} collective-permute-done((bf16[160,256]{1,0:T(8,128)(2,1)S(1)}, bf16[160,256]{1,0:T(8,128)(2,1)S(1)}, u32[]{:S(2)}, u32[]{:S(2)}) %collective-permute-start.15) | collective-permute-done | bytes 81952 | tf_op jit(solution)/shard_map/ppermute | solution.py:177
  72.8 1.5 %shard_map.164 = (bf16[128,2048]{1,0:T(8,128)(2,1)}, bf16[8,1024]{1,0:T(8,128)(2,1)}) custom-call(bf16[512,256]{1,0:T(8,128)(2,1)S(1)} %get-tuple-element.53.refs_0_, bf16[512,256]{1,0:T(8,128)(2,1)S(1)} %collective-permute-done.9.refs_1_, bf16[512,256]{1,0:T(8,128)(2,1)S(1)} %collective-permute-done.10.refs_2_, ...), custom_call_target="tpu_custom_call" | custom-call | tf_op jit(solution)/shard_map/pallas_call | solution.py:341
  (37 shorter events, 8.0 us)
Async XLA Ops:
  0.6 42.6 %copy-start.7 = (bf16[1,128,1024]{2,1,0:T(8,128)(2,1)S(1)}, bf16[1,128,1024]{2,1,0:T(8,128)(2,1)}, u32[]{:S(2)}) copy-start(bf16[1,128,1024]{2,1,0:T(8,128)(2,1)} %param.16) | copy-start | bytes 786436
  0.6 45.3 %copy-start.9 = (f32[2048]{0:T(1024)S(1)}, f32[2048]{0:T(1024)}, u32[]{:S(2)}) copy-start(f32[2048]{0:T(1024)} %param.23) | copy-start | bytes 24580
  3.4 42.6 %copy-start = (bf16[1024,2048]{1,0:T(8,128)(2,1)S(1)}, bf16[1024,2048]{1,0:T(8,128)(2,1)}, u32[]{:S(2)}) copy-start(bf16[1024,2048]{1,0:T(8,128)(2,1)} %refs_9_.1) | copy-start | bytes 12582916
  3.4 16.9 %collective-permute-start = (bf16[640,128]{1,0:T(8,128)(2,1)}, bf16[640,128]{1,0:T(8,128)(2,1)S(1)}, u32[]{:S(2)}, u32[]{:S(2)}) collective-permute-start(bf16[640,128]{1,0:T(8,128)(2,1)} %get-tuple-element.42), channel_id=1, source_target_pairs={{0,4},{4,0},{8,12},{12,8},{1,5},{5,1},{9,13},{13,9},{2,6},{6,2},{1... | collective-permute-start | bytes 491528 | tf_op jit(solution)/shard_map/ppermute | solution.py:177
  6.5 16.0 %collective-permute-start.1 = (bf16[640,128]{1,0:T(8,128)(2,1)}, bf16[640,128]{1,0:T(8,128)(2,1)S(1)}, u32[]{:S(2)}, u32[]{:S(2)}) collective-permute-start(bf16[640,128]{1,0:T(8,128)(2,1)} %get-tuple-element.43), channel_id=1, source_target_pairs={{0,8},{4,12},{8,0},{12,4},{1,9},{5,13},{9,1},{13,5},{2,10},{6,14},... | collective-permute-start | bytes 491528 | tf_op jit(solution)/shard_map/ppermute | solution.py:177
  9.1 13.4 %collective-permute-start.2 = (bf16[640,128]{1,0:T(8,128)(2,1)}, bf16[640,128]{1,0:T(8,128)(2,1)S(1)}, u32[]{:S(2)}, u32[]{:S(2)}) collective-permute-start(bf16[640,128]{1,0:T(8,128)(2,1)} %get-tuple-element.44), channel_id=1, source_target_pairs={{0,12},{4,8},{8,4},{12,0},{1,13},{5,9},{9,5},{13,1},{2,14},{6,10},... | collective-permute-start | bytes 491528 | tf_op jit(solution)/shard_map/ppermute | solution.py:177
  9.1 1.0 %copy-start.2 = (bf16[1,128,2048]{2,1,0:T(8,128)(2,1)S(1)}, bf16[1,128,2048]{2,1,0:T(8,128)(2,1)}, u32[]{:S(2)}) copy-start(bf16[1,128,2048]{2,1,0:T(8,128)(2,1)} %param.13) | copy-start | bytes 1572868
  10.1 1.0 %copy-start.3 = (bf16[1,128,2048]{2,1,0:T(8,128)(2,1)S(1)}, bf16[1,128,2048]{2,1,0:T(8,128)(2,1)}, u32[]{:S(2)}) copy-start(bf16[1,128,2048]{2,1,0:T(8,128)(2,1)} %param.14) | copy-start | bytes 1572868
  11.2 1.0 %copy-start.4 = (bf16[1,128,2048]{2,1,0:T(8,128)(2,1)S(1)}, bf16[1,128,2048]{2,1,0:T(8,128)(2,1)}, u32[]{:S(2)}) copy-start(bf16[1,128,2048]{2,1,0:T(8,128)(2,1)} %param.15) | copy-start | bytes 1572868
  12.2 0.9 %copy-start.5 = (bf16[1,128,1024]{2,1,0:T(8,128)(2,1)S(1)}, bf16[1,128,1024]{2,1,0:T(8,128)(2,1)}, u32[]{:S(2)}) copy-start(bf16[1,128,1024]{2,1,0:T(8,128)(2,1)} %param.20) | copy-start | bytes 786436
  15.8 18.6 %collective-permute-start.3 = (bf16[384,128]{1,0:T(8,128)(2,1)S(1)}, bf16[384,128]{1,0:T(8,128)(2,1)S(1)}, u32[]{:S(2)}, u32[]{:S(2)}) collective-permute-start(bf16[384,128]{1,0:T(8,128)(2,1)S(1)} %get-tuple-element.46), channel_id=1, source_target_pairs={{0,4},{4,0},{8,12},{12,8},{1,5},{5,1},{9,13},{13,9},{2,6},{6,2},{1... | collective-permute-start | bytes 294920 | tf_op jit(solution)/shard_map/ppermute | solution.py:177
  16.8 17.7 %collective-permute-start.4 = (bf16[384,128]{1,0:T(8,128)(2,1)S(1)}, bf16[384,128]{1,0:T(8,128)(2,1)S(1)}, u32[]{:S(2)}, u32[]{:S(2)}) collective-permute-start(bf16[384,128]{1,0:T(8,128)(2,1)S(1)} %get-tuple-element.47), channel_id=1, source_target_pairs={{0,8},{4,12},{8,0},{12,4},{1,9},{5,13},{9,1},{13,5},{2,10},{6,14},... | collective-permute-start | bytes 294920 | tf_op jit(solution)/shard_map/ppermute | solution.py:177
  20.3 14.2 %collective-permute-start.5 = (bf16[384,128]{1,0:T(8,128)(2,1)S(1)}, bf16[384,128]{1,0:T(8,128)(2,1)S(1)}, u32[]{:S(2)}, u32[]{:S(2)}) collective-permute-start(bf16[384,128]{1,0:T(8,128)(2,1)S(1)} %get-tuple-element.48), channel_id=1, source_target_pairs={{0,12},{4,8},{8,4},{12,0},{1,13},{5,9},{9,5},{13,1},{2,14},{6,10},... | collective-permute-start | bytes 294920 | tf_op jit(solution)/shard_map/ppermute | solution.py:177
  24.5 30.0 %copy-start.1 = (bf16[2048,1024]{1,0:T(8,128)(2,1)S(1)}, bf16[2048,1024]{1,0:T(8,128)(2,1)}, u32[]{:S(2)}) copy-start(bf16[2048,1024]{1,0:T(8,128)(2,1)} %down.1) | copy-start | bytes 12582916
  24.5 13.3 %collective-permute-start.8 = (bf16[32,1152]{1,0:T(8,128)(2,1)S(1)}, bf16[32,1152]{1,0:T(8,128)(2,1)S(1)}, u32[]{:S(2)}, u32[]{:S(2)}) collective-permute-start(bf16[32,1152]{1,0:T(8,128)(2,1)S(1)} %shard_map.159.refs_0_), channel_id=1, source_target_pairs={{0,12},{4,8},{8,4},{12,0},{1,13},{5,9},{9,5},{13,1},{2,14},{6,10},... | collective-permute-start | bytes 221192 | tf_op jit(solution)/shard_map/ppermute | solution.py:177
  30.4 7.4 %collective-permute-start.7 = (bf16[32,1152]{1,0:T(8,128)(2,1)S(1)}, bf16[32,1152]{1,0:T(8,128)(2,1)S(1)}, u32[]{:S(2)}, u32[]{:S(2)}) collective-permute-start(bf16[32,1152]{1,0:T(8,128)(2,1)S(1)} %shard_map.159.refs_0_), channel_id=1, source_target_pairs={{0,8},{4,12},{8,0},{12,4},{1,9},{5,13},{9,1},{13,5},{2,10},{6,14},... | collective-permute-start | bytes 221192 | tf_op jit(solution)/shard_map/ppermute | solution.py:177
  34.4 4.4 %collective-permute-start.6 = (bf16[32,1152]{1,0:T(8,128)(2,1)S(1)}, bf16[32,1152]{1,0:T(8,128)(2,1)S(1)}, u32[]{:S(2)}, u32[]{:S(2)}) collective-permute-start(bf16[32,1152]{1,0:T(8,128)(2,1)S(1)} %shard_map.159.refs_0_), channel_id=1, source_target_pairs={{0,4},{4,0},{8,12},{12,8},{1,5},{5,1},{9,13},{13,9},{2,6},{6,2},{1... | collective-permute-start | bytes 221192 | tf_op jit(solution)/shard_map/ppermute | solution.py:177
  38.8 17.1 %collective-permute-start.11 = (bf16[512,256]{1,0:T(8,128)(2,1)S(1)}, bf16[512,256]{1,0:T(8,128)(2,1)S(1)}, u32[]{:S(2)}, u32[]{:S(2)}) collective-permute-start(bf16[512,256]{1,0:T(8,128)(2,1)S(1)} %get-tuple-element.61), channel_id=1, source_target_pairs={{0,12},{4,8},{8,4},{12,0},{1,13},{5,9},{9,5},{13,1},{2,14},{6,10},... | collective-permute-start | bytes 786440 | tf_op jit(solution)/shard_map/ppermute | solution.py:177
  41.5 20.0 %collective-permute-start.10 = (bf16[512,256]{1,0:T(8,128)(2,1)S(1)}, bf16[512,256]{1,0:T(8,128)(2,1)S(1)}, u32[]{:S(2)}, u32[]{:S(2)}) collective-permute-start(bf16[512,256]{1,0:T(8,128)(2,1)S(1)} %get-tuple-element.59), channel_id=1, source_target_pairs={{0,8},{4,12},{8,0},{12,4},{1,9},{5,13},{9,1},{13,5},{2,10},{6,14},... | collective-permute-start | bytes 786440 | tf_op jit(solution)/shard_map/ppermute | solution.py:177
  41.5 20.0 %collective-permute-start.9 = (bf16[512,256]{1,0:T(8,128)(2,1)S(1)}, bf16[512,256]{1,0:T(8,128)(2,1)S(1)}, u32[]{:S(2)}, u32[]{:S(2)}) collective-permute-start(bf16[512,256]{1,0:T(8,128)(2,1)S(1)} %get-tuple-element.57), channel_id=1, source_target_pairs={{0,4},{4,0},{8,12},{12,8},{1,5},{5,1},{9,13},{13,9},{2,6},{6,2},{1... | collective-permute-start | bytes 786440 | tf_op jit(solution)/shard_map/ppermute | solution.py:177
  49.2 5.3 %collective-permute-start.12 = (bf16[5,32,512]{2,1,0:T(8,128)(2,1)S(1)}, bf16[5,32,512]{2,1,0:T(8,128)(2,1)S(1)}, u32[]{:S(2)}, u32[]{:S(2)}) collective-permute-start(bf16[5,32,512]{2,1,0:T(8,128)(2,1)S(1)} %get-tuple-element.64), channel_id=1, source_target_pairs={{0,2},{2,0},{1,3},{3,1},{4,6},{6,4},{5,7},{7,5},{8,10},{10,8},{9,1... | collective-permute-start | bytes 491528 | tf_op jit(solution)/shard_map/ppermute | solution.py:558
  63.8 4.7 %collective-permute-start.13 = (bf16[160,256]{1,0:T(8,128)(2,1)S(1)}, bf16[160,256]{1,0:T(8,128)(2,1)S(1)}, u32[]{:S(2)}, u32[]{:S(2)}) collective-permute-start(bf16[160,256]{1,0:T(8,128)(2,1)S(1)} %get-tuple-element.70), channel_id=1, source_target_pairs={{0,4},{4,0},{8,12},{12,8},{1,5},{5,1},{9,13},{13,9},{2,6},{6,2},{1... | collective-permute-start | bytes 245768 | tf_op jit(solution)/shard_map/ppermute | solution.py:177
  63.9 7.1 %collective-permute-start.14 = (bf16[160,256]{1,0:T(8,128)(2,1)S(1)}, bf16[160,256]{1,0:T(8,128)(2,1)S(1)}, u32[]{:S(2)}, u32[]{:S(2)}) collective-permute-start(bf16[160,256]{1,0:T(8,128)(2,1)S(1)} %get-tuple-element.71), channel_id=1, source_target_pairs={{0,8},{4,12},{8,0},{12,4},{1,9},{5,13},{9,1},{13,5},{2,10},{6,14},... | collective-permute-start | bytes 245768 | tf_op jit(solution)/shard_map/ppermute | solution.py:177
  66.5 6.3 %collective-permute-start.15 = (bf16[160,256]{1,0:T(8,128)(2,1)S(1)}, bf16[160,256]{1,0:T(8,128)(2,1)S(1)}, u32[]{:S(2)}, u32[]{:S(2)}) collective-permute-start(bf16[160,256]{1,0:T(8,128)(2,1)S(1)} %get-tuple-element.72), channel_id=1, source_target_pairs={{0,12},{4,8},{8,4},{12,0},{1,13},{5,9},{9,5},{13,1},{2,14},{6,10},... | collective-permute-start | bytes 245768 | tf_op jit(solution)/shard_map/ppermute | solution.py:177
  (2 other events, 1.9 us)

commit v4 on v3

--- a/solution.py
+++ b/solution.py
@@ -184,32 +184,46 @@
 
 
 def pack_kernel(n, first, widths, audio_count, kept, q, k, v, *refs):
+    count = n * len(widths)
     audio, refs = refs[:audio_count], refs[audio_count:]
-    keep, outs, sem = refs[:kept], refs[kept:-1], refs[-1]
+    keep, refs = refs[:kept], refs[kept:]
+    outs, passed, refs = refs[:count], refs[count : count + kept], refs[count + kept :]
+    built = refs[:count] if audio else outs
+    lines, sem, audio_sem, out_sem = refs[-3 - audio_count : -3], refs[-3], refs[-2], refs[-1]
     me = lax.axis_index("seq")
     tokens = q.shape[0]
     group = q.shape[1] // n
-    copies = []
+    fetches = [pltpu.make_async_copy(ref, to, audio_sem.at[i]) for i, (ref, to) in enumerate(zip(audio, lines))]
+    for copy in fetches:
+        copy.start()
+    copies, arrivals = [], []
     for c, width in enumerate(widths):
         for s in range(n):
-            dest = lax.bitwise_xor(me, s)
-            at = pl.ds(pl.multiple_of(dest * group + first, LANES), width)
+            at = pl.ds(pl.multiple_of(lax.bitwise_xor(me, s) * group + first, LANES), width)
             for i, ref in enumerate((q, k, v)):
-                to = outs[c * n + s].at[pl.ds(i * tokens, tokens), :]
-                copies.append(pltpu.make_async_copy(ref.at[:, at], to, sem.at[len(copies)]))
-                copies[-1].start()
+                to = built[c * n + s].at[pl.ds(i * tokens, tokens), :]
+                arrivals.append(pltpu.make_async_copy(ref.at[:, at], to, sem.at[len(arrivals)]))
+                arrivals[-1].start()
         first += width
-    for ref, to in zip(keep, outs[n * len(widths) :]):
-        copies.append(pltpu.make_async_copy(ref, to, sem.at[len(copies)]))
+    for i, (ref, to) in enumerate(zip(keep, passed)):
+        copies.append(pltpu.make_async_copy(ref, to, out_sem.at[count + i]))
         copies[-1].start()
     if audio:
-        half = audio[0].shape[1]
+        for copy in fetches:
+            copy.wait()
+        half = lines[0].shape[1]
         mine = pl.ds(pl.multiple_of(lax.axis_index("tp") * half, LANES), half)
-        parts = [ref[...].astype(F32) for ref in audio[:3]] + [audio[3][:, mine].astype(F32)]
+        parts = [ref[...].astype(F32) for ref in lines[:3]] + [lines[3][:, mine].astype(F32)]
         blocks = [part[:, c : c + widths[0]] for part in parts for c in range(0, half, widths[0])]
         extra = jnp.concatenate(blocks, axis=0).astype(BF16)
         for s in range(n):
-            outs[s][3 * tokens :, :] = extra
+            built[s][3 * tokens :, :] = extra
+    for i in range(count):
+        for copy in arrivals[3 * i : 3 * i + 3]:
+            copy.wait()
+        if audio:
+            copies.append(pltpu.make_async_copy(built[i], outs[i], out_sem.at[i]))
+            copies[-1].start()
     for copy in copies:
         copy.wait()
 
@@ -217,14 +231,17 @@
 def pack(video, audio, keep, n, first, widths, limit, moved):
     tokens = video[0].shape[0]
     extra = 4 * audio[0].size // widths[0] if audio else 0
-    shapes = [sds((3 * tokens + extra, w)) for w in widths for _ in range(n)]
+    shapes = [(3 * tokens + extra, w) for w in widths for _ in range(n)]
     stay = pl.BlockSpec(memory_space=pl.ANY)
+    dma = pltpu.SemaphoreType.DMA
     return pl.pallas_call(
         functools.partial(pack_kernel, n, first, widths, len(audio), len(keep)),
-        out_shape=tuple(shapes) + tuple(sds(x.shape) for x in keep),
-        in_specs=[stay] * 3 + [whole()] * len(audio) + [stay] * len(keep),
-        out_specs=(whole(),) * (len(shapes) + len(keep)),
-        scratch_shapes=[pltpu.SemaphoreType.DMA((3 * len(shapes) + len(keep),))],
+        out_shape=tuple(sds(x) for x in shapes) + tuple(sds(x.shape) for x in keep),
+        in_specs=[stay] * (3 + len(audio) + len(keep)),
+        out_specs=(stay if audio else whole(),) * (len(shapes) + len(keep)),
+        scratch_shapes=[pltpu.VMEM(x, BF16) for x in shapes if audio]
+        + [pltpu.VMEM(x.shape, BF16) for x in audio]
+        + [dma((3 * len(shapes),)), dma((max(len(audio), 1),)), dma((len(shapes) + len(keep),))],
         compiler_params=pltpu.CompilerParams(vmem_limit_bytes=limit * MIB),
         cost_estimate=pl.CostEstimate(flops=0, bytes_accessed=moved, transcendentals=0),
     )(*video, *audio, *keep)
@@ -306,8 +323,8 @@
 
 
 def unpack_kernel(n, heads, tokens, *refs):
-    middles, lasts, own = refs[:n], refs[n : 2 * n], refs[2 * n]
-    out, mlp, sem = refs[2 * n + 1 :]
+    middles, lasts, own = refs[:n], refs[n : 2 * n][::-1], refs[2 * n]
+    out, mlp, line, sem = refs[2 * n + 1 :]
     me = lax.axis_index("seq")
     width = lasts[0].shape[1]
     group = heads * VHEAD
@@ -331,7 +348,9 @@
         total = own[:, c * width : (c + 1) * width]
         for tail in tails:
             total = total + tail[c * rows : (c + 1) * rows]
-        mlp[:, c * width : (c + 1) * width] = total.astype(BF16)
+        line[:, c * width : (c + 1) * width] = total.astype(BF16)
+    copies.append(pltpu.make_async_copy(line, mlp, sem.at[len(copies)]))
+    copies[-1].start()
     for copy in copies:
         copy.wait()
 
@@ -342,10 +361,10 @@
         functools.partial(unpack_kernel, n, heads, tokens),
         out_shape=(sds((tokens, n * heads * VHEAD)), sds(own.shape)),
         in_specs=[pl.BlockSpec(memory_space=pltpu.VMEM)] * (2 * n + 1),
-        out_specs=(pl.BlockSpec(memory_space=pl.ANY), whole()),
-        scratch_shapes=[pltpu.SemaphoreType.DMA((count,))],
+        out_specs=(pl.BlockSpec(memory_space=pl.ANY),) * 2,
+        scratch_shapes=[pltpu.VMEM(own.shape, BF16), pltpu.SemaphoreType.DMA((count + 1,))],
         compiler_params=pltpu.CompilerParams(vmem_limit_bytes=16 * MIB),
-    )(*middles, *lasts, own)
+    )(*middles, *lasts[::-1], own)
 
 
 def low_half(shape):
@@ -353,7 +372,7 @@
 
 
 def listen_kernel(n, tokens, rows, *refs):
-    pieces, keys, values, out = refs[:n], refs[n], refs[n + 1], refs[n + 2]
+    pieces, keys, values, out = refs[:n][::-1], refs[n], refs[n + 1], refs[n + 2]
     columns = keys.shape[1]
     pairs = columns // LANES
     tails = [p[3 * tokens :, :].astype(F32) for p in pieces]
@@ -361,7 +380,8 @@
     scale = LOG2E / math.sqrt(CHEAD)
     low = low_half((count, LANES))
     lane = lax.broadcasted_iota(jnp.int32, (count, LANES), 1)
-    stats = jnp.zeros((count, LANES), F32)
+    peaks = jnp.zeros((count, LANES), F32)
+    totals = jnp.zeros((count, LANES), F32)
     heads = columns // CHEAD
     for pair in range(pairs):
         cols = slice(pair * LANES, (pair + 1) * LANES)
@@ -375,46 +395,107 @@
         o = jnp.dot(w.astype(BF16), values[:, cols], preferred_element_type=F32) / total
         out[:, cols] = jnp.where(low, o[:count], o[count:]).astype(BF16)
         for i in range(2):
-            head = 2 * pair + i
-            sel = slice(i * count, (i + 1) * count)
-            for j, part in enumerate(parts3(peak[sel]) + parts3(total[sel])):
-                stats = jnp.where(lane == j * heads + head, part, stats)
-    out[:, columns:] = stats.astype(BF16)
-
-
-def combine_kernel(n, tokens, rows, *refs):
-    got, pieces = refs[:n], refs[n : 2 * n]
-    gain, up = refs[2 * n], refs[2 * n + 1]
-    own_sum, sent_sum, seen, x_ref = refs[2 * n + 2 :]
+            head = lane == 2 * pair + i
+            peaks = jnp.where(head, peak[i * count : (i + 1) * count], peaks)
+            totals = jnp.where(head, total[i * count : (i + 1) * count], totals)
+    out[:, columns:] = share_stats(peaks[:, :heads], totals[:, :heads])
+
+
+def read_shares(wholes, columns):
+    heads = columns // CHEAD
+    peaks, totals, parts = [], [], []
+    for whole in wholes:
+        parts.append(whole[:, :columns])
+        piece = [whole[:, columns + j * heads : columns + (j + 1) * heads] for j in range(6)]
+        peaks.append(piece[0] + piece[1] + piece[2])
+        totals.append(piece[3] + piece[4] + piece[5])
+    top = functools.reduce(jnp.maximum, peaks)
+    weight = [t * jnp.exp2(p - top) for t, p in zip(totals, peaks)]
+    every = functools.reduce(jnp.add, weight)
+    return parts, [w / every for w in weight], top, every
+
+
+def reorder(whole, order, n):
+    rows = whole.shape[0] // n
+    return jnp.concatenate([whole[(i ^ order) * rows :][:rows] for i in range(n)], axis=0)
+
+
+def joint(parts, weight, pair):
+    low = low_half((parts[0].shape[0], LANES))
+    o = jnp.zeros(low.shape, F32)
+    for w, part in zip(weight, parts):
+        a, b = w[:, 2 * pair : 2 * pair + 1], w[:, 2 * pair + 1 : 2 * pair + 2]
+        o = o + jnp.where(low, a, b) * part[:, pair * LANES : (pair + 1) * LANES]
+    return o.astype(BF16)
+
+
+def share_stats(peaks, totals):
+    stats = jnp.concatenate(parts3(peaks) + parts3(totals), axis=1)
+    rest = jnp.zeros((stats.shape[0], LANES - stats.shape[1]), F32)
+    return jnp.concatenate([stats, rest], axis=1).astype(BF16)
+
+
+def merge_kernel(n, order, own, other, out):
+    columns = out.shape[1] - LANES
+    wholes = own[...].astype(F32), reorder(other[...].astype(F32), order, n)
+    parts, weight, top, every = read_shares(wholes, columns)
+    for pair in range(columns // LANES):
+        out[:, pair * LANES : (pair + 1) * LANES] = joint(parts, weight, pair)
+    out[:, columns:] = share_stats(top, every)
+
+
+def append_kernel(n, orders, piece, *refs):
+    shares, out, sem = refs[:-2], refs[-2], refs[-1]
+    count = shares[0].shape[0]
+    columns = shares[0].shape[1] - LANES
+    width = out.shape[1]
+    base = piece.shape[0]
+    copy = pltpu.make_async_copy(piece, out.at[pl.ds(0, base), :], sem)
+    copy.start()
+    wholes = [reorder(ref[...].astype(F32), order, n) for ref, order in zip(shares, orders)]
+    parts, weight, top, every = read_shares(wholes, columns)
+    blocks = [joint(parts, weight, pair) for pair in range(columns // LANES)]
+    blocks.append(share_stats(top, every))
+    for c, block in enumerate(blocks):
+        at, side = base + c * LANES // width * count, c * LANES % width
+        out[at : at + count, side : side + LANES] = block
+    if len(blocks) * LANES % width:
+        side = len(blocks) * LANES % width
+        out[at : at + count, side:] = jnp.zeros((count, width - side), BF16)
+    copy.wait()
+
+
+def append(n, orders, piece, shares):
+    count, columns = shares[0].shape
+    width = piece.shape[1]
+    tall = piece.shape[0] + -(-columns // width) * count
+    return pl.pallas_call(
+        functools.partial(append_kernel, n, orders),
+        out_shape=sds((tall, width)),
+        in_specs=[pl.BlockSpec(memory_space=pl.ANY)] + [whole()] * len(shares),
+        out_specs=whole(),
+        scratch_shapes=[pltpu.SemaphoreType.DMA],
+        compiler_params=pltpu.CompilerParams(vmem_limit_bytes=16 * MIB),
+    )(piece, *shares)
+
+
+def combine_kernel(n, base, tokens, rows, *refs):
+    got, pieces, (gain, up) = refs[:2], refs[2 : 2 + n], refs[2 + n : 4 + n]
+    own_sum, sent_sum, seen, x_ref = refs[4 + n :]
 
     @pl.when(pl.program_id(0) == 0)
     def _():
         columns = seen.shape[1]
-        heads = columns // CHEAD
-        peaks, totals, parts = [], [], []
-        for s in range(n):
-            whole = got[s][...].astype(F32)
-            if s:
-                whole = jnp.concatenate([whole[(i ^ s) * rows :][:rows] for i in range(n)], axis=0)
-            whole, stats = whole[:, :columns], whole[:, columns:]
-            piece = [stats[:, j * heads : (j + 1) * heads] for j in range(6)]
-            peaks.append(piece[0] + piece[1] + piece[2])
-            totals.append(piece[3] + piece[4] + piece[5])
-            parts.append(whole)
-        top = functools.reduce(jnp.maximum, peaks)
-        weight = [t * jnp.exp2(p - top) for t, p in zip(totals, peaks)]
-        every = functools.reduce(jnp.add, weight)
-        weight = [w / every for w in weight]
+        wholes = []
+        for ref, order in zip(got, (0, 1)):
+            blocks = [ref[at : at + n * rows, :] for at in range(base, ref.shape[0], n * rows)]
+            wholes.append(reorder(jnp.concatenate(blocks, axis=1).astype(F32), order, n))
+        parts, weight, _, _ = read_shares(wholes, columns)
         tails = [p[3 * tokens :, :].astype(F32) for p in pieces]
-        low = low_half((n * rows, LANES))
         square = jnp.zeros((n * rows, 1), F32)
         for pair in range(columns // LANES):
             cols = slice(pair * LANES, (pair + 1) * LANES)
-            o = jnp.zeros((n * rows, LANES), F32)
-            for w, part in zip(weight, parts):
-                a, b = w[:, 2 * pair : 2 * pair + 1], w[:, 2 * pair + 1 : 2 * pair + 2]
-                o = o + jnp.where(low, a, b) * part[:, cols]
-            o = o.astype(BF16)
+            o = joint(parts, weight, pair)
             seen[:, cols] = o[:rows]
             residual = audio_rows(tails, 3, pair, rows, columns // LANES) + o.astype(F32)
             square = square + jnp.sum(residual * residual, axis=1, keepdims=True)
@@ -434,14 +515,14 @@
         sent_sum[0] = product.astype(BF16)
 
 
-def combine(got, pieces, gain, up, tokens, rows, block):
-    n = len(got)
+def combine(got, base, pieces, gain, up, tokens, rows, block):
+    n = len(pieces)
     columns, units = up.shape
     steps = units // block + 1
     held = lambda ref: pl.BlockSpec(ref.shape, lambda i: (0,) * ref.ndim)
     moved = pl.BlockSpec((1, n * rows, block), lambda i: (i, 0, 0))
     return pl.pallas_call(
-        functools.partial(combine_kernel, n, tokens, rows),
+        functools.partial(combine_kernel, n, base, tokens, rows),
         grid=(steps,),
         out_shape=(
             sds((steps, n * rows, block), F32),
@@ -539,13 +620,25 @@
     chunk_1 = send(packed[:n])
     (share,) = call(
         functools.partial(listen_kernel, n, tokens, rows),
-        (*chunk_0, ck, cv),
+        (*chunk_0[::-1], ck, cv),
         [sds((n * rows, columns + LANES))],
         moved=4 * vq.size,
         limit=16,
     )
-    shares = send([share] * n)
-    chunk_2 = send(middle([chunk_0, chunk_1], packed[n:], n, MIB), *shares[1:])
+    order = n // 2
+    while order > 2:
+        (share,) = call(
+            functools.partial(merge_kernel, n, order),
+            (share, trade(share, order)),
+            [sds(share.shape)],
+            limit=16,
+        )
+        order //= 2
+    shares = [share, trade(share, 2)] if n > 2 else [share]
+    built = middle([chunk_0, chunk_1], packed[n:], n, MIB)
+    below = append(n, (0, 2), built[1], shares)
+    chunk_2 = [built[0], trade(below, 1)]
+    chunk_2 += [trade(after(built[s], shares[1]), s) for s in range(2, n)]
     (heard,) = call(
         functools.partial(heard_kernel, n, tokens, rows),
         (cq, *chunk_0),
@@ -554,7 +647,7 @@
         limit=16,
     )
     gain = after(gain.reshape(1, -1), heard)
-    own_sum, sent_sum, seen = combine(shares, chunk_0, gain, up, tokens, rows, 512)
+    own_sum, sent_sum, seen = combine((below, chunk_2[1]), built[1].shape[0], chunk_0, gain, up, tokens, rows, 512)
     other_sum = lax.ppermute(sent_sum, "tp", [(0, 1), (1, 0)])
     results = finish(own_sum, other_sum, down, n, rows, features, 512)
     ends = call(
@@ -580,7 +673,7 @@
         and n * vq.shape[0] <= 1024
         and aq.shape[0] % 8 == 0
         and n * aq.shape[0] <= 64
-        and 6 * (aq.shape[1] // CHEAD) <= LANES
+        and 6 * (aq.shape[1] // CHEAD) < LANES
         and aq.shape[1] % VHEAD == 0
         and up.shape[1] % 512 == 0
         and down.shape[1] % 512 == 0

time: 74.7 us -> 71.4 us (0.956)
  starting transfers between devices: 30.4 us -> 28.5 us
  Pallas kernels: 20 us -> 18.9 us
    ppermute x15 -> x13, starting transfers between devices: 28.9 us -> 27 us  [trade(): return lax.ppermute(value, 'seq', [(i, i ^ by) for i in range(n)])]
    ppermute x15 -> x13, waiting for transfers between devices: 13.3 us -> 13.1 us  [trade(): return lax.ppermute(value, 'seq', [(i, i ^ by) for i in range(n)])]
    pallas_call x1 -> x2, Pallas kernels: 3.29 us -> 3.35 us  [the longest x1 2.89 us: combine(): pl.pallas_call(functools.partial(combine_kernel, n, base, tokens, rows),...]
  transfers between devices with their start and end apart: 16 -> 14, of which waited for: 7 -> 6; matrix products, arithmetic and copies ran while one was open for 0% -> 0% of each run, Pallas kernels for 18% -> 19%
where the time goes in v4:
time: 71.4 us; the launch traced here: 71 us
  starting transfers between devices  28.5 us (40%)
  Pallas kernels  18.9 us (26%)
  waiting for transfers between devices  17 us (24%)
  local copies, waits for them, and re-layouts  5.96 us (8%)
  between operations  0.75 us (1%)
    ppermute x13, starting transfers between devices, trade(): return lax.ppermute(value, 'seq', [(i, i ^ by) for i in range(n)])  27 us
    ppermute x13, waiting for transfers between devices, trade(): return lax.ppermute(value, 'seq', [(i, i ^ by) for i in range(n)])  13.1 us
    pallas_call x3, Pallas kernels, call(): pl.pallas_call(kernel, out_shape=tuple(outs), in_specs=[whole()] * len(in...  7.05 us
    unnamed x20, local copies, waits for them, and re-layouts  5.96 us
    ppermute x1, waiting for transfers between devices, short_body(): other_sum = lax.ppermute(sent_sum, 'tp', [(0, 1), (1, 0)])  3.84 us
    pallas_call x1, Pallas kernels, middle(): pl.pallas_call(functools.partial(middle_kernel, n, counts), out_shape=(sd...  3.3 us
    pallas_call x2, Pallas kernels, pack(): pl.pallas_call(functools.partial(pack_kernel, n, first, widths, len(audio...  2.91 us
    pallas_call x1, Pallas kernels, combine(): pl.pallas_call(functools.partial(combine_kernel, n, base, tokens, rows),...  2.89 us
  transfers between devices with their start and end apart: 14, of which 6 were waited for; matrix products, arithmetic and copies ran while one was open for 0% of the time, Pallas kernels for 19%

profile of v4, /device:TPU:0, one launch (start us, length us, event | category | flops | bytes accessed | tf_op | source)
XLA Modules:
  0.0 71.0 jit_solution(5383592183690596524)
XLA Ops:
  0.7 2.0 %shard_map.156 = (bf16[640,128]{1,0:T(8,128)(2,1)}, bf16[640,128]{1,0:T(8,128)(2,1)}, bf16[640,128]{1,0:T(8,128)(2,1)}, bf16[640,128]{1,0:T(8,128)(2,1)}) custom-call(bf16[128,2048]{1,0:T(8,128)(2,1)} %bitcast.15, bf16[128,2048]{1,0:T(8,128)(2,1)} %bitcast.17, bf16[128,2048]{1,0:T(8,128)(2,1)} %bitcast.19, bf16[8,1024]{1,0:T(8,128)(2,1)} %bitcast.27, ...), custom_call_target="tpu_custom_call" | custom-call | bytes 1572864 | tf_op jit(solution)/shard_map/pallas_call | solution.py:237
  2.7 3.1 %collective-permute-start = (bf16[640,128]{1,0:T(8,128)(2,1)}, bf16[640,128]{1,0:T(8,128)(2,1)S(1)}, u32[]{:S(2)}, u32[]{:S(2)}) collective-permute-start(bf16[640,128]{1,0:T(8,128)(2,1)} %get-tuple-element.41), channel_id=1, source_target_pairs={{0,4},{4,0},{8,12},{12,8},{1,5},{5,1},{9,13},{13,9},{2,6},{6,2},{1... | collective-permute-start | bytes 491528 | tf_op jit(solution)/shard_map/ppermute | solution.py:177
  5.8 2.6 %collective-permute-start.1 = (bf16[640,128]{1,0:T(8,128)(2,1)}, bf16[640,128]{1,0:T(8,128)(2,1)S(1)}, u32[]{:S(2)}, u32[]{:S(2)}) collective-permute-start(bf16[640,128]{1,0:T(8,128)(2,1)} %get-tuple-element.42), channel_id=1, source_target_pairs={{0,8},{4,12},{8,0},{12,4},{1,9},{5,13},{9,1},{13,5},{2,10},{6,14},... | collective-permute-start | bytes 491528 | tf_op jit(solution)/shard_map/ppermute | solution.py:177
  8.4 1.0 %copy-done.2 = bf16[1,128,2048]{2,1,0:T(8,128)(2,1)S(1)} copy-done((bf16[1,128,2048]{2,1,0:T(8,128)(2,1)S(1)}, bf16[1,128,2048]{2,1,0:T(8,128)(2,1)}, u32[]{:S(2)}) %copy-start.2) | copy-done | bytes 524312
  9.4 1.0 %copy-done.3 = bf16[1,128,2048]{2,1,0:T(8,128)(2,1)S(1)} copy-done((bf16[1,128,2048]{2,1,0:T(8,128)(2,1)S(1)}, bf16[1,128,2048]{2,1,0:T(8,128)(2,1)}, u32[]{:S(2)}) %copy-start.3) | copy-done | bytes 524312
  10.5 1.0 %copy-done.4 = bf16[1,128,2048]{2,1,0:T(8,128)(2,1)S(1)} copy-done((bf16[1,128,2048]{2,1,0:T(8,128)(2,1)S(1)}, bf16[1,128,2048]{2,1,0:T(8,128)(2,1)}, u32[]{:S(2)}) %copy-start.4) | copy-done | bytes 524312
  16.2 3.5 %collective-permute-start.4 = (bf16[384,128]{1,0:T(8,128)(2,1)S(1)}, bf16[384,128]{1,0:T(8,128)(2,1)S(1)}, u32[]{:S(2)}, u32[]{:S(2)}) collective-permute-start(bf16[384,128]{1,0:T(8,128)(2,1)S(1)} %get-tuple-element.46), channel_id=1, source_target_pairs={{0,8},{4,12},{8,0},{12,4},{1,9},{5,13},{9,1},{13,5},{2,10},{6,14},... | collective-permute-start | bytes 294920 | tf_op jit(solution)/shard_map/ppermute | solution.py:177
  19.7 2.1 %collective-permute-done.1.refs_2_.refs_1_.refs_4_ = bf16[640,128]{1,0:T(8,128)(2,1)S(1)} collective-permute-done((bf16[640,128]{1,0:T(8,128)(2,1)}, bf16[640,128]{1,0:T(8,128)(2,1)S(1)}, u32[]{:S(2)}, u32[]{:S(2)}) %collective-permute-start.1) | collective-permute-done | bytes 163872 | tf_op jit(solution)/shard_map/ppermute | solution.py:177
  21.8 2.0 %shard_map.159.refs_0_ = bf16[32,1152]{1,0:T(8,128)(2,1)S(1)} custom-call(bf16[640,128]{1,0:T(8,128)(2,1)S(1)} %collective-permute-done.2.refs_3_.refs_0_.refs_5_, bf16[640,128]{1,0:T(8,128)(2,1)S(1)} %collective-permute-done.1.refs_2_.refs_1_.refs_4_, bf16[640,128]{1,0:T(8,128)(2,1)S(1)} %collective-permute-done.refs_1_.refs_2_.refs_3_, ...), custom_call_target="tpu_custom_call" | custom-call | bytes 1048576 | tf_op jit(solution)/shard_map/pallas_call | solution.py:165
  23.8 8.5 %collective-permute-start.6 = (bf16[32,1152]{1,0:T(8,128)(2,1)S(1)}, bf16[32,1152]{1,0:T(8,128)(2,1)S(1)}, u32[]{:S(2)}, u32[]{:S(2)}) collective-permute-start(bf16[32,1152]{1,0:T(8,128)(2,1)S(1)} %shard_map.159.refs_0_), channel_id=1, source_target_pairs={{0,8},{4,12},{8,0},{12,4},{1,9},{5,13},{9,1},{13,5},{2,10},{6,14},... | collective-permute-start | bytes 221192 | tf_op jit(solution)/shard_map/ppermute | solution.py:177
  32.3 3.3 %shard_map.158 = (bf16[512,256]{1,0:T(8,128)(2,1)S(1)}, bf16[512,256]{1,0:T(8,128)(2,1)S(1)}, bf16[512,256]{1,0:T(8,128)(2,1)S(1)}, bf16[512,256]{1,0:T(8,128)(2,1)S(1)}) custom-call(bf16[640,128]{1,0:T(8,128)(2,1)S(1)} %get-tuple-element.40.refs_0_.refs_3_.refs_2_, bf16[640,128]{1,0:T(8,128)(2,1)S(1)} %collective-permute-done.refs_1_.refs_2_.refs_3_, ...), custom_call_target="tpu_custom_call" | custom-call | bytes 1048576 | tf_op jit(solution)/shard_map/pallas_call | solution.py:300
  36.1 1.4 %collective-permute-start.7 = (bf16[672,256]{1,0:T(8,128)(2,1)S(1)}, bf16[672,256]{1,0:T(8,128)(2,1)S(1)}, u32[]{:S(2)}, u32[]{:S(2)}) collective-permute-start(bf16[672,256]{1,0:T(8,128)(2,1)S(1)} %shard_map.160.refs_0_), channel_id=1, source_target_pairs={{0,4},{4,0},{8,12},{12,8},{1,5},{5,1},{9,13},{13,9},{2,6},{6,2},{1... | collective-permute-start | bytes 1032200 | tf_op jit(solution)/shard_map/ppermute | solution.py:177
  37.5 2.5 %collective-permute-start.9 = (bf16[512,256]{1,0:T(8,128)(2,1)S(1)}, bf16[512,256]{1,0:T(8,128)(2,1)S(1)}, u32[]{:S(2)}, u32[]{:S(2)}) collective-permute-start(bf16[512,256]{1,0:T(8,128)(2,1)S(1)} %get-tuple-element.59), channel_id=1, source_target_pairs={{0,12},{4,8},{8,4},{12,0},{1,13},{5,9},{9,5},{13,1},{2,14},{6,10},... | collective-permute-start | bytes 786440 | tf_op jit(solution)/shard_map/ppermute | solution.py:177
  40.1 2.8 %shard_map.161 = bf16[128,1024]{1,0:T(8,128)(2,1)} custom-call(bf16[128,1024]{1,0:T(8,128)(2,1)S(1)} %bitcast.23, bf16[640,128]{1,0:T(8,128)(2,1)S(1)} %get-tuple-element.40.refs_0_.refs_3_.refs_2_, bf16[640,128]{1,0:T(8,128)(2,1)S(1)} %collective-permute-done.refs_1_.refs_2_.refs_3_, bf16[640,128]{1,0:T(8,128)(2,1)S(1)} %collective-permute-done.1.refs_2_.refs_1_.refs_4_, ...), custom_call_target="tpu_custom_call" | custom-call | bytes 1048576 | tf_op jit(solution)/shard_map/pallas_call | solution.py:165
  42.8 6.4 %collective-permute-done.7.refs_1_ = bf16[672,256]{1,0:T(8,128)(2,1)S(1)} collective-permute-done((bf16[672,256]{1,0:T(8,128)(2,1)S(1)}, bf16[672,256]{1,0:T(8,128)(2,1)S(1)}, u32[]{:S(2)}, u32[]{:S(2)}) %collective-permute-start.7) | collective-permute-done | bytes 344096 | tf_op jit(solution)/shard_map/ppermute | solution.py:177
  49.2 2.9 %shard_map.162 = (f32[5,32,512]{2,1,0:T(8,128)S(1)}, bf16[5,32,512]{2,1,0:T(8,128)(2,1)S(1)}, bf16[8,1024]{1,0:T(8,128)(2,1)}) custom-call(bf16[672,256]{1,0:T(8,128)(2,1)S(1)} %shard_map.160.refs_0_, bf16[672,256]{1,0:T(8,128)(2,1)S(1)} %collective-permute-done.7.refs_1_, bf16[640,128]{1,0:T(8,128)(2,1)S(1)} %get-tuple-element.40.refs_0_.refs_3_.refs_2_, ...), custom_call_target="tpu_custom_call" | custom-call | tf_op jit(solution)/shard_map/pallas_call | solution.py:524
  52.1 1.5 %collective-permute-start.10 = (bf16[5,32,512]{2,1,0:T(8,128)(2,1)S(1)}, bf16[5,32,512]{2,1,0:T(8,128)(2,1)S(1)}, u32[]{:S(2)}, u32[]{:S(2)}) collective-permute-start(bf16[5,32,512]{2,1,0:T(8,128)(2,1)S(1)} %get-tuple-element.62), channel_id=1, source_target_pairs={{0,2},{2,0},{1,3},{3,1},{4,6},{6,4},{5,7},{7,5},{8,10},{10,8},{9,1... | collective-permute-start | bytes 491528 | tf_op jit(solution)/shard_map/ppermute | solution.py:651
  53.6 3.8 %collective-permute-done.10.other = bf16[5,32,512]{2,1,0:T(8,128)(2,1)S(1)} collective-permute-done((bf16[5,32,512]{2,1,0:T(8,128)(2,1)S(1)}, bf16[5,32,512]{2,1,0:T(8,128)(2,1)S(1)}, u32[]{:S(2)}, u32[]{:S(2)}) %collective-permute-start.10) | collective-permute-done | bytes 163872 | tf_op jit(solution)/shard_map/ppermute | solution.py:651
  57.4 1.4 %shard_map.163 = (f32[8,1024]{1,0:T(8,128)S(1)}, bf16[8,1024]{1,0:T(8,128)(2,1)S(1)}, bf16[8,1024]{1,0:T(8,128)(2,1)S(1)}, bf16[8,1024]{1,0:T(8,128)(2,1)S(1)}) custom-call(f32[5,32,512]{2,1,0:T(8,128)S(1)} %get-tuple-element.61.own, bf16[5,32,512]{2,1,0:T(8,128)(2,1)S(1)} %collective-permute-done.10.other, bf16[2048,1024]{1,0:T(8,128)(2,1)S(1)} %copy-done), custom_call_target="tpu_custom_call" | custom-call | tf_op jit(solution)/shard_map/pallas_call | solution.py:565
  59.8 2.3 %shard_map.164 = (bf16[160,256]{1,0:T(8,128)(2,1)S(1)}, bf16[160,256]{1,0:T(8,128)(2,1)S(1)}, bf16[160,256]{1,0:T(8,128)(2,1)S(1)}, bf16[160,256]{1,0:T(8,128)(2,1)S(1)}) custom-call(bf16[512,256]{1,0:T(8,128)(2,1)S(1)} %get-tuple-element.52.refs_0_, bf16[672,256]{1,0:T(8,128)(2,1)S(1)} %collective-permute-done.7.refs_1_, ...), custom_call_target="tpu_custom_call" | custom-call | tf_op jit(solution)/shard_map/pallas_call | solution.py:165
  62.1 2.5 %collective-permute-start.11 = (bf16[160,256]{1,0:T(8,128)(2,1)S(1)}, bf16[160,256]{1,0:T(8,128)(2,1)S(1)}, u32[]{:S(2)}, u32[]{:S(2)}) collective-permute-start(bf16[160,256]{1,0:T(8,128)(2,1)S(1)} %get-tuple-element.67), channel_id=1, source_target_pairs={{0,12},{4,8},{8,4},{12,0},{1,13},{5,9},{9,5},{13,1},{2,14},{6,10},... | collective-permute-start | bytes 245768 | tf_op jit(solution)/shard_map/ppermute | solution.py:177
  64.6 2.0 %collective-permute-start.13 = (bf16[160,256]{1,0:T(8,128)(2,1)S(1)}, bf16[160,256]{1,0:T(8,128)(2,1)S(1)}, u32[]{:S(2)}, u32[]{:S(2)}) collective-permute-start(bf16[160,256]{1,0:T(8,128)(2,1)S(1)} %get-tuple-element.69), channel_id=1, source_target_pairs={{0,4},{4,0},{8,12},{12,8},{1,5},{5,1},{9,13},{13,9},{2,6},{6,2},{1... | collective-permute-start | bytes 245768 | tf_op jit(solution)/shard_map/ppermute | solution.py:177
  66.6 1.9 %collective-permute-done.11.refs_4_ = bf16[160,256]{1,0:T(8,128)(2,1)S(1)} collective-permute-done((bf16[160,256]{1,0:T(8,128)(2,1)S(1)}, bf16[160,256]{1,0:T(8,128)(2,1)S(1)}, u32[]{:S(2)}, u32[]{:S(2)}) %collective-permute-start.11) | collective-permute-done | bytes 81952 | tf_op jit(solution)/shard_map/ppermute | solution.py:177
  68.4 1.7 %collective-permute-done.12.refs_5_ = bf16[160,256]{1,0:T(8,128)(2,1)S(1)} collective-permute-done((bf16[160,256]{1,0:T(8,128)(2,1)S(1)}, bf16[160,256]{1,0:T(8,128)(2,1)S(1)}, u32[]{:S(2)}, u32[]{:S(2)}) %collective-permute-start.12) | collective-permute-done | bytes 81952 | tf_op jit(solution)/shard_map/ppermute | solution.py:177
  (34 shorter events, 7.0 us)
Async XLA Ops:
  0.6 39.4 %copy-start.7 = (bf16[1,128,1024]{2,1,0:T(8,128)(2,1)S(1)}, bf16[1,128,1024]{2,1,0:T(8,128)(2,1)}, u32[]{:S(2)}) copy-start(bf16[1,128,1024]{2,1,0:T(8,128)(2,1)} %param.16) | copy-start | bytes 786436
  0.6 48.6 %copy-start.9 = (f32[2048]{0:T(1024)S(1)}, f32[2048]{0:T(1024)}, u32[]{:S(2)}) copy-start(f32[2048]{0:T(1024)} %param.23) | copy-start | bytes 24580
  2.7 46.5 %copy-start.1 = (bf16[1024,2048]{1,0:T(8,128)(2,1)S(1)}, bf16[1024,2048]{1,0:T(8,128)(2,1)}, u32[]{:S(2)}) copy-start(bf16[1024,2048]{1,0:T(8,128)(2,1)} %refs_7_.1) | copy-start | bytes 12582916
  2.7 17.0 %collective-permute-start = (bf16[640,128]{1,0:T(8,128)(2,1)}, bf16[640,128]{1,0:T(8,128)(2,1)S(1)}, u32[]{:S(2)}, u32[]{:S(2)}) collective-permute-start(bf16[640,128]{1,0:T(8,128)(2,1)} %get-tuple-element.41), channel_id=1, source_target_pairs={{0,4},{4,0},{8,12},{12,8},{1,5},{5,1},{9,13},{13,9},{2,6},{6,2},{1... | collective-permute-start | bytes 491528 | tf_op jit(solution)/shard_map/ppermute | solution.py:177
  5.8 16.0 %collective-permute-start.1 = (bf16[640,128]{1,0:T(8,128)(2,1)}, bf16[640,128]{1,0:T(8,128)(2,1)S(1)}, u32[]{:S(2)}, u32[]{:S(2)}) collective-permute-start(bf16[640,128]{1,0:T(8,128)(2,1)} %get-tuple-element.42), channel_id=1, source_target_pairs={{0,8},{4,12},{8,0},{12,4},{1,9},{5,13},{9,1},{13,5},{2,10},{6,14},... | collective-permute-start | bytes 491528 | tf_op jit(solution)/shard_map/ppermute | solution.py:177
  8.4 13.4 %collective-permute-start.2 = (bf16[640,128]{1,0:T(8,128)(2,1)}, bf16[640,128]{1,0:T(8,128)(2,1)S(1)}, u32[]{:S(2)}, u32[]{:S(2)}) collective-permute-start(bf16[640,128]{1,0:T(8,128)(2,1)} %get-tuple-element.43), channel_id=1, source_target_pairs={{0,12},{4,8},{8,4},{12,0},{1,13},{5,9},{9,5},{13,1},{2,14},{6,10},... | collective-permute-start | bytes 491528 | tf_op jit(solution)/shard_map/ppermute | solution.py:177
  8.4 1.0 %copy-start.2 = (bf16[1,128,2048]{2,1,0:T(8,128)(2,1)S(1)}, bf16[1,128,2048]{2,1,0:T(8,128)(2,1)}, u32[]{:S(2)}) copy-start(bf16[1,128,2048]{2,1,0:T(8,128)(2,1)} %param.13) | copy-start | bytes 1572868
  9.4 1.0 %copy-start.3 = (bf16[1,128,2048]{2,1,0:T(8,128)(2,1)S(1)}, bf16[1,128,2048]{2,1,0:T(8,128)(2,1)}, u32[]{:S(2)}) copy-start(bf16[1,128,2048]{2,1,0:T(8,128)(2,1)} %param.14) | copy-start | bytes 1572868
  10.5 1.0 %copy-start.4 = (bf16[1,128,2048]{2,1,0:T(8,128)(2,1)S(1)}, bf16[1,128,2048]{2,1,0:T(8,128)(2,1)}, u32[]{:S(2)}) copy-start(bf16[1,128,2048]{2,1,0:T(8,128)(2,1)} %param.15) | copy-start | bytes 1572868
  11.5 0.9 %copy-start.5 = (bf16[1,128,1024]{2,1,0:T(8,128)(2,1)S(1)}, bf16[1,128,1024]{2,1,0:T(8,128)(2,1)}, u32[]{:S(2)}) copy-start(bf16[1,128,1024]{2,1,0:T(8,128)(2,1)} %param.20) | copy-start | bytes 786436
  12.5 0.9 %copy-start.6 = (bf16[1,128,1024]{2,1,0:T(8,128)(2,1)S(1)}, bf16[1,128,1024]{2,1,0:T(8,128)(2,1)}, u32[]{:S(2)}) copy-start(bf16[1,128,1024]{2,1,0:T(8,128)(2,1)} %param.21) | copy-start | bytes 786436
  13.4 0.9 %copy-start.8 = (bf16[640,128]{1,0:T(8,128)(2,1)S(1)}, bf16[640,128]{1,0:T(8,128)(2,1)}, u32[]{:S(2)}) copy-start(bf16[640,128]{1,0:T(8,128)(2,1)} %get-tuple-element.39.refs_0_) | copy-start | bytes 491524
  15.2 17.1 %collective-permute-start.3 = (bf16[384,128]{1,0:T(8,128)(2,1)S(1)}, bf16[384,128]{1,0:T(8,128)(2,1)S(1)}, u32[]{:S(2)}, u32[]{:S(2)}) collective-permute-start(bf16[384,128]{1,0:T(8,128)(2,1)S(1)} %get-tuple-element.45), channel_id=1, source_target_pairs={{0,4},{4,0},{8,12},{12,8},{1,5},{5,1},{9,13},{13,9},{2,6},{6,2},{1... | collective-permute-start | bytes 294920 | tf_op jit(solution)/shard_map/ppermute | solution.py:177
  16.2 16.2 %collective-permute-start.4 = (bf16[384,128]{1,0:T(8,128)(2,1)S(1)}, bf16[384,128]{1,0:T(8,128)(2,1)S(1)}, u32[]{:S(2)}, u32[]{:S(2)}) collective-permute-start(bf16[384,128]{1,0:T(8,128)(2,1)S(1)} %get-tuple-element.46), channel_id=1, source_target_pairs={{0,8},{4,12},{8,0},{12,4},{1,9},{5,13},{9,1},{13,5},{2,10},{6,14},... | collective-permute-start | bytes 294920 | tf_op jit(solution)/shard_map/ppermute | solution.py:177
  19.7 12.7 %collective-permute-start.5 = (bf16[384,128]{1,0:T(8,128)(2,1)S(1)}, bf16[384,128]{1,0:T(8,128)(2,1)S(1)}, u32[]{:S(2)}, u32[]{:S(2)}) collective-permute-start(bf16[384,128]{1,0:T(8,128)(2,1)S(1)} %get-tuple-element.47), channel_id=1, source_target_pairs={{0,12},{4,8},{8,4},{12,0},{1,13},{5,9},{9,5},{13,1},{2,14},{6,10},... | collective-permute-start | bytes 294920 | tf_op jit(solution)/shard_map/ppermute | solution.py:177
  23.8 11.8 %collective-permute-start.6 = (bf16[32,1152]{1,0:T(8,128)(2,1)S(1)}, bf16[32,1152]{1,0:T(8,128)(2,1)S(1)}, u32[]{:S(2)}, u32[]{:S(2)}) collective-permute-start(bf16[32,1152]{1,0:T(8,128)(2,1)S(1)} %shard_map.159.refs_0_), channel_id=1, source_target_pairs={{0,8},{4,12},{8,0},{12,4},{1,9},{5,13},{9,1},{13,5},{2,10},{6,14},... | collective-permute-start | bytes 221192 | tf_op jit(solution)/shard_map/ppermute | solution.py:177
  35.6 21.8 %copy-start = (bf16[2048,1024]{1,0:T(8,128)(2,1)S(1)}, bf16[2048,1024]{1,0:T(8,128)(2,1)}, u32[]{:S(2)}) copy-start(bf16[2048,1024]{1,0:T(8,128)(2,1)} %down.1) | copy-start | bytes 12582916
  36.1 13.1 %collective-permute-start.7 = (bf16[672,256]{1,0:T(8,128)(2,1)S(1)}, bf16[672,256]{1,0:T(8,128)(2,1)S(1)}, u32[]{:S(2)}, u32[]{:S(2)}) collective-permute-start(bf16[672,256]{1,0:T(8,128)(2,1)S(1)} %shard_map.160.refs_0_), channel_id=1, source_target_pairs={{0,4},{4,0},{8,12},{12,8},{1,5},{5,1},{9,13},{13,9},{2,6},{6,2},{1... | collective-permute-start | bytes 1032200 | tf_op jit(solution)/shard_map/ppermute | solution.py:177
  37.5 21.3 %collective-permute-start.9 = (bf16[512,256]{1,0:T(8,128)(2,1)S(1)}, bf16[512,256]{1,0:T(8,128)(2,1)S(1)}, u32[]{:S(2)}, u32[]{:S(2)}) collective-permute-start(bf16[512,256]{1,0:T(8,128)(2,1)S(1)} %get-tuple-element.59), channel_id=1, source_target_pairs={{0,12},{4,8},{8,4},{12,0},{1,13},{5,9},{9,5},{13,1},{2,14},{6,10},... | collective-permute-start | bytes 786440 | tf_op jit(solution)/shard_map/ppermute | solution.py:177
  40.1 19.8 %collective-permute-start.8 = (bf16[512,256]{1,0:T(8,128)(2,1)S(1)}, bf16[512,256]{1,0:T(8,128)(2,1)S(1)}, u32[]{:S(2)}, u32[]{:S(2)}) collective-permute-start(bf16[512,256]{1,0:T(8,128)(2,1)S(1)} %get-tuple-element.57), channel_id=1, source_target_pairs={{0,8},{4,12},{8,0},{12,4},{1,9},{5,13},{9,1},{13,5},{2,10},{6,14},... | collective-permute-start | bytes 786440 | tf_op jit(solution)/shard_map/ppermute | solution.py:177
  52.1 5.3 %collective-permute-start.10 = (bf16[5,32,512]{2,1,0:T(8,128)(2,1)S(1)}, bf16[5,32,512]{2,1,0:T(8,128)(2,1)S(1)}, u32[]{:S(2)}, u32[]{:S(2)}) collective-permute-start(bf16[5,32,512]{2,1,0:T(8,128)(2,1)S(1)} %get-tuple-element.62), channel_id=1, source_target_pairs={{0,2},{2,0},{1,3},{3,1},{4,6},{6,4},{5,7},{7,5},{8,10},{10,8},{9,1... | collective-permute-start | bytes 491528 | tf_op jit(solution)/shard_map/ppermute | solution.py:651
  62.1 6.3 %collective-permute-start.11 = (bf16[160,256]{1,0:T(8,128)(2,1)S(1)}, bf16[160,256]{1,0:T(8,128)(2,1)S(1)}, u32[]{:S(2)}, u32[]{:S(2)}) collective-permute-start(bf16[160,256]{1,0:T(8,128)(2,1)S(1)} %get-tuple-element.67), channel_id=1, source_target_pairs={{0,12},{4,8},{8,4},{12,0},{1,13},{5,9},{9,5},{13,1},{2,14},{6,10},... | collective-permute-start | bytes 245768 | tf_op jit(solution)/shard_map/ppermute | solution.py:177
  64.6 5.6 %collective-permute-start.12 = (bf16[160,256]{1,0:T(8,128)(2,1)S(1)}, bf16[160,256]{1,0:T(8,128)(2,1)S(1)}, u32[]{:S(2)}, u32[]{:S(2)}) collective-permute-start(bf16[160,256]{1,0:T(8,128)(2,1)S(1)} %get-tuple-element.68), channel_id=1, source_target_pairs={{0,8},{4,12},{8,0},{12,4},{1,9},{5,13},{9,1},{13,5},{2,10},{6,14},... | collective-permute-start | bytes 245768 | tf_op jit(solution)/shard_map/ppermute | solution.py:177
  64.6 5.6 %collective-permute-start.13 = (bf16[160,256]{1,0:T(8,128)(2,1)S(1)}, bf16[160,256]{1,0:T(8,128)(2,1)S(1)}, u32[]{:S(2)}, u32[]{:S(2)}) collective-permute-start(bf16[160,256]{1,0:T(8,128)(2,1)S(1)} %get-tuple-element.69), channel_id=1, source_target_pairs={{0,4},{4,0},{8,12},{12,8},{1,5},{5,1},{9,13},{13,9},{2,6},{6,2},{1... | collective-permute-start | bytes 245768 | tf_op jit(solution)/shard_map/ppermute | solution.py:177

commit v5 on v4

--- a/solution.py
+++ b/solution.py
@@ -259,53 +259,58 @@
         cols = slice(h * VHEAD, (h + 1) * VHEAD)
         keys = jnp.concatenate([p[tokens : 2 * tokens, cols] for p in pieces], axis=0)
         values = jnp.concatenate([p[2 * tokens : 3 * tokens, cols] for p in pieces], axis=0)
+        values = jnp.concatenate([values, jnp.ones_like(values)], axis=1)
         for s, p in enumerate(pieces):
-            t = lax.dot_general(p[0:tokens, cols], keys, NT, preferred_element_type=F32) * scale
-            w = jnp.exp2(t - jnp.max(t, axis=1, keepdims=True))
-            total = jnp.sum(w, axis=1, keepdims=True)
+            t = lax.dot_general(p[0:tokens, cols], keys, NT, preferred_element_type=F32)
+            w = jnp.exp2((t - jnp.max(t, axis=1, keepdims=True)) * scale)
             o = jnp.dot(w.astype(BF16), values, preferred_element_type=F32)
-            put(s, h, (o / total).astype(BF16))
-
-
-def middle_kernel(n, counts, *refs):
-    inputs, last, outs, sem = refs[: -2 * n - 1], refs[-2 * n - 1 : -n - 1], refs[-n - 1 : -1], refs[-1]
+            put(s, h, (o[:, :VHEAD] / o[:, VHEAD:]).astype(BF16))
+
+
+def first_kernel(n, tokens, *refs):
+    pieces, outs = refs[:n], refs[n:]
+
+    def put(s, h, rows):
+        outs[s][:, h * VHEAD : (h + 1) * VHEAD] = rows
+
+    attend_heads(pieces, tokens, put)
+
+
+def middle_kernel(n, *refs):
+    pieces, before, last = refs[:n], refs[n : 2 * n], refs[2 * n : 3 * n]
+    outs, sem = refs[3 * n : -1], refs[-1]
     tokens = last[0].shape[0] // 3
-    top = pl.ds(0, 3 * tokens)
-    copies = [
-        pltpu.make_async_copy(last[s], outs[s].at[top, :], sem.at[s]) for s in range(n)
-    ]
+    early, width = before[0].shape[1], outs[0].shape[1]
+    copies = []
+    for s in range(n):
+        top, below = pl.ds(0, 3 * tokens), pl.ds(3 * tokens, tokens)
+        copies.append(pltpu.make_async_copy(last[s], outs[s].at[top, :], sem.at[2 * s]))
+        to = outs[s].at[below, pl.ds(0, early)]
+        copies.append(pltpu.make_async_copy(before[s], to, sem.at[2 * s + 1]))
     for copy in copies:
         copy.start()
-    head = 0
-    for c, count in enumerate(counts):
-        first = head * VHEAD
-
-        def put(s, h, rows, first=first):
-            at = first + h * VHEAD
-            low, side = (at // outs[0].shape[1]) * tokens + 3 * tokens, at % outs[0].shape[1]
-            outs[s][low : low + tokens, side : side + VHEAD] = rows
-
-        attend_heads(inputs[c * n : (c + 1) * n], tokens, put)
-        head += count
+
+    def put(s, h, rows):
+        at = early + h * VHEAD
+        outs[s][3 * tokens :, at : at + VHEAD] = rows
+
+    attend_heads(pieces, tokens, put)
     for copy in copies:
         copy.wait()
 
 
-def middle(chunks, last, n, moved):
-    counts = [c[0].shape[1] // VHEAD for c in chunks]
+def middle(chunk, before, last, n, moved):
     tokens = last[0].shape[0] // 3
-    width = last[0].shape[1]
-    tall = 3 * tokens + -(-sum(counts) * VHEAD // width) * tokens
-    pieces = [p for c in chunks for p in c]
+    stay = pl.BlockSpec(memory_space=pl.ANY)
     return pl.pallas_call(
-        functools.partial(middle_kernel, n, counts),
-        out_shape=(sds((tall, width)),) * n,
-        in_specs=[whole()] * len(pieces) + [pl.BlockSpec(memory_space=pl.ANY)] * n,
+        functools.partial(middle_kernel, n),
+        out_shape=(sds((4 * tokens, last[0].shape[1])),) * n,
+        in_specs=[whole()] * n + [stay] * (2 * n),
         out_specs=(whole(),) * n,
-        scratch_shapes=[pltpu.SemaphoreType.DMA((n,))],
+        scratch_shapes=[pltpu.SemaphoreType.DMA((2 * n,))],
         compiler_params=pltpu.CompilerParams(vmem_limit_bytes=16 * MIB),
         cost_estimate=pl.CostEstimate(flops=0, bytes_accessed=moved, transcendentals=0),
-    )(*pieces, *last)
+    )(*chunk, *before, *last)
 
 
 def last_kernel(n, tokens, *refs):
@@ -391,8 +396,9 @@
         s = s * scale
         peak = jnp.max(s, axis=1, keepdims=True)
         w = jnp.exp2(s - peak)
-        total = jnp.sum(w, axis=1, keepdims=True)
-        o = jnp.dot(w.astype(BF16), values[:, cols], preferred_element_type=F32) / total
+        wide = jnp.concatenate([values[:, cols], jnp.ones_like(values[:, cols])], axis=1)
+        o = jnp.dot(w.astype(BF16), wide, preferred_element_type=F32)
+        o, total = o[:, :LANES] / o[:, LANES:], o[:, LANES:]
         out[:, cols] = jnp.where(low, o[:count], o[count:]).astype(BF16)
         for i in range(2):
             head = lane == 2 * pair + i
@@ -635,10 +641,16 @@
         )
         order //= 2
     shares = [share, trade(share, 2)] if n > 2 else [share]
-    built = middle([chunk_0, chunk_1], packed[n:], n, MIB)
+    first = call(
+        functools.partial(first_kernel, n, tokens),
+        (after(chunk_0[0], share), *chunk_0[1:]),
+        [sds((tokens, widths[0]))] * n,
+        limit=16,
+    )
+    built = middle(chunk_1, first, packed[n:], n, MIB)
     below = append(n, (0, 2), built[1], shares)
     chunk_2 = [built[0], trade(below, 1)]
-    chunk_2 += [trade(after(built[s], shares[1]), s) for s in range(2, n)]
+    chunk_2 += [trade(built[s], s) for s in range(2, n)]
     (heard,) = call(
         functools.partial(heard_kernel, n, tokens, rows),
         (cq, *chunk_0),
@@ -668,7 +680,7 @@
         n in (2, 4, 8)
         and lax.axis_size("tp") == 2
         and heads % n == 0
-        and heads // n > 2
+        and heads // n == 4
         and vq.shape[0] == LANES
         and n * vq.shape[0] <= 1024
         and aq.shape[0] % 8 == 0

time: 71.4 us -> 70 us (0.980)
  waiting for transfers between devices: 17 us -> 25.4 us
  starting transfers between devices: 28.5 us -> 20.7 us
  Pallas kernels: 18.9 us -> 16.8 us
    ppermute x13, waiting for transfers between devices: 13.1 us -> 21.6 us  [trade(): return lax.ppermute(value, 'seq', [(i, i ^ by) for i in range(n)])]
    ppermute x13, starting transfers between devices: 27 us -> 19.2 us  [trade(): return lax.ppermute(value, 'seq', [(i, i ^ by) for i in range(n)])]
    pallas_call x1, Pallas kernels: 3.3 us -> 1.8 us  [middle(): pl.pallas_call(functools.partial(middle_kernel, n), out_shape=(sds((4 * t...]
    pallas_call x3 -> x4, Pallas kernels: 7.05 us -> 6.5 us  [call(): pl.pallas_call(kernel, out_shape=tuple(outs), in_specs=[whole()] * len(in...]
  transfers between devices with their start and end apart: 14 -> 14, of which waited for: 6 -> 6; matrix products, arithmetic and copies ran while one was open for 0% -> 0% of each run, Pallas kernels for 19% -> 18%
where the time goes in v5:
time: 70 us; the launch traced here: 69.7 us
  waiting for transfers between devices  25.4 us (36%)
  starting transfers between devices  20.7 us (30%)
  Pallas kernels  16.8 us (24%)
  local copies, waits for them, and re-layouts  5.96 us (9%)
  between operations  0.79 us (1%)
    ppermute x13, waiting for transfers between devices, trade(): return lax.ppermute(value, 'seq', [(i, i ^ by) for i in range(n)])  21.6 us
    ppermute x13, starting transfers between devices, trade(): return lax.ppermute(value, 'seq', [(i, i ^ by) for i in range(n)])  19.2 us
    pallas_call x4, Pallas kernels, call(): pl.pallas_call(kernel, out_shape=tuple(outs), in_specs=[whole()] * len(in...  6.5 us
    unnamed x20, local copies, waits for them, and re-layouts  5.96 us
    ppermute x1, waiting for transfers between devices, short_body(): other_sum = lax.ppermute(sent_sum, 'tp', [(0, 1), (1, 0)])  3.83 us
    pallas_call x2, Pallas kernels, pack(): pl.pallas_call(functools.partial(pack_kernel, n, first, widths, len(audio...  2.91 us
    pallas_call x1, Pallas kernels, combine(): pl.pallas_call(functools.partial(combine_kernel, n, base, tokens, rows),...  2.89 us
    pallas_call x1, Pallas kernels, middle(): pl.pallas_call(functools.partial(middle_kernel, n), out_shape=(sds((4 * t...  1.8 us
  transfers between devices with their start and end apart: 14, of which 6 were waited for; matrix products, arithmetic and copies ran while one was open for 0% of the time, Pallas kernels for 18%

profile of v5, /device:TPU:0, one launch (start us, length us, event | category | flops | bytes accessed | tf_op | source)
XLA Modules:
  0.0 69.7 jit_solution(14711979855311679094)
XLA Ops:
  0.7 2.0 %shard_map.156 = (bf16[640,128]{1,0:T(8,128)(2,1)}, bf16[640,128]{1,0:T(8,128)(2,1)}, bf16[640,128]{1,0:T(8,128)(2,1)}, bf16[640,128]{1,0:T(8,128)(2,1)}) custom-call(bf16[128,2048]{1,0:T(8,128)(2,1)} %bitcast.15, bf16[128,2048]{1,0:T(8,128)(2,1)} %bitcast.17, bf16[128,2048]{1,0:T(8,128)(2,1)} %bitcast.19, bf16[8,1024]{1,0:T(8,128)(2,1)} %bitcast.27, ...), custom_call_target="tpu_custom_call" | custom-call | bytes 1572864 | tf_op jit(solution)/shard_map/pallas_call | solution.py:237
  2.7 5.1 %collective-permute-start.3 = (bf16[640,128]{1,0:T(8,128)(2,1)}, bf16[640,128]{1,0:T(8,128)(2,1)S(1)}, u32[]{:S(2)}, u32[]{:S(2)}) collective-permute-start(bf16[640,128]{1,0:T(8,128)(2,1)} %get-tuple-element.48), channel_id=1, source_target_pairs={{0,12},{4,8},{8,4},{12,0},{1,13},{5,9},{9,5},{13,1},{2,14},{6,10},... | collective-permute-start | bytes 491528 | tf_op jit(solution)/shard_map/ppermute | solution.py:177
  8.5 1.0 %copy-done.2 = bf16[1,128,2048]{2,1,0:T(8,128)(2,1)S(1)} copy-done((bf16[1,128,2048]{2,1,0:T(8,128)(2,1)S(1)}, bf16[1,128,2048]{2,1,0:T(8,128)(2,1)}, u32[]{:S(2)}) %copy-start.2) | copy-done | bytes 524312
  9.5 1.0 %copy-done.3 = bf16[1,128,2048]{2,1,0:T(8,128)(2,1)S(1)} copy-done((bf16[1,128,2048]{2,1,0:T(8,128)(2,1)S(1)}, bf16[1,128,2048]{2,1,0:T(8,128)(2,1)}, u32[]{:S(2)}) %copy-start.3) | copy-done | bytes 524312
  10.6 1.0 %copy-done.4 = bf16[1,128,2048]{2,1,0:T(8,128)(2,1)S(1)} copy-done((bf16[1,128,2048]{2,1,0:T(8,128)(2,1)S(1)}, bf16[1,128,2048]{2,1,0:T(8,128)(2,1)}, u32[]{:S(2)}) %copy-start.4) | copy-done | bytes 524312
  15.3 1.5 %collective-permute-start = (bf16[384,128]{1,0:T(8,128)(2,1)S(1)}, bf16[384,128]{1,0:T(8,128)(2,1)S(1)}, u32[]{:S(2)}, u32[]{:S(2)}) collective-permute-start(bf16[384,128]{1,0:T(8,128)(2,1)S(1)} %get-tuple-element.44), channel_id=1, source_target_pairs={{0,4},{4,0},{8,12},{12,8},{1,5},{5,1},{9,13},{13,9},{2,6},{6,2},{1... | collective-permute-start | bytes 294920 | tf_op jit(solution)/shard_map/ppermute | solution.py:177
  16.7 2.9 %collective-permute-start.1 = (bf16[384,128]{1,0:T(8,128)(2,1)S(1)}, bf16[384,128]{1,0:T(8,128)(2,1)S(1)}, u32[]{:S(2)}, u32[]{:S(2)}) collective-permute-start(bf16[384,128]{1,0:T(8,128)(2,1)S(1)} %get-tuple-element.45), channel_id=1, source_target_pairs={{0,8},{4,12},{8,0},{12,4},{1,9},{5,13},{9,1},{13,5},{2,10},{6,14},... | collective-permute-start | bytes 294920 | tf_op jit(solution)/shard_map/ppermute | solution.py:177
  19.8 8.2 %collective-permute-done.4.refs_1_.refs_2_.refs_4_ = bf16[640,128]{1,0:T(8,128)(2,1)S(1)} collective-permute-done((bf16[640,128]{1,0:T(8,128)(2,1)}, bf16[640,128]{1,0:T(8,128)(2,1)S(1)}, u32[]{:S(2)}, u32[]{:S(2)}) %collective-permute-start.4) | collective-permute-done | bytes 163872 | tf_op jit(solution)/shard_map/ppermute | solution.py:177
  27.9 2.1 %shard_map.158.refs_0_ = bf16[32,1152]{1,0:T(8,128)(2,1)S(1)} custom-call(bf16[640,128]{1,0:T(8,128)(2,1)S(1)} %collective-permute-done.3.refs_0_.refs_3_.refs_5_, bf16[640,128]{1,0:T(8,128)(2,1)S(1)} %collective-permute-done.4.refs_1_.refs_2_.refs_4_, bf16[640,128]{1,0:T(8,128)(2,1)S(1)} %collective-permute-done.5.refs_2_.refs_1_.refs_3_, ...), custom_call_target="tpu_custom_call" | custom-call | bytes 1048576 | tf_op jit(solution)/shard_map/pallas_call | solution.py:165
  30.8 1.8 %shard_map.160 = (bf16[512,256]{1,0:T(8,128)(2,1)S(1)}, bf16[512,256]{1,0:T(8,128)(2,1)S(1)}, bf16[512,256]{1,0:T(8,128)(2,1)S(1)}, bf16[512,256]{1,0:T(8,128)(2,1)S(1)}) custom-call(bf16[384,128]{1,0:T(8,128)(2,1)S(1)} %get-tuple-element.43.refs_0_, bf16[384,128]{1,0:T(8,128)(2,1)S(1)} %collective-permute-done.refs_1_, ...), custom_call_target="tpu_custom_call" | custom-call | bytes 1048576 | tf_op jit(solution)/shard_map/pallas_call | solution.py:305
  32.6 3.4 %collective-permute-done.6.refs_1_ = bf16[32,1152]{1,0:T(8,128)(2,1)S(1)} collective-permute-done((bf16[32,1152]{1,0:T(8,128)(2,1)S(1)}, bf16[32,1152]{1,0:T(8,128)(2,1)S(1)}, u32[]{:S(2)}, u32[]{:S(2)}) %collective-permute-start.6) | collective-permute-done | bytes 73760 | tf_op jit(solution)/shard_map/ppermute | solution.py:177
  36.5 2.7 %collective-permute-start.8 = (bf16[512,256]{1,0:T(8,128)(2,1)S(1)}, bf16[512,256]{1,0:T(8,128)(2,1)S(1)}, u32[]{:S(2)}, u32[]{:S(2)}) collective-permute-start(bf16[512,256]{1,0:T(8,128)(2,1)S(1)} %get-tuple-element.64), channel_id=1, source_target_pairs={{0,8},{4,12},{8,0},{12,4},{1,9},{5,13},{9,1},{13,5},{2,10},{6,14},... | collective-permute-start | bytes 786440 | tf_op jit(solution)/shard_map/ppermute | solution.py:177
  39.2 1.7 %collective-permute-start.9 = (bf16[512,256]{1,0:T(8,128)(2,1)S(1)}, bf16[512,256]{1,0:T(8,128)(2,1)S(1)}, u32[]{:S(2)}, u32[]{:S(2)}) collective-permute-start(bf16[512,256]{1,0:T(8,128)(2,1)S(1)} %get-tuple-element.65), channel_id=1, source_target_pairs={{0,12},{4,8},{8,4},{12,0},{1,13},{5,9},{9,5},{13,1},{2,14},{6,10},... | collective-permute-start | bytes 786440 | tf_op jit(solution)/shard_map/ppermute | solution.py:177
  40.9 2.8 %shard_map.162 = bf16[128,1024]{1,0:T(8,128)(2,1)} custom-call(bf16[128,1024]{1,0:T(8,128)(2,1)S(1)} %bitcast.23, bf16[640,128]{1,0:T(8,128)(2,1)S(1)} %get-tuple-element.53.refs_3_.refs_0_.refs_2_, bf16[640,128]{1,0:T(8,128)(2,1)S(1)} %collective-permute-done.5.refs_2_.refs_1_.refs_3_, bf16[640,128]{1,0:T(8,128)(2,1)S(1)} %collective-permute-done.4.refs_1_.refs_2_.refs_4_, ...), custom_call_target="tpu_custom_call" | custom-call | bytes 1048576 | tf_op jit(solution)/shard_map/pallas_call | solution.py:165
  43.6 6.4 %collective-permute-done.7.refs_1_ = bf16[672,256]{1,0:T(8,128)(2,1)S(1)} collective-permute-done((bf16[672,256]{1,0:T(8,128)(2,1)S(1)}, bf16[672,256]{1,0:T(8,128)(2,1)S(1)}, u32[]{:S(2)}, u32[]{:S(2)}) %collective-permute-start.7) | collective-permute-done | bytes 344096 | tf_op jit(solution)/shard_map/ppermute | solution.py:177
  50.1 2.9 %shard_map.163 = (f32[5,32,512]{2,1,0:T(8,128)S(1)}, bf16[5,32,512]{2,1,0:T(8,128)(2,1)S(1)}, bf16[8,1024]{1,0:T(8,128)(2,1)}) custom-call(bf16[672,256]{1,0:T(8,128)(2,1)S(1)} %shard_map.161.refs_0_, bf16[672,256]{1,0:T(8,128)(2,1)S(1)} %collective-permute-done.7.refs_1_, bf16[640,128]{1,0:T(8,128)(2,1)S(1)} %get-tuple-element.53.refs_3_.refs_0_.refs_2_, ...), custom_call_target="tpu_custom_call" | custom-call | tf_op jit(solution)/shard_map/pallas_call | solution.py:530
  53.0 1.5 %collective-permute-start.10 = (bf16[5,32,512]{2,1,0:T(8,128)(2,1)S(1)}, bf16[5,32,512]{2,1,0:T(8,128)(2,1)S(1)}, u32[]{:S(2)}, u32[]{:S(2)}) collective-permute-start(bf16[5,32,512]{2,1,0:T(8,128)(2,1)S(1)} %get-tuple-element.68), channel_id=1, source_target_pairs={{0,2},{2,0},{1,3},{3,1},{4,6},{6,4},{5,7},{7,5},{8,10},{10,8},{9,1... | collective-permute-start | bytes 491528 | tf_op jit(solution)/shard_map/ppermute | solution.py:663
  54.5 3.8 %collective-permute-done.10.other = bf16[5,32,512]{2,1,0:T(8,128)(2,1)S(1)} collective-permute-done((bf16[5,32,512]{2,1,0:T(8,128)(2,1)S(1)}, bf16[5,32,512]{2,1,0:T(8,128)(2,1)S(1)}, u32[]{:S(2)}, u32[]{:S(2)}) %collective-permute-start.10) | collective-permute-done | bytes 163872 | tf_op jit(solution)/shard_map/ppermute | solution.py:663
  58.3 1.4 %shard_map.164 = (f32[8,1024]{1,0:T(8,128)S(1)}, bf16[8,1024]{1,0:T(8,128)(2,1)S(1)}, bf16[8,1024]{1,0:T(8,128)(2,1)S(1)}, bf16[8,1024]{1,0:T(8,128)(2,1)S(1)}) custom-call(f32[5,32,512]{2,1,0:T(8,128)S(1)} %get-tuple-element.67.own, bf16[5,32,512]{2,1,0:T(8,128)(2,1)S(1)} %collective-permute-done.10.other, bf16[2048,1024]{1,0:T(8,128)(2,1)S(1)} %copy-done), custom_call_target="tpu_custom_call" | custom-call | tf_op jit(solution)/shard_map/pallas_call | solution.py:571
  59.7 1.0 %shard_map.165 = (bf16[160,256]{1,0:T(8,128)(2,1)S(1)}, bf16[160,256]{1,0:T(8,128)(2,1)S(1)}, bf16[160,256]{1,0:T(8,128)(2,1)S(1)}, bf16[160,256]{1,0:T(8,128)(2,1)S(1)}) custom-call(bf16[512,256]{1,0:T(8,128)(2,1)S(1)} %get-tuple-element.62.refs_0_, bf16[672,256]{1,0:T(8,128)(2,1)S(1)} %collective-permute-done.7.refs_1_, ...), custom_call_target="tpu_custom_call" | custom-call | tf_op jit(solution)/shard_map/pallas_call | solution.py:165
  60.7 2.3 %collective-permute-start.11 = (bf16[160,256]{1,0:T(8,128)(2,1)S(1)}, bf16[160,256]{1,0:T(8,128)(2,1)S(1)}, u32[]{:S(2)}, u32[]{:S(2)}) collective-permute-start(bf16[160,256]{1,0:T(8,128)(2,1)S(1)} %get-tuple-element.73), channel_id=1, source_target_pairs={{0,12},{4,8},{8,4},{12,0},{1,13},{5,9},{9,5},{13,1},{2,14},{6,10},... | collective-permute-start | bytes 245768 | tf_op jit(solution)/shard_map/ppermute | solution.py:177
  63.0 2.2 %collective-permute-start.13 = (bf16[160,256]{1,0:T(8,128)(2,1)S(1)}, bf16[160,256]{1,0:T(8,128)(2,1)S(1)}, u32[]{:S(2)}, u32[]{:S(2)}) collective-permute-start(bf16[160,256]{1,0:T(8,128)(2,1)S(1)} %get-tuple-element.75), channel_id=1, source_target_pairs={{0,4},{4,0},{8,12},{12,8},{1,5},{5,1},{9,13},{13,9},{2,6},{6,2},{1... | collective-permute-start | bytes 245768 | tf_op jit(solution)/shard_map/ppermute | solution.py:177
  65.2 1.9 %collective-permute-done.11.refs_4_ = bf16[160,256]{1,0:T(8,128)(2,1)S(1)} collective-permute-done((bf16[160,256]{1,0:T(8,128)(2,1)S(1)}, bf16[160,256]{1,0:T(8,128)(2,1)S(1)}, u32[]{:S(2)}, u32[]{:S(2)}) %collective-permute-start.11) | collective-permute-done | bytes 81952 | tf_op jit(solution)/shard_map/ppermute | solution.py:177
  67.1 1.7 %collective-permute-done.12.refs_5_ = bf16[160,256]{1,0:T(8,128)(2,1)S(1)} collective-permute-done((bf16[160,256]{1,0:T(8,128)(2,1)S(1)}, bf16[160,256]{1,0:T(8,128)(2,1)S(1)}, u32[]{:S(2)}, u32[]{:S(2)}) %collective-permute-start.12) | collective-permute-done | bytes 81952 | tf_op jit(solution)/shard_map/ppermute | solution.py:177
  (35 shorter events, 6.6 us)
Async XLA Ops:
  0.6 40.3 %copy-start.7 = (bf16[1,128,1024]{2,1,0:T(8,128)(2,1)S(1)}, bf16[1,128,1024]{2,1,0:T(8,128)(2,1)}, u32[]{:S(2)}) copy-start(bf16[1,128,1024]{2,1,0:T(8,128)(2,1)} %param.16) | copy-start | bytes 786436
  0.6 49.5 %copy-start.9 = (f32[2048]{0:T(1024)S(1)}, f32[2048]{0:T(1024)}, u32[]{:S(2)}) copy-start(f32[2048]{0:T(1024)} %param.23) | copy-start | bytes 24580
  2.7 47.4 %copy-start.1 = (bf16[1024,2048]{1,0:T(8,128)(2,1)S(1)}, bf16[1024,2048]{1,0:T(8,128)(2,1)}, u32[]{:S(2)}) copy-start(bf16[1024,2048]{1,0:T(8,128)(2,1)} %refs_7_.1) | copy-start | bytes 12582916
  2.7 17.0 %collective-permute-start.3 = (bf16[640,128]{1,0:T(8,128)(2,1)}, bf16[640,128]{1,0:T(8,128)(2,1)S(1)}, u32[]{:S(2)}, u32[]{:S(2)}) collective-permute-start(bf16[640,128]{1,0:T(8,128)(2,1)} %get-tuple-element.48), channel_id=1, source_target_pairs={{0,12},{4,8},{8,4},{12,0},{1,13},{5,9},{9,5},{13,1},{2,14},{6,10},... | collective-permute-start | bytes 491528 | tf_op jit(solution)/shard_map/ppermute | solution.py:177
  7.8 20.1 %collective-permute-start.4 = (bf16[640,128]{1,0:T(8,128)(2,1)}, bf16[640,128]{1,0:T(8,128)(2,1)S(1)}, u32[]{:S(2)}, u32[]{:S(2)}) collective-permute-start(bf16[640,128]{1,0:T(8,128)(2,1)} %get-tuple-element.49), channel_id=1, source_target_pairs={{0,8},{4,12},{8,0},{12,4},{1,9},{5,13},{9,1},{13,5},{2,10},{6,14},... | collective-permute-start | bytes 491528 | tf_op jit(solution)/shard_map/ppermute | solution.py:177
  7.8 20.1 %collective-permute-start.5 = (bf16[640,128]{1,0:T(8,128)(2,1)}, bf16[640,128]{1,0:T(8,128)(2,1)S(1)}, u32[]{:S(2)}, u32[]{:S(2)}) collective-permute-start(bf16[640,128]{1,0:T(8,128)(2,1)} %get-tuple-element.50), channel_id=1, source_target_pairs={{0,4},{4,0},{8,12},{12,8},{1,5},{5,1},{9,13},{13,9},{2,6},{6,2},{1... | collective-permute-start | bytes 491528 | tf_op jit(solution)/shard_map/ppermute | solution.py:177
  8.5 1.0 %copy-start.2 = (bf16[1,128,2048]{2,1,0:T(8,128)(2,1)S(1)}, bf16[1,128,2048]{2,1,0:T(8,128)(2,1)}, u32[]{:S(2)}) copy-start(bf16[1,128,2048]{2,1,0:T(8,128)(2,1)} %param.13) | copy-start | bytes 1572868
  9.5 1.0 %copy-start.3 = (bf16[1,128,2048]{2,1,0:T(8,128)(2,1)S(1)}, bf16[1,128,2048]{2,1,0:T(8,128)(2,1)}, u32[]{:S(2)}) copy-start(bf16[1,128,2048]{2,1,0:T(8,128)(2,1)} %param.14) | copy-start | bytes 1572868
  10.6 1.0 %copy-start.4 = (bf16[1,128,2048]{2,1,0:T(8,128)(2,1)S(1)}, bf16[1,128,2048]{2,1,0:T(8,128)(2,1)}, u32[]{:S(2)}) copy-start(bf16[1,128,2048]{2,1,0:T(8,128)(2,1)} %param.15) | copy-start | bytes 1572868
  11.6 0.9 %copy-start.5 = (bf16[1,128,1024]{2,1,0:T(8,128)(2,1)S(1)}, bf16[1,128,1024]{2,1,0:T(8,128)(2,1)}, u32[]{:S(2)}) copy-start(bf16[1,128,1024]{2,1,0:T(8,128)(2,1)} %param.20) | copy-start | bytes 786436
  12.5 0.9 %copy-start.6 = (bf16[1,128,1024]{2,1,0:T(8,128)(2,1)S(1)}, bf16[1,128,1024]{2,1,0:T(8,128)(2,1)}, u32[]{:S(2)}) copy-start(bf16[1,128,1024]{2,1,0:T(8,128)(2,1)} %param.21) | copy-start | bytes 786436
  13.5 0.9 %copy-start.8 = (bf16[640,128]{1,0:T(8,128)(2,1)S(1)}, bf16[640,128]{1,0:T(8,128)(2,1)}, u32[]{:S(2)}) copy-start(bf16[640,128]{1,0:T(8,128)(2,1)} %get-tuple-element.42.refs_0_) | copy-start | bytes 491524
  15.3 15.5 %collective-permute-start = (bf16[384,128]{1,0:T(8,128)(2,1)S(1)}, bf16[384,128]{1,0:T(8,128)(2,1)S(1)}, u32[]{:S(2)}, u32[]{:S(2)}) collective-permute-start(bf16[384,128]{1,0:T(8,128)(2,1)S(1)} %get-tuple-element.44), channel_id=1, source_target_pairs={{0,4},{4,0},{8,12},{12,8},{1,5},{5,1},{9,13},{13,9},{2,6},{6,2},{1... | collective-permute-start | bytes 294920 | tf_op jit(solution)/shard_map/ppermute | solution.py:177
  16.7 14.0 %collective-permute-start.1 = (bf16[384,128]{1,0:T(8,128)(2,1)S(1)}, bf16[384,128]{1,0:T(8,128)(2,1)S(1)}, u32[]{:S(2)}, u32[]{:S(2)}) collective-permute-start(bf16[384,128]{1,0:T(8,128)(2,1)S(1)} %get-tuple-element.45), channel_id=1, source_target_pairs={{0,8},{4,12},{8,0},{12,4},{1,9},{5,13},{9,1},{13,5},{2,10},{6,14},... | collective-permute-start | bytes 294920 | tf_op jit(solution)/shard_map/ppermute | solution.py:177
  19.7 11.1 %collective-permute-start.2 = (bf16[384,128]{1,0:T(8,128)(2,1)S(1)}, bf16[384,128]{1,0:T(8,128)(2,1)S(1)}, u32[]{:S(2)}, u32[]{:S(2)}) collective-permute-start(bf16[384,128]{1,0:T(8,128)(2,1)S(1)} %get-tuple-element.46), channel_id=1, source_target_pairs={{0,12},{4,8},{8,4},{12,0},{1,13},{5,9},{9,5},{13,1},{2,14},{6,10},... | collective-permute-start | bytes 294920 | tf_op jit(solution)/shard_map/ppermute | solution.py:177
  30.0 6.0 %collective-permute-start.6 = (bf16[32,1152]{1,0:T(8,128)(2,1)S(1)}, bf16[32,1152]{1,0:T(8,128)(2,1)S(1)}, u32[]{:S(2)}, u32[]{:S(2)}) collective-permute-start(bf16[32,1152]{1,0:T(8,128)(2,1)S(1)} %shard_map.158.refs_0_), channel_id=1, source_target_pairs={{0,8},{4,12},{8,0},{12,4},{1,9},{5,13},{9,1},{13,5},{2,10},{6,14},... | collective-permute-start | bytes 221192 | tf_op jit(solution)/shard_map/ppermute | solution.py:177
  30.8 27.5 %copy-start = (bf16[2048,1024]{1,0:T(8,128)(2,1)S(1)}, bf16[2048,1024]{1,0:T(8,128)(2,1)}, u32[]{:S(2)}) copy-start(bf16[2048,1024]{1,0:T(8,128)(2,1)} %down.1) | copy-start | bytes 12582916
  36.4 13.7 %collective-permute-start.7 = (bf16[672,256]{1,0:T(8,128)(2,1)S(1)}, bf16[672,256]{1,0:T(8,128)(2,1)S(1)}, u32[]{:S(2)}, u32[]{:S(2)}) collective-permute-start(bf16[672,256]{1,0:T(8,128)(2,1)S(1)} %shard_map.161.refs_0_), channel_id=1, source_target_pairs={{0,4},{4,0},{8,12},{12,8},{1,5},{5,1},{9,13},{13,9},{2,6},{6,2},{1... | collective-permute-start | bytes 1032200 | tf_op jit(solution)/shard_map/ppermute | solution.py:177
  36.5 23.2 %collective-permute-start.8 = (bf16[512,256]{1,0:T(8,128)(2,1)S(1)}, bf16[512,256]{1,0:T(8,128)(2,1)S(1)}, u32[]{:S(2)}, u32[]{:S(2)}) collective-permute-start(bf16[512,256]{1,0:T(8,128)(2,1)S(1)} %get-tuple-element.64), channel_id=1, source_target_pairs={{0,8},{4,12},{8,0},{12,4},{1,9},{5,13},{9,1},{13,5},{2,10},{6,14},... | collective-permute-start | bytes 786440 | tf_op jit(solution)/shard_map/ppermute | solution.py:177
  39.2 20.5 %collective-permute-start.9 = (bf16[512,256]{1,0:T(8,128)(2,1)S(1)}, bf16[512,256]{1,0:T(8,128)(2,1)S(1)}, u32[]{:S(2)}, u32[]{:S(2)}) collective-permute-start(bf16[512,256]{1,0:T(8,128)(2,1)S(1)} %get-tuple-element.65), channel_id=1, source_target_pairs={{0,12},{4,8},{8,4},{12,0},{1,13},{5,9},{9,5},{13,1},{2,14},{6,10},... | collective-permute-start | bytes 786440 | tf_op jit(solution)/shard_map/ppermute | solution.py:177
  53.0 5.3 %collective-permute-start.10 = (bf16[5,32,512]{2,1,0:T(8,128)(2,1)S(1)}, bf16[5,32,512]{2,1,0:T(8,128)(2,1)S(1)}, u32[]{:S(2)}, u32[]{:S(2)}) collective-permute-start(bf16[5,32,512]{2,1,0:T(8,128)(2,1)S(1)} %get-tuple-element.68), channel_id=1, source_target_pairs={{0,2},{2,0},{1,3},{3,1},{4,6},{6,4},{5,7},{7,5},{8,10},{10,8},{9,1... | collective-permute-start | bytes 491528 | tf_op jit(solution)/shard_map/ppermute | solution.py:663
  60.7 6.3 %collective-permute-start.11 = (bf16[160,256]{1,0:T(8,128)(2,1)S(1)}, bf16[160,256]{1,0:T(8,128)(2,1)S(1)}, u32[]{:S(2)}, u32[]{:S(2)}) collective-permute-start(bf16[160,256]{1,0:T(8,128)(2,1)S(1)} %get-tuple-element.73), channel_id=1, source_target_pairs={{0,12},{4,8},{8,4},{12,0},{1,13},{5,9},{9,5},{13,1},{2,14},{6,10},... | collective-permute-start | bytes 245768 | tf_op jit(solution)/shard_map/ppermute | solution.py:177
  63.0 5.8 %collective-permute-start.12 = (bf16[160,256]{1,0:T(8,128)(2,1)S(1)}, bf16[160,256]{1,0:T(8,128)(2,1)S(1)}, u32[]{:S(2)}, u32[]{:S(2)}) collective-permute-start(bf16[160,256]{1,0:T(8,128)(2,1)S(1)} %get-tuple-element.74), channel_id=1, source_target_pairs={{0,8},{4,12},{8,0},{12,4},{1,9},{5,13},{9,1},{13,5},{2,10},{6,14},... | collective-permute-start | bytes 245768 | tf_op jit(solution)/shard_map/ppermute | solution.py:177
  63.0 5.8 %collective-permute-start.13 = (bf16[160,256]{1,0:T(8,128)(2,1)S(1)}, bf16[160,256]{1,0:T(8,128)(2,1)S(1)}, u32[]{:S(2)}, u32[]{:S(2)}) collective-permute-start(bf16[160,256]{1,0:T(8,128)(2,1)S(1)} %get-tuple-element.75), channel_id=1, source_target_pairs={{0,4},{4,0},{8,12},{12,8},{1,5},{5,1},{9,13},{13,9},{2,6},{6,2},{1... | collective-permute-start | bytes 245768 | tf_op jit(solution)/shard_map/ppermute | solution.py:177

commit v6 on v5

--- a/solution.py
+++ b/solution.py
@@ -183,12 +183,12 @@
     return first, second, value - first - second
 
 
-def pack_kernel(n, first, widths, audio_count, kept, q, k, v, *refs):
+def pack_kernel(n, first, widths, audio_count, kept, staged, columns, q, k, v, *refs):
     count = n * len(widths)
     audio, refs = refs[:audio_count], refs[audio_count:]
     keep, refs = refs[:kept], refs[kept:]
     outs, passed, refs = refs[:count], refs[count : count + kept], refs[count + kept :]
-    built = refs[:count] if audio else outs
+    built = refs[:count] if staged else outs
     lines, sem, audio_sem, out_sem = refs[-3 - audio_count : -3], refs[-3], refs[-2], refs[-1]
     me = lax.axis_index("seq")
     tokens = q.shape[0]
@@ -211,35 +211,41 @@
     if audio:
         for copy in fetches:
             copy.wait()
-        half = lines[0].shape[1]
-        mine = pl.ds(pl.multiple_of(lax.axis_index("tp") * half, LANES), half)
-        parts = [ref[...].astype(F32) for ref in lines[:3]] + [lines[3][:, mine].astype(F32)]
-        blocks = [part[:, c : c + widths[0]] for part in parts for c in range(0, half, widths[0])]
+        parts = []
+        for ref in lines:
+            mine = slice(None)
+            if ref.shape[1] > columns:
+                mine = pl.ds(pl.multiple_of(lax.axis_index("tp") * columns, LANES), columns)
+            parts.append(ref[:, mine].astype(F32))
+        blocks = [part[:, c : c + widths[0]] for part in parts for c in range(0, columns, widths[0])]
         extra = jnp.concatenate(blocks, axis=0).astype(BF16)
         for s in range(n):
-            built[s][3 * tokens :, :] = extra
+            if built[s].shape[0] > 3 * tokens:
+                built[s][3 * tokens :, :] = extra
     for i in range(count):
         for copy in arrivals[3 * i : 3 * i + 3]:
             copy.wait()
-        if audio:
+        if staged:
             copies.append(pltpu.make_async_copy(built[i], outs[i], out_sem.at[i]))
             copies[-1].start()
     for copy in copies:
         copy.wait()
 
 
-def pack(video, audio, keep, n, first, widths, limit, moved):
+def pack(video, audio, spots, keep, n, first, widths, limit, moved, staged):
+    columns = audio[0].shape[1] if audio else 0
+    lines = audio[0].size // widths[0] if audio else 0
     tokens = video[0].shape[0]
-    extra = 4 * audio[0].size // widths[0] if audio else 0
-    shapes = [(3 * tokens + extra, w) for w in widths for _ in range(n)]
+    extra = len(audio) * lines
+    shapes = [(3 * tokens + (extra if s in spots else 0), w) for w in widths for s in range(n)]
     stay = pl.BlockSpec(memory_space=pl.ANY)
     dma = pltpu.SemaphoreType.DMA
     return pl.pallas_call(
-        functools.partial(pack_kernel, n, first, widths, len(audio), len(keep)),
+        functools.partial(pack_kernel, n, first, widths, len(audio), len(keep), staged, columns),
         out_shape=tuple(sds(x) for x in shapes) + tuple(sds(x.shape) for x in keep),
         in_specs=[stay] * (3 + len(audio) + len(keep)),
-        out_specs=(stay if audio else whole(),) * (len(shapes) + len(keep)),
-        scratch_shapes=[pltpu.VMEM(x, BF16) for x in shapes if audio]
+        out_specs=(stay if staged else whole(),) * (len(shapes) + len(keep)),
+        scratch_shapes=[pltpu.VMEM(x, BF16) for x in shapes if staged]
         + [pltpu.VMEM(x.shape, BF16) for x in audio]
         + [dma((3 * len(shapes),)), dma((max(len(audio), 1),)), dma((len(shapes) + len(keep),))],
         compiler_params=pltpu.CompilerParams(vmem_limit_bytes=limit * MIB),
@@ -292,7 +298,8 @@
 
     def put(s, h, rows):
         at = early + h * VHEAD
-        outs[s][3 * tokens :, at : at + VHEAD] = rows
+        low, side = (3 + at // width) * tokens, at % width
+        outs[s][low : low + tokens, side : side + VHEAD] = rows
 
     attend_heads(pieces, tokens, put)
     for copy in copies:
@@ -301,10 +308,12 @@
 
 def middle(chunk, before, last, n, moved):
     tokens = last[0].shape[0] // 3
+    width = last[0].shape[1]
+    tall = tokens * (3 + (before[0].shape[1] + chunk[0].shape[1]) // width)
     stay = pl.BlockSpec(memory_space=pl.ANY)
     return pl.pallas_call(
         functools.partial(middle_kernel, n),
-        out_shape=(sds((4 * tokens, last[0].shape[1])),) * n,
+        out_shape=(sds((tall, width)),) * n,
         in_specs=[whole()] * n + [stay] * (2 * n),
         out_specs=(whole(),) * n,
         scratch_shapes=[pltpu.SemaphoreType.DMA((2 * n,))],
@@ -441,51 +450,21 @@
     return jnp.concatenate([stats, rest], axis=1).astype(BF16)
 
 
-def merge_kernel(n, order, own, other, out):
-    columns = out.shape[1] - LANES
+def merge_kernel(n, order, tokens, own, other, mine, second, out):
+    count, columns = own.shape[0], own.shape[1] - LANES
     wholes = own[...].astype(F32), reorder(other[...].astype(F32), order, n)
     parts, weight, top, every = read_shares(wholes, columns)
     for pair in range(columns // LANES):
         out[:, pair * LANES : (pair + 1) * LANES] = joint(parts, weight, pair)
-    out[:, columns:] = share_stats(top, every)
-
-
-def append_kernel(n, orders, piece, *refs):
-    shares, out, sem = refs[:-2], refs[-2], refs[-1]
-    count = shares[0].shape[0]
-    columns = shares[0].shape[1] - LANES
-    width = out.shape[1]
-    base = piece.shape[0]
-    copy = pltpu.make_async_copy(piece, out.at[pl.ds(0, base), :], sem)
-    copy.start()
-    wholes = [reorder(ref[...].astype(F32), order, n) for ref, order in zip(shares, orders)]
-    parts, weight, top, every = read_shares(wholes, columns)
-    blocks = [joint(parts, weight, pair) for pair in range(columns // LANES)]
-    blocks.append(share_stats(top, every))
-    for c, block in enumerate(blocks):
-        at, side = base + c * LANES // width * count, c * LANES % width
-        out[at : at + count, side : side + LANES] = block
-    if len(blocks) * LANES % width:
-        side = len(blocks) * LANES % width
-        out[at : at + count, side:] = jnp.zeros((count, width - side), BF16)
-    copy.wait()
-
-
-def append(n, orders, piece, shares):
-    count, columns = shares[0].shape
-    width = piece.shape[1]
-    tall = piece.shape[0] + -(-columns // width) * count
-    return pl.pallas_call(
-        functools.partial(append_kernel, n, orders),
-        out_shape=sds((tall, width)),
-        in_specs=[pl.BlockSpec(memory_space=pl.ANY)] + [whole()] * len(shares),
-        out_specs=whole(),
-        scratch_shapes=[pltpu.SemaphoreType.DMA],
-        compiler_params=pltpu.CompilerParams(vmem_limit_bytes=16 * MIB),
-    )(piece, *shares)
-
-
-def combine_kernel(n, base, tokens, rows, *refs):
+    out[:, columns : columns + LANES] = share_stats(top, every)
+    at = columns + LANES
+    for ref in (mine, second):
+        for row in range(3 * tokens, ref.shape[0], count):
+            out[:, at : at + LANES] = ref[row : row + count, :]
+            at += LANES
+
+
+def combine_kernel(n, tokens, rows, *refs):
     got, pieces, (gain, up) = refs[:2], refs[2 : 2 + n], refs[2 + n : 4 + n]
     own_sum, sent_sum, seen, x_ref = refs[4 + n :]
 
@@ -494,8 +473,7 @@
         columns = seen.shape[1]
         wholes = []
         for ref, order in zip(got, (0, 1)):
-            blocks = [ref[at : at + n * rows, :] for at in range(base, ref.shape[0], n * rows)]
-            wholes.append(reorder(jnp.concatenate(blocks, axis=1).astype(F32), order, n))
+            wholes.append(reorder(ref[:, : columns + LANES].astype(F32), order, n))
         parts, weight, _, _ = read_shares(wholes, columns)
         tails = [p[3 * tokens :, :].astype(F32) for p in pieces]
         square = jnp.zeros((n * rows, 1), F32)
@@ -503,7 +481,7 @@
             cols = slice(pair * LANES, (pair + 1) * LANES)
             o = joint(parts, weight, pair)
             seen[:, cols] = o[:rows]
-            residual = audio_rows(tails, 3, pair, rows, columns // LANES) + o.astype(F32)
+            residual = audio_rows(tails, 1, pair, rows, columns // LANES) + o.astype(F32)
             square = square + jnp.sum(residual * residual, axis=1, keepdims=True)
             at = pl.ds(pl.multiple_of(lax.axis_index("tp") * columns + pair * LANES, LANES), LANES)
             x_ref[:, cols] = (residual * gain[:, at]).astype(BF16)
@@ -521,14 +499,14 @@
         sent_sum[0] = product.astype(BF16)
 
 
-def combine(got, base, pieces, gain, up, tokens, rows, block):
+def combine(got, pieces, gain, up, tokens, rows, block):
     n = len(pieces)
     columns, units = up.shape
     steps = units // block + 1
     held = lambda ref: pl.BlockSpec(ref.shape, lambda i: (0,) * ref.ndim)
     moved = pl.BlockSpec((1, n * rows, block), lambda i: (i, 0, 0))
     return pl.pallas_call(
-        functools.partial(combine_kernel, n, base, tokens, rows),
+        functools.partial(combine_kernel, n, tokens, rows),
         grid=(steps,),
         out_shape=(
             sds((steps, n * rows, block), F32),
@@ -582,10 +560,16 @@
     )(own, other, down)
 
 
-def heard_kernel(n, tokens, rows, q, *refs):
-    pieces, out = refs[:n], refs[n]
+def heard_kernel(n, tokens, rows, q, own, second, first, out):
     pairs = q.shape[1] // LANES
-    tails = [p[3 * tokens :, :].astype(F32) for p in pieces]
+    at = first.shape[1] - 2 * (own.shape[0] - 3 * tokens) // first.shape[0] * LANES
+    half = (first.shape[1] - at) // 2
+    far = [
+        jnp.concatenate([first[:, c : c + LANES] for c in range(start, start + half, LANES)], axis=0)
+        for start in (at, at + half)
+    ]
+    tails = [own[3 * tokens :, :], far[0], second[3 * tokens :, :], far[1]]
+    tails = [tail.astype(F32) for tail in tails]
     count = n * rows
     low = low_half((count, LANES))
     scale = LOG2E / math.sqrt(CHEAD)
@@ -596,14 +580,14 @@
 
     for pair in range(pairs):
         cols = slice(pair * LANES, (pair + 1) * LANES)
-        s = lax.dot_general(both(1, pair), q[:, cols], NT, preferred_element_type=F32) * scale
+        s = lax.dot_general(both(0, pair), q[:, cols], NT, preferred_element_type=F32) * scale
         probs = []
         for i in range(2):
             t = s[i * count : (i + 1) * count]
             w = jnp.exp2(t - jnp.max(t, axis=0, keepdims=True))
             probs.append(w / jnp.sum(w, axis=0, keepdims=True))
         w = jnp.concatenate(probs, axis=0).astype(BF16)
-        out[:, cols] = lax.dot_general(w, both(2, pair), TN, preferred_element_type=F32).astype(BF16)
+        out[:, cols] = lax.dot_general(w, both(1, pair), TN, preferred_element_type=F32).astype(BF16)
 
 
 def short_body(vq, vk, vv, cq, ak, av, aq, ck, cv, ai, gain, up, down):
@@ -619,11 +603,13 @@
         return [own[0]] + [trade(after(own[s], *first), s) for s in range(1, n)]
 
     wait = 16 * MIB
-    packed = pack(video, (aq, ak, av, ai), (), n, 0, widths[:1], 60, 6 * vq.size)
+    packed = pack(video, (aq, ai), range(n), (), n, 0, widths[:1], 60, 6 * vq.size, True)
     chunk_0 = send(packed)
-    packed = pack(video, (), (packed[0], ck, cv), n, widths[0], widths[1:], 16, wait)
-    *packed, chunk_0[0], ck, cv = packed
-    chunk_1 = send(packed[:n])
+    packed = pack(video, (ak, av), (0, 2), (), n, widths[0], widths[1:2], 60, wait, True)
+    chunk_1 = send(packed)
+    keep = (chunk_0[0], chunk_1[0], ck, cv)
+    packed = pack(video, (), (), keep, n, widths[0] + widths[1], widths[2:], 16, wait, False)
+    *packed, chunk_0[0], chunk_1[0], ck, cv = packed
     (share,) = call(
         functools.partial(listen_kernel, n, tokens, rows),
         (*chunk_0[::-1], ck, cv),
@@ -647,19 +633,26 @@
         [sds((tokens, widths[0]))] * n,
         limit=16,
     )
-    built = middle(chunk_1, first, packed[n:], n, MIB)
-    below = append(n, (0, 2), built[1], shares)
-    chunk_2 = [built[0], trade(below, 1)]
-    chunk_2 += [trade(built[s], s) for s in range(2, n)]
+    built = middle(chunk_1, first, packed, n, MIB)
+    wide = share.shape[1] + 4 * rows * columns // share.shape[0]
+    (share,) = call(
+        functools.partial(merge_kernel, n, 2, tokens),
+        (after(shares[0], built[0]), shares[1], chunk_1[0], chunk_1[2]),
+        [sds((share.shape[0], wide))],
+        limit=16,
+    )
+    below = trade(share, 1)
+    chunk_2 = [built[0]] + [trade(after(built[s], below), s) for s in range(1, 2)]
+    chunk_2 += [trade(after(built[s], share), s) for s in range(2, n)]
     (heard,) = call(
         functools.partial(heard_kernel, n, tokens, rows),
-        (cq, *chunk_0),
+        (cq, chunk_1[0], chunk_1[2], below),
         [sds(cq.shape)],
-        moved=1 * MIB,
+        moved=0,
         limit=16,
     )
     gain = after(gain.reshape(1, -1), heard)
-    own_sum, sent_sum, seen = combine((below, chunk_2[1]), built[1].shape[0], chunk_0, gain, up, tokens, rows, 512)
+    own_sum, sent_sum, seen = combine((share, below), chunk_0, gain, up, tokens, rows, 512)
     other_sum = lax.ppermute(sent_sum, "tp", [(0, 1), (1, 0)])
     results = finish(own_sum, other_sum, down, n, rows, features, 512)
     ends = call(
@@ -677,7 +670,7 @@
     n = lax.axis_size("seq")
     heads = vq.shape[1] // VHEAD
     return (
-        n in (2, 4, 8)
+        n == 4
         and lax.axis_size("tp") == 2
         and heads % n == 0
         and heads // n == 4

time: 70 us -> 67.9 us (0.970)
  waiting for transfers between devices: 25.4 us -> 15.3 us
  starting transfers between devices: 20.7 us -> 26.1 us
  Pallas kernels: 16.8 us -> 18.4 us
  local copies, waits for them, and re-layouts: 5.96 us -> 6.85 us
    ppermute x13 -> x14, waiting for transfers between devices: 21.6 us -> 11.4 us  [trade(): return lax.ppermute(value, 'seq', [(i, i ^ by) for i in range(n)])]
    ppermute x13 -> x14, starting transfers between devices: 19.2 us -> 24.6 us  [trade(): return lax.ppermute(value, 'seq', [(i, i ^ by) for i in range(n)])]
    pallas_call x2 -> x3, Pallas kernels: 2.91 us -> 4.49 us  [pack(): pl.pallas_call(functools.partial(pack_kernel, n, first, widths, len(audio...]
    unnamed x20 -> x22, local copies, waits for them, and re-layouts: 5.96 us -> 6.85 us
    pallas_call x3 -> x2, Pallas kernels: 5.14 us -> 4.69 us  [the longest x1 2.89 us: combine(): pl.pallas_call(functools.partial(combine_kernel, n, tokens, rows), grid=(...]
    pallas_call x4 -> x5, Pallas kernels: 6.5 us -> 6.93 us  [call(): pl.pallas_call(kernel, out_shape=tuple(outs), in_specs=[whole()] * len(in...]
  transfers between devices with their start and end apart: 14 -> 15, of which waited for: 6 -> 6; matrix products, arithmetic and copies ran while one was open for 0% -> 0% of each run, Pallas kernels for 18% -> 21%
where the time goes in v6:
time: 67.9 us; the launch traced here: 67.3 us
  starting transfers between devices  26.1 us (38%)
  Pallas kernels  18.4 us (27%)
  waiting for transfers between devices  15.3 us (23%)
  local copies, waits for them, and re-layouts  6.85 us (10%)
  between operations  0.76 us (1%)
    ppermute x14, starting transfers between devices, trade(): return lax.ppermute(value, 'seq', [(i, i ^ by) for i in range(n)])  24.6 us
    ppermute x14, waiting for transfers between devices, trade(): return lax.ppermute(value, 'seq', [(i, i ^ by) for i in range(n)])  11.4 us
    pallas_call x5, Pallas kernels, call(): pl.pallas_call(kernel, out_shape=tuple(outs), in_specs=[whole()] * len(in...  6.93 us
    unnamed x22, local copies, waits for them, and re-layouts  6.85 us
    pallas_call x3, Pallas kernels, pack(): pl.pallas_call(functools.partial(pack_kernel, n, first, widths, len(audio...  4.49 us
    ppermute x1, waiting for transfers between devices, short_body(): other_sum = lax.ppermute(sent_sum, 'tp', [(0, 1), (1, 0)])  3.83 us
    pallas_call x1, Pallas kernels, combine(): pl.pallas_call(functools.partial(combine_kernel, n, tokens, rows), grid=(...  2.89 us
    pallas_call x1, Pallas kernels, middle(): pl.pallas_call(functools.partial(middle_kernel, n), out_shape=(sds((tall,...  1.8 us
  transfers between devices with their start and end apart: 15, of which 6 were waited for; matrix products, arithmetic and copies ran while one was open for 0% of the time, Pallas kernels for 21%

profile of v6, /device:TPU:0, one launch (start us, length us, event | category | flops | bytes accessed | tf_op | source)
XLA Modules:
  0.0 67.3 jit_solution(18237913516172130519)
XLA Ops:
  0.6 1.9 %shard_map.156 = (bf16[512,128]{1,0:T(8,128)(2,1)}, bf16[512,128]{1,0:T(8,128)(2,1)}, bf16[512,128]{1,0:T(8,128)(2,1)}, bf16[512,128]{1,0:T(8,128)(2,1)}) custom-call(bf16[128,2048]{1,0:T(8,128)(2,1)} %bitcast.15, bf16[128,2048]{1,0:T(8,128)(2,1)} %bitcast.18, bf16[128,2048]{1,0:T(8,128)(2,1)} %bitcast.21, bf16[8,1024]{1,0:T(8,128)(2,1)} %bitcast.30, ...), custom_call_target="tpu_custom_call" | custom-call | bytes 1572864 | tf_op jit(solution)/shard_map/pallas_call | solution.py:243
  2.6 5.1 %collective-permute-start.3 = (bf16[512,128]{1,0:T(8,128)(2,1)}, bf16[512,128]{1,0:T(8,128)(2,1)S(1)}, u32[]{:S(2)}, u32[]{:S(2)}) collective-permute-start(bf16[512,128]{1,0:T(8,128)(2,1)} %get-tuple-element.54), channel_id=1, source_target_pairs={{0,12},{4,8},{8,4},{12,0},{1,13},{5,9},{9,5},{13,1},{2,14},{6,10},... | collective-permute-start | bytes 393224 | tf_op jit(solution)/shard_map/ppermute | solution.py:177
  8.3 1.9 %shard_map.157 = (bf16[512,128]{1,0:T(8,128)(2,1)}, bf16[384,128]{1,0:T(8,128)(2,1)}, bf16[512,128]{1,0:T(8,128)(2,1)}, bf16[384,128]{1,0:T(8,128)(2,1)}) custom-call(bf16[128,2048]{1,0:T(8,128)(2,1)} %bitcast.16, bf16[128,2048]{1,0:T(8,128)(2,1)} %bitcast.19, bf16[128,2048]{1,0:T(8,128)(2,1)} %bitcast.22, bf16[8,1024]{1,0:T(8,128)(2,1)} %bitcast.31, ...), custom_call_target="tpu_custom_call" | custom-call | bytes 16777216 | tf_op jit(solution)/shard_map/pallas_call | solution.py:243
  10.2 2.4 %collective-permute-start.1 = (bf16[512,128]{1,0:T(8,128)(2,1)}, bf16[512,128]{1,0:T(8,128)(2,1)S(1)}, u32[]{:S(2)}, u32[]{:S(2)}) collective-permute-start(bf16[512,128]{1,0:T(8,128)(2,1)} %get-tuple-element.51), channel_id=1, source_target_pairs={{0,8},{4,12},{8,0},{12,4},{1,9},{5,13},{9,1},{13,5},{2,10},{6,14},... | collective-permute-start | bytes 393224 | tf_op jit(solution)/shard_map/ppermute | solution.py:177
  12.5 2.0 %collective-permute-start = (bf16[384,128]{1,0:T(8,128)(2,1)}, bf16[384,128]{1,0:T(8,128)(2,1)S(1)}, u32[]{:S(2)}, u32[]{:S(2)}) collective-permute-start(bf16[384,128]{1,0:T(8,128)(2,1)} %get-tuple-element.50), channel_id=1, source_target_pairs={{0,4},{4,0},{8,12},{12,8},{1,5},{5,1},{9,13},{13,9},{2,6},{6,2},{1... | collective-permute-start | bytes 294920 | tf_op jit(solution)/shard_map/ppermute | solution.py:177
  14.6 1.6 %collective-permute-start.2 = (bf16[384,128]{1,0:T(8,128)(2,1)}, bf16[384,128]{1,0:T(8,128)(2,1)S(1)}, u32[]{:S(2)}, u32[]{:S(2)}) collective-permute-start(bf16[384,128]{1,0:T(8,128)(2,1)} %get-tuple-element.52), channel_id=1, source_target_pairs={{0,12},{4,8},{8,4},{12,0},{1,13},{5,9},{9,5},{13,1},{2,14},{6,10},... | collective-permute-start | bytes 294920 | tf_op jit(solution)/shard_map/ppermute | solution.py:177
  18.2 1.0 %copy-done.2 = bf16[1,128,2048]{2,1,0:T(8,128)(2,1)S(1)} copy-done((bf16[1,128,2048]{2,1,0:T(8,128)(2,1)S(1)}, bf16[1,128,2048]{2,1,0:T(8,128)(2,1)}, u32[]{:S(2)}) %copy-start.2) | copy-done | bytes 524312
  23.7 1.1 %collective-permute-done.4.refs_1_.refs_2_.refs_4_ = bf16[512,128]{1,0:T(8,128)(2,1)S(1)} collective-permute-done((bf16[512,128]{1,0:T(8,128)(2,1)}, bf16[512,128]{1,0:T(8,128)(2,1)S(1)}, u32[]{:S(2)}, u32[]{:S(2)}) %collective-permute-start.4) | collective-permute-done | bytes 131104 | tf_op jit(solution)/shard_map/ppermute | solution.py:177
  24.8 2.1 %shard_map.159.own = bf16[32,1152]{1,0:T(8,128)(2,1)S(1)} custom-call(bf16[512,128]{1,0:T(8,128)(2,1)S(1)} %collective-permute-done.3.refs_0_.refs_3_.refs_5_, bf16[512,128]{1,0:T(8,128)(2,1)S(1)} %collective-permute-done.4.refs_1_.refs_2_.refs_4_, bf16[512,128]{1,0:T(8,128)(2,1)S(1)} %collective-permute-done.5.refs_2_.refs_1_.refs_3_, ...), custom_call_target="tpu_custom_call" | custom-call | bytes 1048576 | tf_op jit(solution)/shard_map/pallas_call | solution.py:165
  26.9 2.8 %collective-permute-start.6 = (bf16[32,1152]{1,0:T(8,128)(2,1)S(1)}, bf16[32,1152]{1,0:T(8,128)(2,1)S(1)}, u32[]{:S(2)}, u32[]{:S(2)}) collective-permute-start(bf16[32,1152]{1,0:T(8,128)(2,1)S(1)} %shard_map.159.own), channel_id=1, source_target_pairs={{0,8},{4,12},{8,0},{12,4},{1,9},{5,13},{9,1},{13,5},{2,10},{6,14},... | collective-permute-start | bytes 221192 | tf_op jit(solution)/shard_map/ppermute | solution.py:177
  30.4 1.8 %shard_map.161 = (bf16[512,256]{1,0:T(8,128)(2,1)S(1)}, bf16[512,256]{1,0:T(8,128)(2,1)S(1)}, bf16[512,256]{1,0:T(8,128)(2,1)S(1)}, bf16[512,256]{1,0:T(8,128)(2,1)S(1)}) custom-call(bf16[512,128]{1,0:T(8,128)(2,1)S(1)} %get-tuple-element.49.refs_0_.mine.own, bf16[384,128]{1,0:T(8,128)(2,1)S(1)} %collective-permute-done.refs_1_, ...), custom_call_target="tpu_custom_call" | custom-call | bytes 1048576 | tf_op jit(solution)/shard_map/pallas_call | solution.py:314
  32.7 3.0 %collective-permute-start.7 = (bf16[32,2176]{1,0:T(8,128)(2,1)S(1)}, bf16[32,2176]{1,0:T(8,128)(2,1)S(1)}, u32[]{:S(2)}, u32[]{:S(2)}) collective-permute-start(bf16[32,2176]{1,0:T(8,128)(2,1)S(1)} %shard_map.162.refs_0_), channel_id=1, source_target_pairs={{0,4},{4,0},{8,12},{12,8},{1,5},{5,1},{9,13},{13,9},{2,6},{6,2},{1... | collective-permute-start | bytes 417800 | tf_op jit(solution)/shard_map/ppermute | solution.py:177
  35.7 1.9 %collective-permute-start.10 = (bf16[512,256]{1,0:T(8,128)(2,1)S(1)}, bf16[512,256]{1,0:T(8,128)(2,1)S(1)}, u32[]{:S(2)}, u32[]{:S(2)}) collective-permute-start(bf16[512,256]{1,0:T(8,128)(2,1)S(1)} %get-tuple-element.75), channel_id=1, source_target_pairs={{0,12},{4,8},{8,4},{12,0},{1,13},{5,9},{9,5},{13,1},{2,14},{6,10},... | collective-permute-start | bytes 786440 | tf_op jit(solution)/shard_map/ppermute | solution.py:177
  37.6 4.0 %collective-permute-done.7.first.refs_1_ = bf16[32,2176]{1,0:T(8,128)(2,1)S(1)} collective-permute-done((bf16[32,2176]{1,0:T(8,128)(2,1)S(1)}, bf16[32,2176]{1,0:T(8,128)(2,1)S(1)}, u32[]{:S(2)}, u32[]{:S(2)}) %collective-permute-start.7) | collective-permute-done | bytes 139296 | tf_op jit(solution)/shard_map/ppermute | solution.py:177
  42.3 2.8 %shard_map.163 = bf16[128,1024]{1,0:T(8,128)(2,1)} custom-call(bf16[128,1024]{1,0:T(8,128)(2,1)S(1)} %bitcast.26, bf16[512,128]{1,0:T(8,128)(2,1)S(1)} %get-tuple-element.49.refs_0_.mine.own, bf16[512,128]{1,0:T(8,128)(2,1)S(1)} %collective-permute-done.1.refs_2_.second, bf16[32,2176]{1,0:T(8,128)(2,1)S(1)} %collective-permute-done.7.first.refs_1_), custom_call_target="tpu_custom_call" | custom-call | tf_op jit(solution)/shard_map/pallas_call | solution.py:165
  45.1 2.9 %shard_map.164 = (f32[5,32,512]{2,1,0:T(8,128)S(1)}, bf16[5,32,512]{2,1,0:T(8,128)(2,1)S(1)}, bf16[8,1024]{1,0:T(8,128)(2,1)}) custom-call(bf16[32,2176]{1,0:T(8,128)(2,1)S(1)} %shard_map.162.refs_0_, bf16[32,2176]{1,0:T(8,128)(2,1)S(1)} %collective-permute-done.7.first.refs_1_, bf16[512,128]{1,0:T(8,128)(2,1)S(1)} %get-tuple-element.59.refs_3_.refs_0_.refs_2_, ...), custom_call_target="tpu_custom_call" | custom-call | tf_op jit(solution)/shard_map/pallas_call | solution.py:508
  48.0 1.5 %collective-permute-start.11 = (bf16[5,32,512]{2,1,0:T(8,128)(2,1)S(1)}, bf16[5,32,512]{2,1,0:T(8,128)(2,1)S(1)}, u32[]{:S(2)}, u32[]{:S(2)}) collective-permute-start(bf16[5,32,512]{2,1,0:T(8,128)(2,1)S(1)} %get-tuple-element.78), channel_id=1, source_target_pairs={{0,2},{2,0},{1,3},{3,1},{4,6},{6,4},{5,7},{7,5},{8,10},{10,8},{9,1... | collective-permute-start | bytes 491528 | tf_op jit(solution)/shard_map/ppermute | solution.py:656
  49.5 3.8 %collective-permute-done.11.other = bf16[5,32,512]{2,1,0:T(8,128)(2,1)S(1)} collective-permute-done((bf16[5,32,512]{2,1,0:T(8,128)(2,1)S(1)}, bf16[5,32,512]{2,1,0:T(8,128)(2,1)S(1)}, u32[]{:S(2)}, u32[]{:S(2)}) %collective-permute-start.11) | collective-permute-done | bytes 163872 | tf_op jit(solution)/shard_map/ppermute | solution.py:656
  53.3 1.4 %shard_map.165 = (f32[8,1024]{1,0:T(8,128)S(1)}, bf16[8,1024]{1,0:T(8,128)(2,1)S(1)}, bf16[8,1024]{1,0:T(8,128)(2,1)S(1)}, bf16[8,1024]{1,0:T(8,128)(2,1)S(1)}) custom-call(f32[5,32,512]{2,1,0:T(8,128)S(1)} %get-tuple-element.77.own, bf16[5,32,512]{2,1,0:T(8,128)(2,1)S(1)} %collective-permute-done.11.other, bf16[2048,1024]{1,0:T(8,128)(2,1)S(1)} %copy-done.4), custom_call_target="tpu_custom_call" | custom-call | tf_op jit(solution)/shard_map/pallas_call | solution.py:549
  54.7 2.2 %collective-permute-done.9.refs_2_ = bf16[512,256]{1,0:T(8,128)(2,1)S(1)} collective-permute-done((bf16[512,256]{1,0:T(8,128)(2,1)S(1)}, bf16[512,256]{1,0:T(8,128)(2,1)S(1)}, u32[]{:S(2)}, u32[]{:S(2)}) %collective-permute-start.9) | collective-permute-done | bytes 262176 | tf_op jit(solution)/shard_map/ppermute | solution.py:177
  58.0 2.2 %collective-permute-start.12 = (bf16[160,256]{1,0:T(8,128)(2,1)S(1)}, bf16[160,256]{1,0:T(8,128)(2,1)S(1)}, u32[]{:S(2)}, u32[]{:S(2)}) collective-permute-start(bf16[160,256]{1,0:T(8,128)(2,1)S(1)} %get-tuple-element.83), channel_id=1, source_target_pairs={{0,12},{4,8},{8,4},{12,0},{1,13},{5,9},{9,5},{13,1},{2,14},{6,10},... | collective-permute-start | bytes 245768 | tf_op jit(solution)/shard_map/ppermute | solution.py:177
  60.1 2.3 %collective-permute-start.14 = (bf16[160,256]{1,0:T(8,128)(2,1)S(1)}, bf16[160,256]{1,0:T(8,128)(2,1)S(1)}, u32[]{:S(2)}, u32[]{:S(2)}) collective-permute-start(bf16[160,256]{1,0:T(8,128)(2,1)S(1)} %get-tuple-element.85), channel_id=1, source_target_pairs={{0,4},{4,0},{8,12},{12,8},{1,5},{5,1},{9,13},{13,9},{2,6},{6,2},{1... | collective-permute-start | bytes 245768 | tf_op jit(solution)/shard_map/ppermute | solution.py:177
  62.4 2.5 %collective-permute-done.12.refs_4_ = bf16[160,256]{1,0:T(8,128)(2,1)S(1)} collective-permute-done((bf16[160,256]{1,0:T(8,128)(2,1)S(1)}, bf16[160,256]{1,0:T(8,128)(2,1)S(1)}, u32[]{:S(2)}, u32[]{:S(2)}) %collective-permute-start.12) | collective-permute-done | bytes 81952 | tf_op jit(solution)/shard_map/ppermute | solution.py:177
  64.9 1.6 %collective-permute-done.13.refs_5_ = bf16[160,256]{1,0:T(8,128)(2,1)S(1)} collective-permute-done((bf16[160,256]{1,0:T(8,128)(2,1)S(1)}, bf16[160,256]{1,0:T(8,128)(2,1)S(1)}, u32[]{:S(2)}, u32[]{:S(2)}) %collective-permute-start.13) | collective-permute-done | bytes 81952 | tf_op jit(solution)/shard_map/ppermute | solution.py:177
  (40 shorter events, 11.0 us)
Async XLA Ops:
  2.5 39.8 %copy-start.7 = (bf16[1,128,1024]{2,1,0:T(8,128)(2,1)S(1)}, bf16[1,128,1024]{2,1,0:T(8,128)(2,1)}, u32[]{:S(2)}) copy-start(bf16[1,128,1024]{2,1,0:T(8,128)(2,1)} %param.16) | copy-start | bytes 786436
  2.6 12.0 %collective-permute-start.3 = (bf16[512,128]{1,0:T(8,128)(2,1)}, bf16[512,128]{1,0:T(8,128)(2,1)S(1)}, u32[]{:S(2)}, u32[]{:S(2)}) collective-permute-start(bf16[512,128]{1,0:T(8,128)(2,1)} %get-tuple-element.54), channel_id=1, source_target_pairs={{0,12},{4,8},{8,4},{12,0},{1,13},{5,9},{9,5},{13,1},{2,14},{6,10},... | collective-permute-start | bytes 393224 | tf_op jit(solution)/shard_map/ppermute | solution.py:177
  7.7 17.2 %collective-permute-start.4 = (bf16[512,128]{1,0:T(8,128)(2,1)}, bf16[512,128]{1,0:T(8,128)(2,1)S(1)}, u32[]{:S(2)}, u32[]{:S(2)}) collective-permute-start(bf16[512,128]{1,0:T(8,128)(2,1)} %get-tuple-element.55), channel_id=1, source_target_pairs={{0,8},{4,12},{8,0},{12,4},{1,9},{5,13},{9,1},{13,5},{2,10},{6,14},... | collective-permute-start | bytes 393224 | tf_op jit(solution)/shard_map/ppermute | solution.py:177
  7.7 17.2 %collective-permute-start.5 = (bf16[512,128]{1,0:T(8,128)(2,1)}, bf16[512,128]{1,0:T(8,128)(2,1)S(1)}, u32[]{:S(2)}, u32[]{:S(2)}) collective-permute-start(bf16[512,128]{1,0:T(8,128)(2,1)} %get-tuple-element.56), channel_id=1, source_target_pairs={{0,4},{4,0},{8,12},{12,8},{1,5},{5,1},{9,13},{13,9},{2,6},{6,2},{1... | collective-permute-start | bytes 393224 | tf_op jit(solution)/shard_map/ppermute | solution.py:177
  8.3 36.8 %copy-start.10 = (f32[2048]{0:T(1024)S(1)}, f32[2048]{0:T(1024)}, u32[]{:S(2)}) copy-start(f32[2048]{0:T(1024)} %param.23) | copy-start | bytes 24580
  10.2 20.2 %collective-permute-start.1 = (bf16[512,128]{1,0:T(8,128)(2,1)}, bf16[512,128]{1,0:T(8,128)(2,1)S(1)}, u32[]{:S(2)}, u32[]{:S(2)}) collective-permute-start(bf16[512,128]{1,0:T(8,128)(2,1)} %get-tuple-element.51), channel_id=1, source_target_pairs={{0,8},{4,12},{8,0},{12,4},{1,9},{5,13},{9,1},{13,5},{2,10},{6,14},... | collective-permute-start | bytes 393224 | tf_op jit(solution)/shard_map/ppermute | solution.py:177
  12.5 17.9 %collective-permute-start = (bf16[384,128]{1,0:T(8,128)(2,1)}, bf16[384,128]{1,0:T(8,128)(2,1)S(1)}, u32[]{:S(2)}, u32[]{:S(2)}) collective-permute-start(bf16[384,128]{1,0:T(8,128)(2,1)} %get-tuple-element.50), channel_id=1, source_target_pairs={{0,4},{4,0},{8,12},{12,8},{1,5},{5,1},{9,13},{13,9},{2,6},{6,2},{1... | collective-permute-start | bytes 294920 | tf_op jit(solution)/shard_map/ppermute | solution.py:177
  14.6 15.8 %collective-permute-start.2 = (bf16[384,128]{1,0:T(8,128)(2,1)}, bf16[384,128]{1,0:T(8,128)(2,1)S(1)}, u32[]{:S(2)}, u32[]{:S(2)}) collective-permute-start(bf16[384,128]{1,0:T(8,128)(2,1)} %get-tuple-element.52), channel_id=1, source_target_pairs={{0,12},{4,8},{8,4},{12,0},{1,13},{5,9},{9,5},{13,1},{2,14},{6,10},... | collective-permute-start | bytes 294920 | tf_op jit(solution)/shard_map/ppermute | solution.py:177
  16.1 1.0 %copy-start = (bf16[1,128,2048]{2,1,0:T(8,128)(2,1)S(1)}, bf16[1,128,2048]{2,1,0:T(8,128)(2,1)}, u32[]{:S(2)}) copy-start(bf16[1,128,2048]{2,1,0:T(8,128)(2,1)} %param.13) | copy-start | bytes 1572868
  17.2 1.0 %copy-start.1 = (bf16[1,128,2048]{2,1,0:T(8,128)(2,1)S(1)}, bf16[1,128,2048]{2,1,0:T(8,128)(2,1)}, u32[]{:S(2)}) copy-start(bf16[1,128,2048]{2,1,0:T(8,128)(2,1)} %param.14) | copy-start | bytes 1572868
  18.2 1.0 %copy-start.2 = (bf16[1,128,2048]{2,1,0:T(8,128)(2,1)S(1)}, bf16[1,128,2048]{2,1,0:T(8,128)(2,1)}, u32[]{:S(2)}) copy-start(bf16[1,128,2048]{2,1,0:T(8,128)(2,1)} %param.15) | copy-start | bytes 1572868
  19.3 0.9 %copy-start.5 = (bf16[1,128,1024]{2,1,0:T(8,128)(2,1)S(1)}, bf16[1,128,1024]{2,1,0:T(8,128)(2,1)}, u32[]{:S(2)}) copy-start(bf16[1,128,1024]{2,1,0:T(8,128)(2,1)} %param.20) | copy-start | bytes 786436
  20.2 0.9 %copy-start.6 = (bf16[1,128,1024]{2,1,0:T(8,128)(2,1)S(1)}, bf16[1,128,1024]{2,1,0:T(8,128)(2,1)}, u32[]{:S(2)}) copy-start(bf16[1,128,1024]{2,1,0:T(8,128)(2,1)} %param.21) | copy-start | bytes 786436
  23.0 22.1 %copy-start.3 = (bf16[1024,2048]{1,0:T(8,128)(2,1)S(1)}, bf16[1024,2048]{1,0:T(8,128)(2,1)}, u32[]{:S(2)}) copy-start(bf16[1024,2048]{1,0:T(8,128)(2,1)} %refs_7_.1) | copy-start | bytes 12582916
  26.9 26.4 %copy-start.4 = (bf16[2048,1024]{1,0:T(8,128)(2,1)S(1)}, bf16[2048,1024]{1,0:T(8,128)(2,1)}, u32[]{:S(2)}) copy-start(bf16[2048,1024]{1,0:T(8,128)(2,1)} %down.1) | copy-start | bytes 12582916
  26.9 5.3 %collective-permute-start.6 = (bf16[32,1152]{1,0:T(8,128)(2,1)S(1)}, bf16[32,1152]{1,0:T(8,128)(2,1)S(1)}, u32[]{:S(2)}, u32[]{:S(2)}) collective-permute-start(bf16[32,1152]{1,0:T(8,128)(2,1)S(1)} %shard_map.159.own), channel_id=1, source_target_pairs={{0,8},{4,12},{8,0},{12,4},{1,9},{5,13},{9,1},{13,5},{2,10},{6,14},... | collective-permute-start | bytes 221192 | tf_op jit(solution)/shard_map/ppermute | solution.py:177
  32.7 8.9 %collective-permute-start.7 = (bf16[32,2176]{1,0:T(8,128)(2,1)S(1)}, bf16[32,2176]{1,0:T(8,128)(2,1)S(1)}, u32[]{:S(2)}, u32[]{:S(2)}) collective-permute-start(bf16[32,2176]{1,0:T(8,128)(2,1)S(1)} %shard_map.162.refs_0_), channel_id=1, source_target_pairs={{0,4},{4,0},{8,12},{12,8},{1,5},{5,1},{9,13},{13,9},{2,6},{6,2},{1... | collective-permute-start | bytes 417800 | tf_op jit(solution)/shard_map/ppermute | solution.py:177
  35.7 19.0 %collective-permute-start.10 = (bf16[512,256]{1,0:T(8,128)(2,1)S(1)}, bf16[512,256]{1,0:T(8,128)(2,1)S(1)}, u32[]{:S(2)}, u32[]{:S(2)}) collective-permute-start(bf16[512,256]{1,0:T(8,128)(2,1)S(1)} %get-tuple-element.75), channel_id=1, source_target_pairs={{0,12},{4,8},{8,4},{12,0},{1,13},{5,9},{9,5},{13,1},{2,14},{6,10},... | collective-permute-start | bytes 786440 | tf_op jit(solution)/shard_map/ppermute | solution.py:177
  37.6 19.3 %collective-permute-start.9 = (bf16[512,256]{1,0:T(8,128)(2,1)S(1)}, bf16[512,256]{1,0:T(8,128)(2,1)S(1)}, u32[]{:S(2)}, u32[]{:S(2)}) collective-permute-start(bf16[512,256]{1,0:T(8,128)(2,1)S(1)} %get-tuple-element.73), channel_id=1, source_target_pairs={{0,8},{4,12},{8,0},{12,4},{1,9},{5,13},{9,1},{13,5},{2,10},{6,14},... | collective-permute-start | bytes 786440 | tf_op jit(solution)/shard_map/ppermute | solution.py:177
  41.6 15.4 %collective-permute-start.8 = (bf16[512,256]{1,0:T(8,128)(2,1)S(1)}, bf16[512,256]{1,0:T(8,128)(2,1)S(1)}, u32[]{:S(2)}, u32[]{:S(2)}) collective-permute-start(bf16[512,256]{1,0:T(8,128)(2,1)S(1)} %get-tuple-element.71), channel_id=1, source_target_pairs={{0,4},{4,0},{8,12},{12,8},{1,5},{5,1},{9,13},{13,9},{2,6},{6,2},{1... | collective-permute-start | bytes 786440 | tf_op jit(solution)/shard_map/ppermute | solution.py:177
  48.0 5.3 %collective-permute-start.11 = (bf16[5,32,512]{2,1,0:T(8,128)(2,1)S(1)}, bf16[5,32,512]{2,1,0:T(8,128)(2,1)S(1)}, u32[]{:S(2)}, u32[]{:S(2)}) collective-permute-start(bf16[5,32,512]{2,1,0:T(8,128)(2,1)S(1)} %get-tuple-element.78), channel_id=1, source_target_pairs={{0,2},{2,0},{1,3},{3,1},{4,6},{6,4},{5,7},{7,5},{8,10},{10,8},{9,1... | collective-permute-start | bytes 491528 | tf_op jit(solution)/shard_map/ppermute | solution.py:656
  58.0 7.0 %collective-permute-start.12 = (bf16[160,256]{1,0:T(8,128)(2,1)S(1)}, bf16[160,256]{1,0:T(8,128)(2,1)S(1)}, u32[]{:S(2)}, u32[]{:S(2)}) collective-permute-start(bf16[160,256]{1,0:T(8,128)(2,1)S(1)} %get-tuple-element.83), channel_id=1, source_target_pairs={{0,12},{4,8},{8,4},{12,0},{1,13},{5,9},{9,5},{13,1},{2,14},{6,10},... | collective-permute-start | bytes 245768 | tf_op jit(solution)/shard_map/ppermute | solution.py:177
  60.1 6.3 %collective-permute-start.13 = (bf16[160,256]{1,0:T(8,128)(2,1)S(1)}, bf16[160,256]{1,0:T(8,128)(2,1)S(1)}, u32[]{:S(2)}, u32[]{:S(2)}) collective-permute-start(bf16[160,256]{1,0:T(8,128)(2,1)S(1)} %get-tuple-element.84), channel_id=1, source_target_pairs={{0,8},{4,12},{8,0},{12,4},{1,9},{5,13},{9,1},{13,5},{2,10},{6,14},... | collective-permute-start | bytes 245768 | tf_op jit(solution)/shard_map/ppermute | solution.py:177
  60.1 6.3 %collective-permute-start.14 = (bf16[160,256]{1,0:T(8,128)(2,1)S(1)}, bf16[160,256]{1,0:T(8,128)(2,1)S(1)}, u32[]{:S(2)}, u32[]{:S(2)}) collective-permute-start(bf16[160,256]{1,0:T(8,128)(2,1)S(1)} %get-tuple-element.85), channel_id=1, source_target_pairs={{0,4},{4,0},{8,12},{12,8},{1,5},{5,1},{9,13},{13,9},{2,6},{6,2},{1... | collective-permute-start | bytes 245768 | tf_op jit(solution)/shard_map/ppermute | solution.py:177
  (2 other events, 1.8 us)

commit v7 on v6

--- a/solution.py
+++ b/solution.py
@@ -189,13 +189,10 @@
     keep, refs = refs[:kept], refs[kept:]
     outs, passed, refs = refs[:count], refs[count : count + kept], refs[count + kept :]
     built = refs[:count] if staged else outs
-    lines, sem, audio_sem, out_sem = refs[-3 - audio_count : -3], refs[-3], refs[-2], refs[-1]
+    sem, out_sem = refs[-2], refs[-1]
     me = lax.axis_index("seq")
     tokens = q.shape[0]
     group = q.shape[1] // n
-    fetches = [pltpu.make_async_copy(ref, to, audio_sem.at[i]) for i, (ref, to) in enumerate(zip(audio, lines))]
-    for copy in fetches:
-        copy.start()
     copies, arrivals = [], []
     for c, width in enumerate(widths):
         for s in range(n):
@@ -209,10 +206,8 @@
         copies.append(pltpu.make_async_copy(ref, to, out_sem.at[count + i]))
         copies[-1].start()
     if audio:
-        for copy in fetches:
-            copy.wait()
         parts = []
-        for ref in lines:
+        for ref in audio:
             mine = slice(None)
             if ref.shape[1] > columns:
                 mine = pl.ds(pl.multiple_of(lax.axis_index("tp") * columns, LANES), columns)
@@ -243,11 +238,10 @@
     return pl.pallas_call(
         functools.partial(pack_kernel, n, first, widths, len(audio), len(keep), staged, columns),
         out_shape=tuple(sds(x) for x in shapes) + tuple(sds(x.shape) for x in keep),
-        in_specs=[stay] * (3 + len(audio) + len(keep)),
+        in_specs=[stay] * 3 + [whole()] * len(audio) + [stay] * len(keep),
         out_specs=(stay if staged else whole(),) * (len(shapes) + len(keep)),
         scratch_shapes=[pltpu.VMEM(x, BF16) for x in shapes if staged]
-        + [pltpu.VMEM(x.shape, BF16) for x in audio]
-        + [dma((3 * len(shapes),)), dma((max(len(audio), 1),)), dma((len(shapes) + len(keep),))],
+        + [dma((3 * len(shapes),)), dma((len(shapes) + len(keep),))],
         compiler_params=pltpu.CompilerParams(vmem_limit_bytes=limit * MIB),
         cost_estimate=pl.CostEstimate(flops=0, bytes_accessed=moved, transcendentals=0),
     )(*video, *audio, *keep)
@@ -338,7 +332,7 @@
 
 def unpack_kernel(n, heads, tokens, *refs):
     middles, lasts, own = refs[:n], refs[n : 2 * n][::-1], refs[2 * n]
-    out, mlp, line, sem = refs[2 * n + 1 :]
+    out, mlp, sem = refs[2 * n + 1 :]
     me = lax.axis_index("seq")
     width = lasts[0].shape[1]
     group = heads * VHEAD
@@ -362,9 +356,7 @@
         total = own[:, c * width : (c + 1) * width]
         for tail in tails:
             total = total + tail[c * rows : (c + 1) * rows]
-        line[:, c * width : (c + 1) * width] = total.astype(BF16)
-    copies.append(pltpu.make_async_copy(line, mlp, sem.at[len(copies)]))
-    copies[-1].start()
+        mlp[:, c * width : (c + 1) * width] = total.astype(BF16)
     for copy in copies:
         copy.wait()
 
@@ -375,8 +367,8 @@
         functools.partial(unpack_kernel, n, heads, tokens),
         out_shape=(sds((tokens, n * heads * VHEAD)), sds(own.shape)),
         in_specs=[pl.BlockSpec(memory_space=pltpu.VMEM)] * (2 * n + 1),
-        out_specs=(pl.BlockSpec(memory_space=pl.ANY),) * 2,
-        scratch_shapes=[pltpu.VMEM(own.shape, BF16), pltpu.SemaphoreType.DMA((count + 1,))],
+        out_specs=(pl.BlockSpec(memory_space=pl.ANY), whole()),
+        scratch_shapes=[pltpu.SemaphoreType.DMA((count,))],
         compiler_params=pltpu.CompilerParams(vmem_limit_bytes=16 * MIB),
     )(*middles, *lasts[::-1], own)
 

time: 67.9 us -> 69.5 us (1.024)
  Pallas kernels: 18.4 us -> 20.1 us
  starting transfers between devices: 26.1 us -> 25.2 us
    pallas_call x3, Pallas kernels: 4.49 us -> 5.68 us  [pack(): pl.pallas_call(functools.partial(pack_kernel, n, first, widths, len(audio...]
    ppermute x14, starting transfers between devices: 24.6 us -> 23.7 us  [trade(): return lax.ppermute(value, 'seq', [(i, i ^ by) for i in range(n)])]
where the time goes in v7:
time: 69.5 us; the launch traced here: 68.8 us
  starting transfers between devices  25.2 us (36%)
  Pallas kernels  20.1 us (29%)
  waiting for transfers between devices  15.9 us (23%)
  local copies, waits for them, and re-layouts  6.85 us (10%)
  between operations  0.76 us (1%)
    ppermute x14, starting transfers between devices, trade(): return lax.ppermute(value, 'seq', [(i, i ^ by) for i in range(n)])  23.7 us
    ppermute x14, waiting for transfers between devices, trade(): return lax.ppermute(value, 'seq', [(i, i ^ by) for i in range(n)])  12 us
    pallas_call x5, Pallas kernels, call(): pl.pallas_call(kernel, out_shape=tuple(outs), in_specs=[whole()] * len(in...  6.92 us
    unnamed x22, local copies, waits for them, and re-layouts  6.85 us
    pallas_call x3, Pallas kernels, pack(): pl.pallas_call(functools.partial(pack_kernel, n, first, widths, len(audio...  5.68 us
    ppermute x1, waiting for transfers between devices, short_body(): other_sum = lax.ppermute(sent_sum, 'tp', [(0, 1), (1, 0)])  3.82 us
    pallas_call x1, Pallas kernels, combine(): pl.pallas_call(functools.partial(combine_kernel, n, tokens, rows), grid=(...  2.89 us
    pallas_call x1, Pallas kernels, middle(): pl.pallas_call(functools.partial(middle_kernel, n), out_shape=(sds((tall,...  1.8 us
  transfers between devices with their start and end apart: 15, of which 6 were waited for; matrix products, arithmetic and copies ran while one was open for 0% of the time, Pallas kernels for 21%

profile of v7, /device:TPU:0, one launch (start us, length us, event | category | flops | bytes accessed | tf_op | source)
XLA Modules:
  0.0 68.8 jit_solution(14440461933638757818)
XLA Ops:
  0.6 2.5 %shard_map.156 = (bf16[512,128]{1,0:T(8,128)(2,1)}, bf16[512,128]{1,0:T(8,128)(2,1)}, bf16[512,128]{1,0:T(8,128)(2,1)}, bf16[512,128]{1,0:T(8,128)(2,1)}) custom-call(bf16[128,2048]{1,0:T(8,128)(2,1)} %bitcast.15, bf16[128,2048]{1,0:T(8,128)(2,1)} %bitcast.18, bf16[128,2048]{1,0:T(8,128)(2,1)} %bitcast.21, bf16[8,1024]{1,0:T(8,128)(2,1)} %bitcast.30, ...), custom_call_target="tpu_custom_call" | custom-call | bytes 1572864 | tf_op jit(solution)/shard_map/pallas_call | solution.py:238
  3.1 5.1 %collective-permute-start.3 = (bf16[512,128]{1,0:T(8,128)(2,1)}, bf16[512,128]{1,0:T(8,128)(2,1)S(1)}, u32[]{:S(2)}, u32[]{:S(2)}) collective-permute-start(bf16[512,128]{1,0:T(8,128)(2,1)} %get-tuple-element.54), channel_id=1, source_target_pairs={{0,12},{4,8},{8,4},{12,0},{1,13},{5,9},{9,5},{13,1},{2,14},{6,10},... | collective-permute-start | bytes 393224 | tf_op jit(solution)/shard_map/ppermute | solution.py:177
  8.9 2.5 %shard_map.157 = (bf16[512,128]{1,0:T(8,128)(2,1)}, bf16[384,128]{1,0:T(8,128)(2,1)}, bf16[512,128]{1,0:T(8,128)(2,1)}, bf16[384,128]{1,0:T(8,128)(2,1)}) custom-call(bf16[128,2048]{1,0:T(8,128)(2,1)} %bitcast.16, bf16[128,2048]{1,0:T(8,128)(2,1)} %bitcast.19, bf16[128,2048]{1,0:T(8,128)(2,1)} %bitcast.22, bf16[8,1024]{1,0:T(8,128)(2,1)} %bitcast.31, ...), custom_call_target="tpu_custom_call" | custom-call | bytes 16777216 | tf_op jit(solution)/shard_map/pallas_call | solution.py:238
  11.4 2.3 %collective-permute-start.1 = (bf16[512,128]{1,0:T(8,128)(2,1)}, bf16[512,128]{1,0:T(8,128)(2,1)S(1)}, u32[]{:S(2)}, u32[]{:S(2)}) collective-permute-start(bf16[512,128]{1,0:T(8,128)(2,1)} %get-tuple-element.51), channel_id=1, source_target_pairs={{0,8},{4,12},{8,0},{12,4},{1,9},{5,13},{9,1},{13,5},{2,10},{6,14},... | collective-permute-start | bytes 393224 | tf_op jit(solution)/shard_map/ppermute | solution.py:177
  13.7 2.0 %collective-permute-start = (bf16[384,128]{1,0:T(8,128)(2,1)}, bf16[384,128]{1,0:T(8,128)(2,1)S(1)}, u32[]{:S(2)}, u32[]{:S(2)}) collective-permute-start(bf16[384,128]{1,0:T(8,128)(2,1)} %get-tuple-element.50), channel_id=1, source_target_pairs={{0,4},{4,0},{8,12},{12,8},{1,5},{5,1},{9,13},{13,9},{2,6},{6,2},{1... | collective-permute-start | bytes 294920 | tf_op jit(solution)/shard_map/ppermute | solution.py:177
  16.7 1.0 %copy-done = bf16[1,128,2048]{2,1,0:T(8,128)(2,1)S(1)} copy-done((bf16[1,128,2048]{2,1,0:T(8,128)(2,1)S(1)}, bf16[1,128,2048]{2,1,0:T(8,128)(2,1)}, u32[]{:S(2)}) %copy-start) | copy-done | bytes 524312
  24.3 1.2 %collective-permute-done.4.refs_1_.refs_2_.refs_4_ = bf16[512,128]{1,0:T(8,128)(2,1)S(1)} collective-permute-done((bf16[512,128]{1,0:T(8,128)(2,1)}, bf16[512,128]{1,0:T(8,128)(2,1)S(1)}, u32[]{:S(2)}, u32[]{:S(2)}) %collective-permute-start.4) | collective-permute-done | bytes 131104 | tf_op jit(solution)/shard_map/ppermute | solution.py:177
  25.4 2.1 %shard_map.159.own = bf16[32,1152]{1,0:T(8,128)(2,1)S(1)} custom-call(bf16[512,128]{1,0:T(8,128)(2,1)S(1)} %collective-permute-done.3.refs_0_.refs_3_.refs_5_, bf16[512,128]{1,0:T(8,128)(2,1)S(1)} %collective-permute-done.4.refs_1_.refs_2_.refs_4_, bf16[512,128]{1,0:T(8,128)(2,1)S(1)} %collective-permute-done.5.refs_2_.refs_1_.refs_3_, ...), custom_call_target="tpu_custom_call" | custom-call | bytes 1048576 | tf_op jit(solution)/shard_map/pallas_call | solution.py:165
  27.5 2.8 %collective-permute-start.6 = (bf16[32,1152]{1,0:T(8,128)(2,1)S(1)}, bf16[32,1152]{1,0:T(8,128)(2,1)S(1)}, u32[]{:S(2)}, u32[]{:S(2)}) collective-permute-start(bf16[32,1152]{1,0:T(8,128)(2,1)S(1)} %shard_map.159.own), channel_id=1, source_target_pairs={{0,8},{4,12},{8,0},{12,4},{1,9},{5,13},{9,1},{13,5},{2,10},{6,14},... | collective-permute-start | bytes 221192 | tf_op jit(solution)/shard_map/ppermute | solution.py:177
  31.0 1.8 %shard_map.161 = (bf16[512,256]{1,0:T(8,128)(2,1)S(1)}, bf16[512,256]{1,0:T(8,128)(2,1)S(1)}, bf16[512,256]{1,0:T(8,128)(2,1)S(1)}, bf16[512,256]{1,0:T(8,128)(2,1)S(1)}) custom-call(bf16[512,128]{1,0:T(8,128)(2,1)S(1)} %get-tuple-element.49.refs_0_.mine.own, bf16[384,128]{1,0:T(8,128)(2,1)S(1)} %collective-permute-done.refs_1_, ...), custom_call_target="tpu_custom_call" | custom-call | bytes 1048576 | tf_op jit(solution)/shard_map/pallas_call | solution.py:308
  33.3 2.7 %collective-permute-start.7 = (bf16[32,2176]{1,0:T(8,128)(2,1)S(1)}, bf16[32,2176]{1,0:T(8,128)(2,1)S(1)}, u32[]{:S(2)}, u32[]{:S(2)}) collective-permute-start(bf16[32,2176]{1,0:T(8,128)(2,1)S(1)} %shard_map.162.refs_0_), channel_id=1, source_target_pairs={{0,4},{4,0},{8,12},{12,8},{1,5},{5,1},{9,13},{13,9},{2,6},{6,2},{1... | collective-permute-start | bytes 417800 | tf_op jit(solution)/shard_map/ppermute | solution.py:177
  36.0 2.2 %collective-permute-start.10 = (bf16[512,256]{1,0:T(8,128)(2,1)S(1)}, bf16[512,256]{1,0:T(8,128)(2,1)S(1)}, u32[]{:S(2)}, u32[]{:S(2)}) collective-permute-start(bf16[512,256]{1,0:T(8,128)(2,1)S(1)} %get-tuple-element.75), channel_id=1, source_target_pairs={{0,12},{4,8},{8,4},{12,0},{1,13},{5,9},{9,5},{13,1},{2,14},{6,10},... | collective-permute-start | bytes 786440 | tf_op jit(solution)/shard_map/ppermute | solution.py:177
  38.2 3.9 %collective-permute-done.7.first.refs_1_ = bf16[32,2176]{1,0:T(8,128)(2,1)S(1)} collective-permute-done((bf16[32,2176]{1,0:T(8,128)(2,1)S(1)}, bf16[32,2176]{1,0:T(8,128)(2,1)S(1)}, u32[]{:S(2)}, u32[]{:S(2)}) %collective-permute-start.7) | collective-permute-done | bytes 139296 | tf_op jit(solution)/shard_map/ppermute | solution.py:177
  42.6 2.8 %shard_map.163 = bf16[128,1024]{1,0:T(8,128)(2,1)} custom-call(bf16[128,1024]{1,0:T(8,128)(2,1)S(1)} %bitcast.26, bf16[512,128]{1,0:T(8,128)(2,1)S(1)} %get-tuple-element.49.refs_0_.mine.own, bf16[512,128]{1,0:T(8,128)(2,1)S(1)} %collective-permute-done.1.refs_2_.second, bf16[32,2176]{1,0:T(8,128)(2,1)S(1)} %collective-permute-done.7.first.refs_1_), custom_call_target="tpu_custom_call" | custom-call | tf_op jit(solution)/shard_map/pallas_call | solution.py:165
  45.4 2.9 %shard_map.164 = (f32[5,32,512]{2,1,0:T(8,128)S(1)}, bf16[5,32,512]{2,1,0:T(8,128)(2,1)S(1)}, bf16[8,1024]{1,0:T(8,128)(2,1)}) custom-call(bf16[32,2176]{1,0:T(8,128)(2,1)S(1)} %shard_map.162.refs_0_, bf16[32,2176]{1,0:T(8,128)(2,1)S(1)} %collective-permute-done.7.first.refs_1_, bf16[512,128]{1,0:T(8,128)(2,1)S(1)} %get-tuple-element.59.refs_3_.refs_0_.refs_2_, ...), custom_call_target="tpu_custom_call" | custom-call | tf_op jit(solution)/shard_map/pallas_call | solution.py:500
  48.3 1.5 %collective-permute-start.11 = (bf16[5,32,512]{2,1,0:T(8,128)(2,1)S(1)}, bf16[5,32,512]{2,1,0:T(8,128)(2,1)S(1)}, u32[]{:S(2)}, u32[]{:S(2)}) collective-permute-start(bf16[5,32,512]{2,1,0:T(8,128)(2,1)S(1)} %get-tuple-element.78), channel_id=1, source_target_pairs={{0,2},{2,0},{1,3},{3,1},{4,6},{6,4},{5,7},{7,5},{8,10},{10,8},{9,1... | collective-permute-start | bytes 491528 | tf_op jit(solution)/shard_map/ppermute | solution.py:648
  49.8 3.8 %collective-permute-done.11.other = bf16[5,32,512]{2,1,0:T(8,128)(2,1)S(1)} collective-permute-done((bf16[5,32,512]{2,1,0:T(8,128)(2,1)S(1)}, bf16[5,32,512]{2,1,0:T(8,128)(2,1)S(1)}, u32[]{:S(2)}, u32[]{:S(2)}) %collective-permute-start.11) | collective-permute-done | bytes 163872 | tf_op jit(solution)/shard_map/ppermute | solution.py:648
  53.6 1.4 %shard_map.165 = (f32[8,1024]{1,0:T(8,128)S(1)}, bf16[8,1024]{1,0:T(8,128)(2,1)S(1)}, bf16[8,1024]{1,0:T(8,128)(2,1)S(1)}, bf16[8,1024]{1,0:T(8,128)(2,1)S(1)}) custom-call(f32[5,32,512]{2,1,0:T(8,128)S(1)} %get-tuple-element.77.own, bf16[5,32,512]{2,1,0:T(8,128)(2,1)S(1)} %collective-permute-done.11.other, bf16[2048,1024]{1,0:T(8,128)(2,1)S(1)} %copy-done.4), custom_call_target="tpu_custom_call" | custom-call | tf_op jit(solution)/shard_map/pallas_call | solution.py:541
  55.0 2.4 %collective-permute-done.9.refs_2_ = bf16[512,256]{1,0:T(8,128)(2,1)S(1)} collective-permute-done((bf16[512,256]{1,0:T(8,128)(2,1)S(1)}, bf16[512,256]{1,0:T(8,128)(2,1)S(1)}, u32[]{:S(2)}, u32[]{:S(2)}) %collective-permute-start.9) | collective-permute-done | bytes 262176 | tf_op jit(solution)/shard_map/ppermute | solution.py:177
  58.4 2.6 %collective-permute-start.12 = (bf16[160,256]{1,0:T(8,128)(2,1)S(1)}, bf16[160,256]{1,0:T(8,128)(2,1)S(1)}, u32[]{:S(2)}, u32[]{:S(2)}) collective-permute-start(bf16[160,256]{1,0:T(8,128)(2,1)S(1)} %get-tuple-element.83), channel_id=1, source_target_pairs={{0,12},{4,8},{8,4},{12,0},{1,13},{5,9},{9,5},{13,1},{2,14},{6,10},... | collective-permute-start | bytes 245768 | tf_op jit(solution)/shard_map/ppermute | solution.py:177
  61.0 1.8 %collective-permute-start.14 = (bf16[160,256]{1,0:T(8,128)(2,1)S(1)}, bf16[160,256]{1,0:T(8,128)(2,1)S(1)}, u32[]{:S(2)}, u32[]{:S(2)}) collective-permute-start(bf16[160,256]{1,0:T(8,128)(2,1)S(1)} %get-tuple-element.85), channel_id=1, source_target_pairs={{0,4},{4,0},{8,12},{12,8},{1,5},{5,1},{9,13},{13,9},{2,6},{6,2},{1... | collective-permute-start | bytes 245768 | tf_op jit(solution)/shard_map/ppermute | solution.py:177
  62.9 2.0 %collective-permute-done.12.refs_4_ = bf16[160,256]{1,0:T(8,128)(2,1)S(1)} collective-permute-done((bf16[160,256]{1,0:T(8,128)(2,1)S(1)}, bf16[160,256]{1,0:T(8,128)(2,1)S(1)}, u32[]{:S(2)}, u32[]{:S(2)}) %collective-permute-start.12) | collective-permute-done | bytes 81952 | tf_op jit(solution)/shard_map/ppermute | solution.py:177
  64.8 2.5 %collective-permute-done.13.refs_5_ = bf16[160,256]{1,0:T(8,128)(2,1)S(1)} collective-permute-done((bf16[160,256]{1,0:T(8,128)(2,1)S(1)}, bf16[160,256]{1,0:T(8,128)(2,1)S(1)}, u32[]{:S(2)}, u32[]{:S(2)}) %collective-permute-start.13) | collective-permute-done | bytes 81952 | tf_op jit(solution)/shard_map/ppermute | solution.py:177
  67.4 1.5 %shard_map.167 = (bf16[128,2048]{1,0:T(8,128)(2,1)}, bf16[8,1024]{1,0:T(8,128)(2,1)}) custom-call(bf16[512,256]{1,0:T(8,128)(2,1)S(1)} %get-tuple-element.68.refs_0_, bf16[512,256]{1,0:T(8,128)(2,1)S(1)} %collective-permute-done.8.refs_1_, bf16[512,256]{1,0:T(8,128)(2,1)S(1)} %collective-permute-done.9.refs_2_, ...), custom_call_target="tpu_custom_call" | custom-call | tf_op jit(solution)/shard_map/pallas_call | solution.py:366
  (40 shorter events, 10.8 us)
Async XLA Ops:
  3.1 39.5 %copy-start.7 = (bf16[1,128,1024]{2,1,0:T(8,128)(2,1)S(1)}, bf16[1,128,1024]{2,1,0:T(8,128)(2,1)}, u32[]{:S(2)}) copy-start(bf16[1,128,1024]{2,1,0:T(8,128)(2,1)} %param.16) | copy-start | bytes 786436
  3.1 12.6 %collective-permute-start.3 = (bf16[512,128]{1,0:T(8,128)(2,1)}, bf16[512,128]{1,0:T(8,128)(2,1)S(1)}, u32[]{:S(2)}, u32[]{:S(2)}) collective-permute-start(bf16[512,128]{1,0:T(8,128)(2,1)} %get-tuple-element.54), channel_id=1, source_target_pairs={{0,12},{4,8},{8,4},{12,0},{1,13},{5,9},{9,5},{13,1},{2,14},{6,10},... | collective-permute-start | bytes 393224 | tf_op jit(solution)/shard_map/ppermute | solution.py:177
  8.3 17.2 %collective-permute-start.4 = (bf16[512,128]{1,0:T(8,128)(2,1)}, bf16[512,128]{1,0:T(8,128)(2,1)S(1)}, u32[]{:S(2)}, u32[]{:S(2)}) collective-permute-start(bf16[512,128]{1,0:T(8,128)(2,1)} %get-tuple-element.55), channel_id=1, source_target_pairs={{0,8},{4,12},{8,0},{12,4},{1,9},{5,13},{9,1},{13,5},{2,10},{6,14},... | collective-permute-start | bytes 393224 | tf_op jit(solution)/shard_map/ppermute | solution.py:177
  8.3 17.2 %collective-permute-start.5 = (bf16[512,128]{1,0:T(8,128)(2,1)}, bf16[512,128]{1,0:T(8,128)(2,1)S(1)}, u32[]{:S(2)}, u32[]{:S(2)}) collective-permute-start(bf16[512,128]{1,0:T(8,128)(2,1)} %get-tuple-element.56), channel_id=1, source_target_pairs={{0,4},{4,0},{8,12},{12,8},{1,5},{5,1},{9,13},{13,9},{2,6},{6,2},{1... | collective-permute-start | bytes 393224 | tf_op jit(solution)/shard_map/ppermute | solution.py:177
  8.9 36.5 %copy-start.10 = (f32[2048]{0:T(1024)S(1)}, f32[2048]{0:T(1024)}, u32[]{:S(2)}) copy-start(f32[2048]{0:T(1024)} %param.23) | copy-start | bytes 24580
  11.4 19.6 %collective-permute-start.1 = (bf16[512,128]{1,0:T(8,128)(2,1)}, bf16[512,128]{1,0:T(8,128)(2,1)S(1)}, u32[]{:S(2)}, u32[]{:S(2)}) collective-permute-start(bf16[512,128]{1,0:T(8,128)(2,1)} %get-tuple-element.51), channel_id=1, source_target_pairs={{0,8},{4,12},{8,0},{12,4},{1,9},{5,13},{9,1},{13,5},{2,10},{6,14},... | collective-permute-start | bytes 393224 | tf_op jit(solution)/shard_map/ppermute | solution.py:177
  13.7 17.2 %collective-permute-start = (bf16[384,128]{1,0:T(8,128)(2,1)}, bf16[384,128]{1,0:T(8,128)(2,1)S(1)}, u32[]{:S(2)}, u32[]{:S(2)}) collective-permute-start(bf16[384,128]{1,0:T(8,128)(2,1)} %get-tuple-element.50), channel_id=1, source_target_pairs={{0,4},{4,0},{8,12},{12,8},{1,5},{5,1},{9,13},{13,9},{2,6},{6,2},{1... | collective-permute-start | bytes 294920 | tf_op jit(solution)/shard_map/ppermute | solution.py:177
  15.8 15.2 %collective-permute-start.2 = (bf16[384,128]{1,0:T(8,128)(2,1)}, bf16[384,128]{1,0:T(8,128)(2,1)S(1)}, u32[]{:S(2)}, u32[]{:S(2)}) collective-permute-start(bf16[384,128]{1,0:T(8,128)(2,1)} %get-tuple-element.52), channel_id=1, source_target_pairs={{0,12},{4,8},{8,4},{12,0},{1,13},{5,9},{9,5},{13,1},{2,14},{6,10},... | collective-permute-start | bytes 294920 | tf_op jit(solution)/shard_map/ppermute | solution.py:177
  16.7 1.0 %copy-start = (bf16[1,128,2048]{2,1,0:T(8,128)(2,1)S(1)}, bf16[1,128,2048]{2,1,0:T(8,128)(2,1)}, u32[]{:S(2)}) copy-start(bf16[1,128,2048]{2,1,0:T(8,128)(2,1)} %param.13) | copy-start | bytes 1572868
  17.8 1.0 %copy-start.1 = (bf16[1,128,2048]{2,1,0:T(8,128)(2,1)S(1)}, bf16[1,128,2048]{2,1,0:T(8,128)(2,1)}, u32[]{:S(2)}) copy-start(bf16[1,128,2048]{2,1,0:T(8,128)(2,1)} %param.14) | copy-start | bytes 1572868
  18.8 1.0 %copy-start.2 = (bf16[1,128,2048]{2,1,0:T(8,128)(2,1)S(1)}, bf16[1,128,2048]{2,1,0:T(8,128)(2,1)}, u32[]{:S(2)}) copy-start(bf16[1,128,2048]{2,1,0:T(8,128)(2,1)} %param.15) | copy-start | bytes 1572868
  19.8 0.9 %copy-start.5 = (bf16[1,128,1024]{2,1,0:T(8,128)(2,1)S(1)}, bf16[1,128,1024]{2,1,0:T(8,128)(2,1)}, u32[]{:S(2)}) copy-start(bf16[1,128,1024]{2,1,0:T(8,128)(2,1)} %param.20) | copy-start | bytes 786436
  20.8 0.9 %copy-start.6 = (bf16[1,128,1024]{2,1,0:T(8,128)(2,1)S(1)}, bf16[1,128,1024]{2,1,0:T(8,128)(2,1)}, u32[]{:S(2)}) copy-start(bf16[1,128,1024]{2,1,0:T(8,128)(2,1)} %param.21) | copy-start | bytes 786436
  23.6 21.8 %copy-start.3 = (bf16[1024,2048]{1,0:T(8,128)(2,1)S(1)}, bf16[1024,2048]{1,0:T(8,128)(2,1)}, u32[]{:S(2)}) copy-start(bf16[1024,2048]{1,0:T(8,128)(2,1)} %refs_7_.1) | copy-start | bytes 12582916
  27.5 26.1 %copy-start.4 = (bf16[2048,1024]{1,0:T(8,128)(2,1)S(1)}, bf16[2048,1024]{1,0:T(8,128)(2,1)}, u32[]{:S(2)}) copy-start(bf16[2048,1024]{1,0:T(8,128)(2,1)} %down.1) | copy-start | bytes 12582916
  27.5 5.3 %collective-permute-start.6 = (bf16[32,1152]{1,0:T(8,128)(2,1)S(1)}, bf16[32,1152]{1,0:T(8,128)(2,1)S(1)}, u32[]{:S(2)}, u32[]{:S(2)}) collective-permute-start(bf16[32,1152]{1,0:T(8,128)(2,1)S(1)} %shard_map.159.own), channel_id=1, source_target_pairs={{0,8},{4,12},{8,0},{12,4},{1,9},{5,13},{9,1},{13,5},{2,10},{6,14},... | collective-permute-start | bytes 221192 | tf_op jit(solution)/shard_map/ppermute | solution.py:177
  33.3 8.8 %collective-permute-start.7 = (bf16[32,2176]{1,0:T(8,128)(2,1)S(1)}, bf16[32,2176]{1,0:T(8,128)(2,1)S(1)}, u32[]{:S(2)}, u32[]{:S(2)}) collective-permute-start(bf16[32,2176]{1,0:T(8,128)(2,1)S(1)} %shard_map.162.refs_0_), channel_id=1, source_target_pairs={{0,4},{4,0},{8,12},{12,8},{1,5},{5,1},{9,13},{13,9},{2,6},{6,2},{1... | collective-permute-start | bytes 417800 | tf_op jit(solution)/shard_map/ppermute | solution.py:177
  36.0 19.0 %collective-permute-start.10 = (bf16[512,256]{1,0:T(8,128)(2,1)S(1)}, bf16[512,256]{1,0:T(8,128)(2,1)S(1)}, u32[]{:S(2)}, u32[]{:S(2)}) collective-permute-start(bf16[512,256]{1,0:T(8,128)(2,1)S(1)} %get-tuple-element.75), channel_id=1, source_target_pairs={{0,12},{4,8},{8,4},{12,0},{1,13},{5,9},{9,5},{13,1},{2,14},{6,10},... | collective-permute-start | bytes 786440 | tf_op jit(solution)/shard_map/ppermute | solution.py:177
  38.2 19.2 %collective-permute-start.9 = (bf16[512,256]{1,0:T(8,128)(2,1)S(1)}, bf16[512,256]{1,0:T(8,128)(2,1)S(1)}, u32[]{:S(2)}, u32[]{:S(2)}) collective-permute-start(bf16[512,256]{1,0:T(8,128)(2,1)S(1)} %get-tuple-element.73), channel_id=1, source_target_pairs={{0,8},{4,12},{8,0},{12,4},{1,9},{5,13},{9,1},{13,5},{2,10},{6,14},... | collective-permute-start | bytes 786440 | tf_op jit(solution)/shard_map/ppermute | solution.py:177
  42.1 15.3 %collective-permute-start.8 = (bf16[512,256]{1,0:T(8,128)(2,1)S(1)}, bf16[512,256]{1,0:T(8,128)(2,1)S(1)}, u32[]{:S(2)}, u32[]{:S(2)}) collective-permute-start(bf16[512,256]{1,0:T(8,128)(2,1)S(1)} %get-tuple-element.71), channel_id=1, source_target_pairs={{0,4},{4,0},{8,12},{12,8},{1,5},{5,1},{9,13},{13,9},{2,6},{6,2},{1... | collective-permute-start | bytes 786440 | tf_op jit(solution)/shard_map/ppermute | solution.py:177
  48.3 5.3 %collective-permute-start.11 = (bf16[5,32,512]{2,1,0:T(8,128)(2,1)S(1)}, bf16[5,32,512]{2,1,0:T(8,128)(2,1)S(1)}, u32[]{:S(2)}, u32[]{:S(2)}) collective-permute-start(bf16[5,32,512]{2,1,0:T(8,128)(2,1)S(1)} %get-tuple-element.78), channel_id=1, source_target_pairs={{0,2},{2,0},{1,3},{3,1},{4,6},{6,4},{5,7},{7,5},{8,10},{10,8},{9,1... | collective-permute-start | bytes 491528 | tf_op jit(solution)/shard_map/ppermute | solution.py:648
  58.4 6.4 %collective-permute-start.12 = (bf16[160,256]{1,0:T(8,128)(2,1)S(1)}, bf16[160,256]{1,0:T(8,128)(2,1)S(1)}, u32[]{:S(2)}, u32[]{:S(2)}) collective-permute-start(bf16[160,256]{1,0:T(8,128)(2,1)S(1)} %get-tuple-element.83), channel_id=1, source_target_pairs={{0,12},{4,8},{8,4},{12,0},{1,13},{5,9},{9,5},{13,1},{2,14},{6,10},... | collective-permute-start | bytes 245768 | tf_op jit(solution)/shard_map/ppermute | solution.py:177
  61.0 6.3 %collective-permute-start.13 = (bf16[160,256]{1,0:T(8,128)(2,1)S(1)}, bf16[160,256]{1,0:T(8,128)(2,1)S(1)}, u32[]{:S(2)}, u32[]{:S(2)}) collective-permute-start(bf16[160,256]{1,0:T(8,128)(2,1)S(1)} %get-tuple-element.84), channel_id=1, source_target_pairs={{0,8},{4,12},{8,0},{12,4},{1,9},{5,13},{9,1},{13,5},{2,10},{6,14},... | collective-permute-start | bytes 245768 | tf_op jit(solution)/shard_map/ppermute | solution.py:177
  61.0 6.3 %collective-permute-start.14 = (bf16[160,256]{1,0:T(8,128)(2,1)S(1)}, bf16[160,256]{1,0:T(8,128)(2,1)S(1)}, u32[]{:S(2)}, u32[]{:S(2)}) collective-permute-start(bf16[160,256]{1,0:T(8,128)(2,1)S(1)} %get-tuple-element.85), channel_id=1, source_target_pairs={{0,4},{4,0},{8,12},{12,8},{1,5},{5,1},{9,13},{13,9},{2,6},{6,2},{1... | collective-permute-start | bytes 245768 | tf_op jit(solution)/shard_map/ppermute | solution.py:177
  (2 other events, 1.8 us)
